TPU v7x, 256 devices: a whole 4x4x8 slice. The times are simulated.
256 devices in a mesh: section: 16 (over z_hi, y, core), seq: 16 (over x, z_lo).
Axes of the slice: x: 4, y: 4, z: 8 (z_hi: 2, z_lo: 4; z = z_hi * 4 + z_lo), core: 2. Of those that a mesh axis runs over, the one named last changes fastest.
Arguments:
- tokens_in: bfloat16 [6144, 2560], P('seq'), may hold values from -6 to 6
- stale_values: bfloat16 [16, 6144, 2560], P('section', 'seq'), may hold values from -6 to 6
- mod_scale: float32 [16, 2560], P('section'), may hold values from -0.5 to 0.5
- mod_shift: float32 [16, 2560], P('section'), may hold values from -3 to 3
- query_gain: float32 [16, 2560], P('section'), may hold values from -2.5 to 2.5
- key_gain: float32 [16, 2560], P('section'), may hold values from -2.5 to 2.5
- branch_gain: float32 [16, 2560], P('section'), may hold values from 1 to 3
- tile_list: int32 [96, 18], P('seq'), may hold values from 0 to 95, as said below
- tile_count: int32 [96], P('seq'), may hold values from 1 to 18
- patch_order: int32 [16, 6], P('seq'), may hold values from 0 to 5, each once within a row
Outputs:
- layer_out: bfloat16 [16, 6144, 2560], P('section', 'seq')
Inputs may be any that keep to these rules, and one draw needn't show every extreme that they name: The first tile_count[g] entries of tile_list[g] are distinct, begin with g itself, and name tiles whose frame, tile row and tile column each differ from g's by at most one; later entries are valid tile numbers that are not read. `patch_order`: each row is a permutation of the block's 6 patches.
All inputs are finite; a program needn't handle non-finite values.
Results may differ from a plain program's by a relative error of at most 0.015.
Values may be sent and summed in bfloat16 or wider, within the bound.
No kernel may reach another device: no remote copies, remote signals or barrier semaphores. Data moves between devices by JAX's collectives and lax.ppermute only.
A program may use at most 128 MiB of HBM per device.

v0:
```python
import math

import jax
import jax.numpy as jnp
from jax import lax
from jax.sharding import PartitionSpec as P

HD = 128
TILE = 64


def extended(block, sides, width):
    for axis, dim in sides:
        count = lax.axis_size(axis)
        forward = [(i, i + 1) for i in range(count - 1)]
        backward = [(target, source) for source, target in forward]
        low = lax.ppermute(
            lax.slice_in_dim(block, block.shape[dim] - width, None, axis=dim), axis, forward
        )
        high = lax.ppermute(lax.slice_in_dim(block, 0, width, axis=dim), axis, backward)
        block = jnp.concatenate([low, block, high], axis=dim)
    return block


def from_behind(value, axis, steps):
    count = lax.axis_size(axis)
    leading, last = (max(0, -steps), min(count, count - steps))
    return lax.ppermute(value, axis, [(source, source + steps) for source in range(leading, last)])


def head_norm(matrix, head_size):
    shaped = matrix.reshape(matrix.shape[0], matrix.shape[1] // head_size, head_size)
    power = jnp.mean(shaped * shaped, axis=-1, keepdims=True)
    return (shaped * lax.rsqrt(power + 1e-06)).reshape(matrix.shape)


def keys_from(value_rows, gain, head_size):
    return (head_norm(value_rows.astype(jnp.float32), head_size) * gain).astype(jnp.bfloat16)


def on_device(
    tokens_in,
    stale_values,
    mod_scale,
    mod_shift,
    query_gain,
    key_gain,
    branch_gain,
    tile_list,
    tile_count,
    patch_order,
):
    section_count = lax.axis_size("section")
    section_index = lax.axis_index("section")
    block_index = lax.axis_index("seq")
    tok_rows, channels = tokens_in.shape
    head_count = channels // HD
    patches = tok_rows // TILE
    score_scale = 1.0 / math.sqrt(HD)
    gain_in = 1.0 + mod_scale[0]
    shift_in = mod_shift[0]
    q_gain = query_gain[0]
    k_gain = key_gain[0]
    out_gain = branch_gain[0]
    own_values = stale_values[0]
    own_keys = keys_from(own_values, k_gain, HD)
    rimmed = extended(jnp.stack([own_keys, own_values]), (("seq", 1),), tok_rows)
    side_keys = jnp.concatenate([rimmed[0, :tok_rows], rimmed[0, 2 * tok_rows :]], axis=0)
    side_values = jnp.concatenate([rimmed[1, :tok_rows], rimmed[1, 2 * tok_rows :]], axis=0)
    side_k = side_keys.reshape(2 * tok_rows, head_count, HD)
    side_v = side_values.reshape(2 * tok_rows, head_count, HD)
    slot_live = jnp.arange(tile_list.shape[1])[None, :] < tile_count[:, None]
    window_ids = (block_index - 1) * patches + jnp.arange(3 * patches)
    window = jnp.any(
        (tile_list[:, :, None] == window_ids[None, None, :]) & slot_live[:, :, None], axis=1
    )
    side_ok = jnp.concatenate([window[:, :patches], window[:, 2 * patches :]], axis=1)
    near_ok = window[:, patches : 2 * patches]
    plan = patch_order[0]

    def run_patch(patch_id, rows_in, key_buf, value_buf):
        hidden = head_norm(rows_in.astype(jnp.float32), HD) * gain_in + shift_in
        value_rows = hidden.astype(jnp.bfloat16)
        key_rows = keys_from(value_rows, k_gain, HD)
        query = (head_norm(hidden, HD) * q_gain).astype(jnp.bfloat16).reshape(TILE, head_count, HD)
        start = patch_id * TILE
        key_buf = lax.dynamic_update_slice_in_dim(key_buf, key_rows, start, 0)
        value_buf = lax.dynamic_update_slice_in_dim(value_buf, value_rows, start, 0)
        side_mask = jnp.repeat(side_ok[patch_id], TILE)
        near_mask = jnp.repeat(near_ok[patch_id], TILE)
        side_scores = (
            jnp.einsum("qhd,khd->hqk", query, side_k, preferred_element_type=jnp.float32)
            * score_scale
        )
        side_w = jnp.where(side_mask[None, None, :], jnp.exp(side_scores), 0.0)
        near_keys = key_buf.reshape(tok_rows, head_count, HD)
        near_scores = (
            jnp.einsum("qhd,khd->hqk", query, near_keys, preferred_element_type=jnp.float32)
            * score_scale
        )
        near_w = jnp.where(near_mask[None, None, :], jnp.exp(near_scores), 0.0)
        denominator = jnp.sum(side_w, axis=-1) + jnp.sum(near_w, axis=-1)
        summed = jnp.einsum(
            "hqk,khd->qhd", side_w.astype(jnp.bfloat16), side_v, preferred_element_type=jnp.float32
        )
        summed = summed + jnp.einsum(
            "hqk,khd->qhd",
            near_w.astype(jnp.bfloat16),
            value_buf.reshape(tok_rows, head_count, HD),
            preferred_element_type=jnp.float32,
        )
        mixed = summed / jnp.transpose(denominator)[:, :, None]
        out_rows = (rows_in.astype(jnp.float32) + out_gain * mixed.reshape(TILE, channels)).astype(
            jnp.bfloat16
        )
        return (out_rows, key_buf, value_buf)

    empty_out = jnp.zeros((tok_rows, channels), jnp.bfloat16)

    def advance(tick_index, carry):
        incoming, key_buf, value_buf, result = carry
        position = tick_index - section_index
        active = (position >= 0) & (position < patches)
        patch_id = plan[jnp.clip(position, 0, patches - 1)]
        local_rows = lax.dynamic_slice_in_dim(tokens_in, patch_id * TILE, TILE, 0)
        rows_in = jnp.where(section_index == 0, local_rows, incoming)

        def compute_patch(operands):
            rows_now, key_now, value_now, result_now = operands
            out_rows, key_now, value_now = run_patch(patch_id, rows_now, key_now, value_now)
            result_now = lax.dynamic_update_slice_in_dim(result_now, out_rows, patch_id * TILE, 0)
            return (out_rows, key_now, value_now, result_now)

        def skip_patch(operands):
            rows_now, key_now, value_now, result_now = operands
            return (jnp.zeros_like(rows_now), key_now, value_now, result_now)

        out_rows, key_buf, value_buf, result = lax.cond(
            active, compute_patch, skip_patch, (rows_in, key_buf, value_buf, result)
        )
        incoming = from_behind(out_rows, "section", 1)
        return (incoming, key_buf, value_buf, result)

    start_carry = (jnp.zeros((TILE, channels), jnp.bfloat16), own_keys, own_values, empty_out)
    final = lax.fori_loop(0, section_count + patches - 1, advance, start_carry)
    result = final[3]
    return result[None]


def solution(mesh):
    return jax.shard_map(
        on_device,
        mesh=mesh,
        in_specs=(
            P("seq", None),
            P("section", "seq", None),
            P("section", None),
            P("section", None),
            P("section", None),
            P("section", None),
            P("section", None),
            P("seq", None),
            P("seq"),
            P("seq", None),
        ),
        out_specs=P("section", "seq", None),
        check_vma=False,
    )
```

profile of v0, /device:TPU:221, one launch (start us, length us, event | category | flops | bytes accessed | tf_op | source)
XLA Modules:
  0.0 1074.0 jit_solution(8174999714605015213)
XLA Ops:
  25.2 79.0 %collective-permute-done.2 = bf16[2,384,2560]{1,2,0:T(8,128)(2,1)} collective-permute-done((bf16[2,384,2560]{1,2,0:T(8,128)(2,1)}, bf16[2,384,2560]{1,2,0:T(8,128)(2,1)}, u32[]{:S(2)}, u32[]{:S(2)}) %collective-permute-start.2) | collective-permute-done | bytes 3932192 | tf_op jit(solution)/shard_map/ppermute | solution.py:20
  106.7 84.1 %collective-permute-done.1 = bf16[2,384,2560]{1,2,0:T(8,128)(2,1)} collective-permute-done((bf16[2,384,2560]{1,2,0:T(8,128)(2,1)}, bf16[2,384,2560]{1,2,0:T(8,128)(2,1)}, u32[]{:S(2)}, u32[]{:S(2)}) %collective-permute-start.1) | collective-permute-done | bytes 3932192 | tf_op jit(solution)/shard_map/ppermute | solution.py:17
  214.9 859.1 %while.20 = (s32[]{:T(128)}, bf16[64,2560]{1,0:T(8,128)(2,1)S(1)}, bf16[384,2560]{0,1:T(8,128)(2,1)}, bf16[384,2560]{0,1:T(8,128)(2,1)}, bf16[384,2560]{1,0:T(8,...) while((s32[]{:T(128)}, bf16[64,2560]{1,0:T(8,128)(2,1)S(1)}, ...), condition=%wide.region_10.11_spmd, body=%wide.region_2.10_spmd.sunk | while | flops 768903680 | bytes 78895448 | solution.py:145
  221.4 7.3 collective-permute-done
  230.8 7.3 collective-permute-done
  240.1 7.3 collective-permute-done
  249.4 7.3 collective-permute-done
  258.8 7.3 collective-permute-done
  268.1 7.3 collective-permute-done
  277.5 7.3 collective-permute-done
  286.8 7.3 collective-permute-done
  296.2 10.1 collective-permute-done
  308.3 13.3 %collective-permute-done = bf16[64,2560]{1,0:T(8,128)(2,1)S(1)} collective-permute-done((bf16[64,2560]{1,0:T(8,128)(2,1)}, bf16[64,2560]{1,0:T(8,128)(2,1)S(1)}, u32[]{:S(2)}, u32[]{:S(2)}) %collective-permute-start) | collective-permute-done | bytes 327712 | tf_op jit(solution)/shard_map/while/body/eval_jaxpr/ppermute | solution.py:28
  323.7 13.3 %collective-permute-done = bf16[64,2560]{1,0:T(8,128)(2,1)S(1)} collective-permute-done((bf16[64,2560]{1,0:T(8,128)(2,1)}, bf16[64,2560]{1,0:T(8,128)(2,1)S(1)}, u32[]{:S(2)}, u32[]{:S(2)}) %collective-permute-start) | collective-permute-done | bytes 327712 | tf_op jit(solution)/shard_map/while/body/eval_jaxpr/ppermute | solution.py:28
  339.1 13.3 %collective-permute-done = bf16[64,2560]{1,0:T(8,128)(2,1)S(1)} collective-permute-done((bf16[64,2560]{1,0:T(8,128)(2,1)}, bf16[64,2560]{1,0:T(8,128)(2,1)S(1)}, u32[]{:S(2)}, u32[]{:S(2)}) %collective-permute-start) | collective-permute-done | bytes 327712 | tf_op jit(solution)/shard_map/while/body/eval_jaxpr/ppermute | solution.py:28
  354.4 13.3 %collective-permute-done = bf16[64,2560]{1,0:T(8,128)(2,1)S(1)} collective-permute-done((bf16[64,2560]{1,0:T(8,128)(2,1)}, bf16[64,2560]{1,0:T(8,128)(2,1)S(1)}, u32[]{:S(2)}, u32[]{:S(2)}) %collective-permute-start) | collective-permute-done | bytes 327712 | tf_op jit(solution)/shard_map/while/body/eval_jaxpr/ppermute | solution.py:28
  369.8 438.6 %collective-permute-done = bf16[64,2560]{1,0:T(8,128)(2,1)S(1)} collective-permute-done((bf16[64,2560]{1,0:T(8,128)(2,1)}, bf16[64,2560]{1,0:T(8,128)(2,1)S(1)}, u32[]{:S(2)}, u32[]{:S(2)}) %collective-permute-start) | collective-permute-done | bytes 327712 | tf_op jit(solution)/shard_map/while/body/eval_jaxpr/ppermute | solution.py:28
  808.4 33.9 %conditional.2 = (bf16[64,2560]{1,0:T(8,128)(2,1)}, bf16[384,2560]{0,1:T(8,128)(2,1)}, bf16[384,2560]{0,1:T(8,128)(2,1)}, bf16[384,2560]{1,0:T(8,128)(2,1)}) conditional(s32[]{:T(128)} %convert_element_type.127, (bf16[384,2560]{0,1:T(8,128)(2,1)}, bf16[384,2560]{0,1:T(8,128)(2,1)}, bf16[384,2560]{1,0:T(8,128)(2,1)}) %tuple.66, (pred[]{:T(512)}, ...), branch_computations={%region_3.3_spmd, %region_4.9_spmd} | conditional | flops 768903680 | bytes 77584304 | solution.py:138
  821.0 7.8 dynamic_update_slice.16
  828.8 7.8 dynamic_update_slice.15
  849.0 32.0 %conditional.2 = (bf16[64,2560]{1,0:T(8,128)(2,1)}, bf16[384,2560]{0,1:T(8,128)(2,1)}, bf16[384,2560]{0,1:T(8,128)(2,1)}, bf16[384,2560]{1,0:T(8,128)(2,1)}) conditional(s32[]{:T(128)} %convert_element_type.127, (bf16[384,2560]{0,1:T(8,128)(2,1)}, bf16[384,2560]{0,1:T(8,128)(2,1)}, bf16[384,2560]{1,0:T(8,128)(2,1)}) %tuple.66, (pred[]{:T(512)}, ...), branch_computations={%region_3.3_spmd, %region_4.9_spmd} | conditional | flops 768903680 | bytes 77584304 | solution.py:138
  861.6 6.9 dynamic_update_slice.16
  882.4 12.3 %collective-permute-done = bf16[64,2560]{1,0:T(8,128)(2,1)S(1)} collective-permute-done((bf16[64,2560]{1,0:T(8,128)(2,1)}, bf16[64,2560]{1,0:T(8,128)(2,1)S(1)}, u32[]{:S(2)}, u32[]{:S(2)}) %collective-permute-start) | collective-permute-done | bytes 327712 | tf_op jit(solution)/shard_map/while/body/eval_jaxpr/ppermute | solution.py:28
  894.7 32.6 %conditional.2 = (bf16[64,2560]{1,0:T(8,128)(2,1)}, bf16[384,2560]{0,1:T(8,128)(2,1)}, bf16[384,2560]{0,1:T(8,128)(2,1)}, bf16[384,2560]{1,0:T(8,128)(2,1)}) conditional(s32[]{:T(128)} %convert_element_type.127, (bf16[384,2560]{0,1:T(8,128)(2,1)}, bf16[384,2560]{0,1:T(8,128)(2,1)}, bf16[384,2560]{1,0:T(8,128)(2,1)}) %tuple.66, (pred[]{:T(512)}, ...), branch_computations={%region_3.3_spmd, %region_4.9_spmd} | conditional | flops 768903680 | bytes 77584304 | solution.py:138
  907.3 7.1 dynamic_update_slice.16
  914.4 7.1 dynamic_update_slice.15
  933.8 30.5 %conditional.2 = (bf16[64,2560]{1,0:T(8,128)(2,1)}, bf16[384,2560]{0,1:T(8,128)(2,1)}, bf16[384,2560]{0,1:T(8,128)(2,1)}, bf16[384,2560]{1,0:T(8,128)(2,1)}) conditional(s32[]{:T(128)} %convert_element_type.127, (bf16[384,2560]{0,1:T(8,128)(2,1)}, bf16[384,2560]{0,1:T(8,128)(2,1)}, bf16[384,2560]{1,0:T(8,128)(2,1)}) %tuple.66, (pred[]{:T(512)}, ...), branch_computations={%region_3.3_spmd, %region_4.9_spmd} | conditional | flops 768903680 | bytes 77584304 | solution.py:138
  965.6 32.2 %collective-permute-done = bf16[64,2560]{1,0:T(8,128)(2,1)S(1)} collective-permute-done((bf16[64,2560]{1,0:T(8,128)(2,1)}, bf16[64,2560]{1,0:T(8,128)(2,1)S(1)}, u32[]{:S(2)}, u32[]{:S(2)}) %collective-permute-start) | collective-permute-done | bytes 327712 | tf_op jit(solution)/shard_map/while/body/eval_jaxpr/ppermute | solution.py:28
  997.7 33.9 %conditional.2 = (bf16[64,2560]{1,0:T(8,128)(2,1)}, bf16[384,2560]{0,1:T(8,128)(2,1)}, bf16[384,2560]{0,1:T(8,128)(2,1)}, bf16[384,2560]{1,0:T(8,128)(2,1)}) conditional(s32[]{:T(128)} %convert_element_type.127, (bf16[384,2560]{0,1:T(8,128)(2,1)}, bf16[384,2560]{0,1:T(8,128)(2,1)}, bf16[384,2560]{1,0:T(8,128)(2,1)}) %tuple.66, (pred[]{:T(512)}, ...), branch_computations={%region_3.3_spmd, %region_4.9_spmd} | conditional | flops 768903680 | bytes 77584304 | solution.py:138
  1010.3 7.8 dynamic_update_slice.16
  1018.1 7.8 dynamic_update_slice.15
  1038.3 32.0 %conditional.2 = (bf16[64,2560]{1,0:T(8,128)(2,1)}, bf16[384,2560]{0,1:T(8,128)(2,1)}, bf16[384,2560]{0,1:T(8,128)(2,1)}, bf16[384,2560]{1,0:T(8,128)(2,1)}) conditional(s32[]{:T(128)} %convert_element_type.127, (bf16[384,2560]{0,1:T(8,128)(2,1)}, bf16[384,2560]{0,1:T(8,128)(2,1)}, bf16[384,2560]{1,0:T(8,128)(2,1)}) %tuple.66, (pred[]{:T(512)}, ...), branch_computations={%region_3.3_spmd, %region_4.9_spmd} | conditional | flops 768903680 | bytes 77584304 | solution.py:138
  (335 shorter events, 248.4 us)
Async XLA Ops:
  7.7 2.4 copy-start.2
  16.1 88.0 %collective-permute-start.2 = (bf16[2,384,2560]{1,2,0:T(8,128)(2,1)}, bf16[2,384,2560]{1,2,0:T(8,128)(2,1)}, u32[]{:S(2)}, u32[]{:S(2)}) collective-permute-start(bf16[2,384,2560]{1,2,0:T(8,128)(2,1)} %pad_maximum_fusion), channel_id=1, source_target_pairs={{1,0},{2,1},{3,2},{4,3},{5,4},{6,5},{7,6},{8,7},{9,8},{10,9},{11,1... | collective-permute-start | bytes 11796488 | tf_op jit(solution)/shard_map/ppermute | solution.py:20
  18.7 172.0 %collective-permute-start.1 = (bf16[2,384,2560]{1,2,0:T(8,128)(2,1)}, bf16[2,384,2560]{1,2,0:T(8,128)(2,1)}, u32[]{:S(2)}, u32[]{:S(2)}) collective-permute-start(bf16[2,384,2560]{1,2,0:T(8,128)(2,1)} %pad_maximum_fusion), channel_id=1, source_target_pairs={{0,1},{1,2},{2,3},{3,4},{4,5},{5,6},{6,7},{7,8},{8,9},{9,10},{10,1... | collective-permute-start | bytes 11796488 | tf_op jit(solution)/shard_map/ppermute | solution.py:17
  21.4 3.4 copy-start.8
  21.4 3.4 copy-start.7
  21.4 3.7 copy-start.6
  215.6 3.7 collective-permute-start
  220.1 8.6 collective-permute-start
  229.5 8.6 collective-permute-start
  238.8 8.6 collective-permute-start
  248.1 8.6 collective-permute-start
  257.5 8.6 collective-permute-start
  266.8 8.6 collective-permute-start
  276.2 8.6 collective-permute-start
  285.5 8.6 collective-permute-start
  294.9 11.4 %collective-permute-start = (bf16[64,2560]{1,0:T(8,128)(2,1)}, bf16[64,2560]{1,0:T(8,128)(2,1)S(1)}, u32[]{:S(2)}, u32[]{:S(2)}) collective-permute-start(bf16[64,2560]{1,0:T(8,128)(2,1)} %get-tuple-element.764), channel_id=1, source_target_pairs={{0,16},{16,32},{32,48},{48,64},{64,80},{80,96},{96,112},{112,128},... | collective-permute-start | bytes 983048 | tf_op jit(solution)/shard_map/while/body/eval_jaxpr/ppermute | solution.py:28
  307.1 14.6 %collective-permute-start = (bf16[64,2560]{1,0:T(8,128)(2,1)}, bf16[64,2560]{1,0:T(8,128)(2,1)S(1)}, u32[]{:S(2)}, u32[]{:S(2)}) collective-permute-start(bf16[64,2560]{1,0:T(8,128)(2,1)} %get-tuple-element.764), channel_id=1, source_target_pairs={{0,16},{16,32},{32,48},{48,64},{64,80},{80,96},{96,112},{112,128},... | collective-permute-start | bytes 983048 | tf_op jit(solution)/shard_map/while/body/eval_jaxpr/ppermute | solution.py:28
  322.4 14.6 %collective-permute-start = (bf16[64,2560]{1,0:T(8,128)(2,1)}, bf16[64,2560]{1,0:T(8,128)(2,1)S(1)}, u32[]{:S(2)}, u32[]{:S(2)}) collective-permute-start(bf16[64,2560]{1,0:T(8,128)(2,1)} %get-tuple-element.764), channel_id=1, source_target_pairs={{0,16},{16,32},{32,48},{48,64},{64,80},{80,96},{96,112},{112,128},... | collective-permute-start | bytes 983048 | tf_op jit(solution)/shard_map/while/body/eval_jaxpr/ppermute | solution.py:28
  337.8 14.6 %collective-permute-start = (bf16[64,2560]{1,0:T(8,128)(2,1)}, bf16[64,2560]{1,0:T(8,128)(2,1)S(1)}, u32[]{:S(2)}, u32[]{:S(2)}) collective-permute-start(bf16[64,2560]{1,0:T(8,128)(2,1)} %get-tuple-element.764), channel_id=1, source_target_pairs={{0,16},{16,32},{32,48},{48,64},{64,80},{80,96},{96,112},{112,128},... | collective-permute-start | bytes 983048 | tf_op jit(solution)/shard_map/while/body/eval_jaxpr/ppermute | solution.py:28
  353.1 14.6 %collective-permute-start = (bf16[64,2560]{1,0:T(8,128)(2,1)}, bf16[64,2560]{1,0:T(8,128)(2,1)S(1)}, u32[]{:S(2)}, u32[]{:S(2)}) collective-permute-start(bf16[64,2560]{1,0:T(8,128)(2,1)} %get-tuple-element.764), channel_id=1, source_target_pairs={{0,16},{16,32},{32,48},{48,64},{64,80},{80,96},{96,112},{112,128},... | collective-permute-start | bytes 983048 | tf_op jit(solution)/shard_map/while/body/eval_jaxpr/ppermute | solution.py:28
  368.5 439.9 %collective-permute-start = (bf16[64,2560]{1,0:T(8,128)(2,1)}, bf16[64,2560]{1,0:T(8,128)(2,1)S(1)}, u32[]{:S(2)}, u32[]{:S(2)}) collective-permute-start(bf16[64,2560]{1,0:T(8,128)(2,1)} %get-tuple-element.764), channel_id=1, source_target_pairs={{0,16},{16,32},{32,48},{48,64},{64,80},{80,96},{96,112},{112,128},... | collective-permute-start | bytes 983048 | tf_op jit(solution)/shard_map/while/body/eval_jaxpr/ppermute | solution.py:28
  814.4 2.1 copy-start
  842.3 6.7 collective-permute-start
  855.0 2.1 copy-start
  881.1 13.6 %collective-permute-start = (bf16[64,2560]{1,0:T(8,128)(2,1)}, bf16[64,2560]{1,0:T(8,128)(2,1)S(1)}, u32[]{:S(2)}, u32[]{:S(2)}) collective-permute-start(bf16[64,2560]{1,0:T(8,128)(2,1)} %get-tuple-element.764), channel_id=1, source_target_pairs={{0,16},{16,32},{32,48},{48,64},{64,80},{80,96},{96,112},{112,128},... | collective-permute-start | bytes 983048 | tf_op jit(solution)/shard_map/while/body/eval_jaxpr/ppermute | solution.py:28
  900.7 2.1 copy-start
  927.3 6.5 collective-permute-start
  939.7 2.1 copy-start
  964.3 33.5 %collective-permute-start = (bf16[64,2560]{1,0:T(8,128)(2,1)}, bf16[64,2560]{1,0:T(8,128)(2,1)S(1)}, u32[]{:S(2)}, u32[]{:S(2)}) collective-permute-start(bf16[64,2560]{1,0:T(8,128)(2,1)} %get-tuple-element.764), channel_id=1, source_target_pairs={{0,16},{16,32},{32,48},{48,64},{64,80},{80,96},{96,112},{112,128},... | collective-permute-start | bytes 983048 | tf_op jit(solution)/shard_map/while/body/eval_jaxpr/ppermute | solution.py:28
  1031.6 6.7 collective-permute-start
  1044.2 2.1 copy-start
  1070.3 3.7 collective-permute-start
  (11 other events, 20.6 us)
where the time goes:
time: 1080 us; the launch traced here: 1070 us
  waiting for transfers between devices  789 us (73%)
  local copies, waits for them, and re-layouts  150 us (14%)
  matrix products  43.6 us (4%)
  other arithmetic  43.4 us (4%)
  starting transfers between devices  32.2 us (3%)
  loops' own time  16.3 us (2%)
    ppermute x21, waiting for transfers between devices, from_behind(): lax.ppermute(value, axis, [(source, source + steps) for source in range(l...  626 us
    ppermute x1, waiting for transfers between devices, extended(): lax.ppermute(lax.slice_in_dim(block, block.shape[dim] - width, None, axis...  84.1 us
    ppermute x1, waiting for transfers between devices, extended(): lax.ppermute(lax.slice_in_dim(block, 0, width, axis=dim), axis, backward)  79 us
    dynamic_update_slice x6, local copies, waits for them, and re-layouts, run_patch(): value_buf = lax.dynamic_update_slice_in_dim(value_buf, value_rows, start, 0)  42.5 us
    dynamic_update_slice x6, local copies, waits for them, and re-layouts, run_patch(): key_buf = lax.dynamic_update_slice_in_dim(key_buf, key_rows, start, 0)  42.5 us
    ppermute x21, starting transfers between devices, from_behind(): lax.ppermute(value, axis, [(source, source + steps) for source in range(l...  26.9 us
  transfers between devices with their start and end apart: 23, of which 23 were waited for; matrix products, arithmetic and copies ran while one was open for 1% of the time, Pallas kernels for 0%

commit v1 on v0

v1 whole, which is shorter than its diff:
```python
import functools
import math

import jax
import jax.numpy as jnp
from jax import lax
from jax.experimental import pallas as pl
from jax.experimental.pallas import tpu as pltpu
from jax.sharding import PartitionSpec as P

HD = 128
TILE = 64
HT = 2
WT = 3
NPATCH = 6
ROWS = 384
HALF = 192
CHANNELS = 2560
GROUP = 8
LAYERS = 8
KEYS = 1536
COLKEYS = 512
OWN_ROWS = 960
MASKED = -16384.0
QUERY_SCALE = math.log2(math.e) / math.sqrt(HD)
EPS = 1e-06

ANY = pl.BlockSpec(memory_space=pl.ANY)
VMEM = pl.BlockSpec(memory_space=pltpu.VMEM)
SMEM = pl.BlockSpec(memory_space=pltpu.SMEM)

QUERY_ROWS = ((0, 256), (0, 384), (128, 384))


def column_order():
    return [(row, column) for column in range(WT) for row in range(HT)]


def first_heads_kernel(values, chunk):
    for h in range(GROUP):
        chunk[h] = values[0, :, h * HD : (h + 1) * HD]


def by_owner_kernel(values, owned):
    for d in range(GROUP):
        second, head, half = GROUP + d, 2 * GROUP + d // 2, (d % 2) * HALF
        owned[d, :ROWS] = values[0, :, d * HD : (d + 1) * HD]
        owned[d, ROWS : 2 * ROWS] = values[0, :, second * HD : (second + 1) * HD]
        owned[d, 2 * ROWS :] = values[0, half : half + HALF, head * HD : (head + 1) * HD]


def home_kernel(first_head, place, *refs):
    pieces, sems, out = refs[:GROUP], refs[-1], refs[-2]
    mine = place[1]
    copies = []
    for k in range(GROUP):
        start = pl.multiple_of((first_head + lax.bitwise_xor(mine, k)) * HD, HD)
        copies.append(
            pltpu.make_async_copy(pieces[k], out.at[0, :, pl.ds(start, HD)], sems.at[k])
        )
    for copy in copies:
        copy.start()
    for copy in copies:
        copy.wait()


def home_last_kernel(first_head, place, *refs):
    pieces, sems, out = refs[:GROUP], refs[-1], refs[-2]
    mine = place[1]
    for core in range(2):

        @pl.when(lax.rem(mine, 2) == core)
        def _():
            copies = []
            for k in range(core, GROUP, 2):
                head = first_head + lax.div(lax.bitwise_xor(mine, k), 2)
                start = pl.multiple_of(head * HD, HD)
                copies.append(
                    pltpu.make_async_copy(pieces[k], out.at[0, :, pl.ds(start, HD)], sems.at[k])
                )
            for copy in copies:
                copy.start()
            for copy in copies:
                copy.wait()


def row_scale(matrix):
    return lax.rsqrt(jnp.mean(matrix * matrix, axis=-1, keepdims=True) + EPS)


def attention_kernel(spec, place, active_ref, x_in, params, bias, *refs):
    halves, chunk, from_tokens, n_kv, n_prev, own_offset, lo_offset, hi_offset = spec
    kv_refs = refs[:n_kv]
    outs = refs[n_kv + n_prev : n_kv + n_prev + GROUP]
    x_out = refs[n_kv + n_prev + GROUP]
    (x_buf, kv_buf, out_buf, key_buf, value_buf, query_buf, kv_sems, x_sem, out_sems) = refs[
        n_kv + n_prev + GROUP + 1 :
    ]
    mine = place[1]

    @pl.when(active_ref[0] == 1)
    def _():
        if from_tokens:
            if halves:
                head = 2 * GROUP + lax.div(mine, 2)
            else:
                head = chunk * GROUP + mine
            source = x_in.at[:, pl.ds(pl.multiple_of(head * HD, HD), HD)]
        else:
            source = x_in
        x_copy = pltpu.make_async_copy(source, x_buf, x_sem)
        x_copy.start()

        def kv_copies(layer):
            copies = []
            if halves:
                for i, (ref, offset) in enumerate(zip(kv_refs, (own_offset, 0, 0, 0, 0, 0))):
                    copies.append(
                        pltpu.make_async_copy(
                            ref.at[layer, pl.ds(offset, HALF)],
                            kv_buf.at[layer, i // 2, pl.ds((i % 2) * HALF, HALF)],
                            kv_sems.at[layer, i],
                        )
                    )
            else:
                for i, (ref, offset) in enumerate(
                    zip(kv_refs, (own_offset, lo_offset, hi_offset))
                ):
                    copies.append(
                        pltpu.make_async_copy(
                            ref.at[layer, pl.ds(offset, ROWS)],
                            kv_buf.at[layer, i],
                            kv_sems.at[layer, i],
                        )
                    )
            return copies

        for layer in range(LAYERS):
            for copy in kv_copies(layer):
                copy.start()

        tile_of_row = lax.broadcasted_iota(jnp.int32, (KEYS, HD), 0) // TILE
        tile_of_lane = lax.broadcasted_iota(jnp.int32, (KEYS, HD), 1)
        key_buf[:, HD:] = jnp.where(tile_of_row == tile_of_lane, 1.0, 0.0).astype(jnp.bfloat16)
        value_buf[:, HD:] = jnp.ones((KEYS, HD), jnp.bfloat16)
        query_buf[:, HD:] = bias[...]

        x_copy.wait()
        if from_tokens:
            x0 = jnp.concatenate(
                [
                    x_buf[(row * WT + column) * TILE : (row * WT + column + 1) * TILE]
                    for row, column in column_order()
                ],
                axis=0,
            )
        else:
            x0 = x_buf[...]

        def layer_step(layer, x):
            for copy in kv_copies(layer):
                copy.wait()

            def gain(i):
                return params[layer, i : i + 1, chunk * HD : (chunk + 1) * HD]

            key_gain = gain(3)
            for column in range(WT):
                for slot, which in ((0, 1), (2, 2), (4, 0)):
                    for row in range(HT):
                        at = column * COLKEYS + (slot + row) * TILE
                        tile = (row * WT + column) * TILE
                        stale = kv_buf[layer, which, tile : tile + TILE]
                        value_buf[at : at + TILE, :HD] = stale
                        wide = stale.astype(jnp.float32)
                        key_buf[at : at + TILE, :HD] = (
                            wide * row_scale(wide) * key_gain
                        ).astype(jnp.bfloat16)

            hidden = x * row_scale(x) * (1.0 + gain(0)) + gain(1)
            new_values = hidden.astype(jnp.bfloat16)
            wide_values = new_values.astype(jnp.float32)
            new_keys = (wide_values * row_scale(wide_values) * key_gain).astype(jnp.bfloat16)
            query_buf[:, :HD] = (hidden * row_scale(hidden) * (gain(2) * QUERY_SCALE)).astype(
                jnp.bfloat16
            )
            for column in range(WT):
                at = column * COLKEYS + 6 * TILE
                rows = slice(column * 2 * TILE, (column + 1) * 2 * TILE)
                value_buf[at : at + 2 * TILE, :HD] = new_values[rows]
                key_buf[at : at + 2 * TILE, :HD] = new_keys[rows]

            sums = []
            for column in range(WT):
                keys = slice(column * COLKEYS, (column + 1) * COLKEYS)
                first, last = QUERY_ROWS[column]
                scores = lax.dot_general(
                    query_buf[first:last],
                    key_buf[keys],
                    (((1,), (1,)), ((), ())),
                    preferred_element_type=jnp.float32,
                )
                weights = jnp.exp2(scores).astype(jnp.bfloat16)
                sums.append(
                    jnp.dot(weights, value_buf[keys], preferred_element_type=jnp.float32)
                )
            total = [
                sums[0][:128] + sums[1][:128],
                sums[0][128:] + sums[1][128:256] + sums[2][:128],
                sums[1][256:] + sums[2][128:],
            ]
            mixed = jnp.concatenate([t[:, :HD] / t[:, HD:] for t in total], axis=0)
            out = (x + gain(4) * mixed).astype(jnp.bfloat16)
            for i, (row, column) in enumerate(column_order()):
                tile = (row * WT + column) * TILE
                out_buf[layer, tile : tile + TILE] = out[i * TILE : (i + 1) * TILE]

            return out.astype(jnp.float32)

        last = lax.fori_loop(0, LAYERS, layer_step, x0.astype(jnp.float32))
        x_buf[...] = last.astype(jnp.bfloat16)
        copies = [
            pltpu.make_async_copy(out_buf.at[lax.bitwise_xor(mine, k)], outs[k], out_sems.at[k])
            for k in range(GROUP)
        ]
        copies.append(pltpu.make_async_copy(x_buf, x_out, out_sems.at[GROUP]))
        for copy in copies:
            copy.start()
        for copy in copies:
            copy.wait()


def attention(
    place, active, x_in, params, bias, kv, previous, halves, chunk, from_tokens, own, lo, hi
):
    n_kv, n_prev = len(kv), len(previous)
    spec = (halves, chunk, from_tokens, n_kv, n_prev, own, lo, hi)
    piece = jax.ShapeDtypeStruct((ROWS, HD), jnp.bfloat16)
    pushes = 2 * 2 * 2 * 256 * 256 * 896 * LAYERS
    return pl.pallas_call(
        functools.partial(attention_kernel, spec),
        out_shape=[piece] * (GROUP + 1),
        in_specs=[SMEM, SMEM, ANY, VMEM, VMEM] + [ANY] * (n_kv + n_prev),
        out_specs=[ANY] * (GROUP + 1),
        scratch_shapes=[
            pltpu.VMEM((ROWS, HD), jnp.bfloat16),
            pltpu.VMEM((LAYERS, 3, ROWS, HD), jnp.bfloat16),
            pltpu.VMEM((LAYERS, ROWS, HD), jnp.bfloat16),
            pltpu.VMEM((KEYS, 2 * HD), jnp.bfloat16),
            pltpu.VMEM((KEYS, 2 * HD), jnp.bfloat16),
            pltpu.VMEM((ROWS, 2 * HD), jnp.bfloat16),
            pltpu.SemaphoreType.DMA((LAYERS, 6 if halves else 3)),
            pltpu.SemaphoreType.DMA,
            pltpu.SemaphoreType.DMA((GROUP + 1,)),
        ],
        input_output_aliases={5 + n_kv + i: i for i in range(n_prev)},
        compiler_params=pltpu.CompilerParams(vmem_limit_bytes=24 * 1024 * 1024),
        cost_estimate=pl.CostEstimate(
            flops=pushes, bytes_accessed=3 * 786432, transcendentals=896 * 512 * LAYERS
        ),
    )(place, active, x_in, params, bias, *kv, *previous)


def bias_table(tile_list, tile_count, plan, block_index):
    slot_live = jnp.arange(tile_list.shape[1])[None, :] < tile_count[:, None]
    window_ids = (block_index - 1) * NPATCH + jnp.arange(3 * NPATCH)
    window = jnp.any(
        (tile_list[:, :, None] == window_ids[None, None, :]) & slot_live[:, :, None], axis=1
    )
    patches = jnp.arange(NPATCH)
    position = jnp.sum(jnp.where(plan[None, :] == patches[:, None], patches[None, :], 0), axis=1)
    is_new = position[None, :] <= position[:, None]
    near = window[:, NPATCH : 2 * NPATCH]
    kinds = [window[:, :NPATCH], window[:, 2 * NPATCH :], near & ~is_new, near & is_new]
    listed = jnp.stack(kinds, axis=1).reshape(NPATCH, 4, HT, WT).transpose(0, 3, 1, 2)
    listed = listed.reshape(HT, WT, 4 * NPATCH).transpose(1, 0, 2).reshape(NPATCH, 4 * NPATCH)
    bias = jnp.where(listed, 0.0, MASKED).astype(jnp.bfloat16)
    bias = jnp.pad(bias, ((0, 0), (0, HD - 4 * NPATCH)))
    return jnp.repeat(bias, TILE, axis=0)


def on_device(
    tokens_in,
    stale_values,
    mod_scale,
    mod_shift,
    query_gain,
    key_gain,
    branch_gain,
    tile_list,
    tile_count,
    patch_order,
):
    n_section, n_seq = lax.axis_size("section"), lax.axis_size("seq")
    section = lax.axis_index("section")
    mine = lax.rem(section, GROUP)
    upper = lax.div(section, GROUP)
    core = lax.rem(section, 2)
    groups = [list(range(GROUP)), list(range(GROUP, 2 * GROUP))]
    forward = [(i, i + 1) for i in range(n_seq - 1)]
    backward = [(i + 1, i) for i in range(n_seq - 1)]
    place = jnp.stack([section, mine]).astype(jnp.int32)

    def exchange(array):
        return lax.all_to_all(array, "section", 0, 0, axis_index_groups=groups, tiled=True)

    chunk0 = pl.pallas_call(
        first_heads_kernel,
        out_shape=jax.ShapeDtypeStruct((GROUP, ROWS, HD), jnp.bfloat16),
        grid=(1,),
        in_specs=[pl.BlockSpec((1, ROWS, GROUP * HD), lambda i: (0, 0, 0))],
        out_specs=pl.BlockSpec((GROUP, ROWS, HD), lambda i: (0, 0, 0)),
    )(stale_values)
    low0 = lax.ppermute(chunk0, "seq", forward)
    high0 = lax.ppermute(chunk0, "seq", backward)

    later_values, gains, _ = lax.optimization_barrier(
        (stale_values, (mod_scale, mod_shift, query_gain, key_gain, branch_gain), chunk0)
    )
    owned = pl.pallas_call(
        by_owner_kernel,
        out_shape=jax.ShapeDtypeStruct((GROUP, OWN_ROWS, HD), jnp.bfloat16),
        in_specs=[VMEM],
        out_specs=VMEM,
    )(later_values)
    own = exchange(owned)
    own1 = own[:, ROWS : 2 * ROWS]
    low1 = lax.ppermute(own1, "seq", forward)
    high1 = lax.ppermute(own1, "seq", backward)
    own2 = own[:, 2 * ROWS :]

    def to_first_core(array, step, from_core):
        pairs = []
        for s in range(from_core, n_section, 2):
            for f in range(n_seq):
                if 0 <= f + step < n_seq:
                    pairs.append((s * n_seq + f, (s - from_core) * n_seq + f + step))
        return lax.ppermute(array, ("section", "seq"), pairs)

    own2_other = to_first_core(own2, 0, 1)
    low2 = [to_first_core(own2, 1, c) for c in range(2)]
    high2 = [to_first_core(own2, -1, c) for c in range(2)]

    vectors = jnp.concatenate(gains, axis=0).reshape(5, 20, HD)
    vectors = jnp.concatenate(
        [
            vectors[:, :GROUP],
            vectors[:, GROUP : 2 * GROUP],
            jnp.repeat(vectors[:, 2 * GROUP :], 2, axis=1),
        ],
        axis=-1,
    ).transpose(1, 0, 2)
    params = exchange(vectors)
    bias = bias_table(tile_list, tile_count, patch_order[0], lax.axis_index("seq"))

    sides0 = exchange(jnp.concatenate([low0, high0], axis=1))

    chunks = [
        (False, [own, sides0, sides0], (0, 0, ROWS)),
        (False, [own, low1, high1], (ROWS, 0, 0)),
        (True, [own, own2_other] + low2 + high2, (2 * ROWS, 0, 0)),
    ]
    out = None
    for chunk, (halves, kv, offsets) in enumerate(chunks):
        works = (core == 0) if halves else True
        step = 2 if halves else 1

        def run(stage, x_in, previous):
            active = jnp.logical_and(upper == stage, works).astype(jnp.int32).reshape(1)
            return attention(
                place, active, x_in, params, bias, kv, previous, halves, chunk, stage == 0, *offsets
            )

        *pieces, x_last = run(0, tokens_in, [])
        x_next = lax.ppermute(
            x_last, "section", [(i, i + GROUP) for i in range(0, GROUP, step)]
        )
        *pieces, _ = run(1, x_next, pieces)
        arrived = [pieces[0]]
        for k in range(1, GROUP):
            pairs = [
                (base + i, base + (i ^ k)) for base in (0, GROUP) for i in range(0, GROUP, step)
            ]
            arrived.append(lax.ppermute(pieces[k], "section", pairs))
        kernel = home_last_kernel if halves else home_kernel
        first_head = 2 * GROUP if halves else chunk * GROUP
        before = [] if out is None else [out]
        out = pl.pallas_call(
            functools.partial(kernel, first_head),
            out_shape=jax.ShapeDtypeStruct((1, ROWS, CHANNELS), jnp.bfloat16),
            in_specs=[SMEM] + [VMEM] * GROUP + [ANY] * len(before),
            out_specs=ANY,
            scratch_shapes=[pltpu.SemaphoreType.DMA((GROUP,))],
            input_output_aliases={1 + GROUP: 0} if before else {},
        )(place, *arrived, *before)
    return out


def solution(mesh):
    return jax.shard_map(
        on_device,
        mesh=mesh,
        in_specs=(
            P("seq", None),
            P("section", "seq", None),
            P("section", None),
            P("section", None),
            P("section", None),
            P("section", None),
            P("section", None),
            P("seq", None),
            P("seq"),
            P("seq", None),
        ),
        out_specs=P("section", "seq", None),
        check_vma=False,
    )
```

time: 1080 us -> 216 us (0.20)
  the two profiles are of different devices: /device:TPU:221 before, /device:TPU:198 now
where the time goes in v1:
time: 216 us; the launch traced here: 215 us
  waiting for transfers between devices  71.2 us (33%)
  starting transfers between devices  69.7 us (32%)
  Pallas kernels  53.3 us (25%)
  local copies, waits for them, and re-layouts  16.9 us (8%)
  other arithmetic  2.96 us (1%)
    pallas_call x6, Pallas kernels, attention(): pl.pallas_call(functools.partial(attention_kernel, spec), out_shape=[piec...  41.5 us
    ppermute x21, starting transfers between devices, on_device(): arrived.append(lax.ppermute(pieces[k], 'section', pairs))  31.4 us
    ppermute x3, waiting for transfers between devices, on_device(): lax.ppermute(x_last, 'section', [(i, i + GROUP) for i in range(0, GROUP,...  28.2 us
    ppermute x1, waiting for transfers between devices, on_device(): low0 = lax.ppermute(chunk0, 'seq', forward)  18.5 us
    ppermute x1, waiting for transfers between devices, on_device(): high0 = lax.ppermute(chunk0, 'seq', backward)  15.8 us
    all_to_all x3, starting transfers between devices, exchange(): lax.all_to_all(array, 'section', 0, 0, axis_index_groups=groups, tiled=True)  12.7 us
    unnamed x98, local copies, waits for them, and re-layouts  10.4 us
    ppermute x5, starting transfers between devices, to_first_core(): return lax.ppermute(array, ('section', 'seq'), pairs)  9.71 us
  transfers between devices with their start and end apart: 36, of which 7 were waited for; matrix products, arithmetic and copies ran while one was open for 4% of the time, Pallas kernels for 23%

profile of v1, /device:TPU:198, one launch (start us, length us, event | category | flops | bytes accessed | tf_op | source)
XLA Modules:
  0.0 215.0 jit_solution(6071228231404759300)
XLA Ops:
  0.0 2.2 %shard_map.100 = bf16[8,384,128]{2,1,0:T(8,128)(2,1)} custom-call(bf16[1,384,2560]{2,1,0:T(8,128)(2,1)} %values.2), custom_call_target="tpu_custom_call" | custom-call | tf_op jit(solution)/shard_map/pallas_call | solution.py:307
  3.0 4.5 %all-to-all-start = ((f32[8,5,384]{2,1,0:T(8,128)}), f32[8,5,384]{2,1,0:T(8,128)S(1)}, u32[]{:S(2)}, u32[]{:S(2)}) async-start(f32[8,5,384]{2,1,0:T(8,128)} %maximum_bitcast_fusion), calls=%async_computation | async-start | bytes 196608 | tf_op jit(solution)/shard_map/all_to_all | solution.py:305
  7.5 3.2 %shard_map.101 = bf16[8,960,128]{2,1,0:T(8,128)(2,1)} custom-call(bf16[1,384,2560]{2,1,0:T(8,128)(2,1)} %values.2), custom_call_target="tpu_custom_call" | custom-call | tf_op jit(solution)/shard_map/pallas_call | solution.py:320
  10.7 2.6 %all-to-all-done.params = f32[8,5,384]{2,1,0:T(8,128)S(1)} async-done(((f32[8,5,384]{2,1,0:T(8,128)}), f32[8,5,384]{2,1,0:T(8,128)S(1)}, u32[]{:S(2)}, u32[]{:S(2)}) %all-to-all-start) | async-done | bytes 61472 | tf_op jit(solution)/shard_map/all_to_all | solution.py:305
  14.0 3.6 %all-to-all-start.1 = ((bf16[8,960,128]{2,1,0:T(8,128)(2,1)}), bf16[8,960,128]{2,1,0:T(8,128)(2,1)S(1)}, u32[]{:S(2)}, u32[]{:S(2)}) async-start(bf16[8,960,128]{2,1,0:T(8,128)(2,1)} %shard_map.101), calls=%async_computation.1 | async-start | bytes 3932160 | tf_op jit(solution)/shard_map/all_to_all | solution.py:305
  17.6 2.9 %collective-permute-start.24 = (bf16[8,384,128]{2,1,0:T(8,128)(2,1)S(1)}, bf16[8,384,128]{2,1,0:T(8,128)(2,1)S(1)}, u32[]{:S(2)}, u32[]{:S(2)}) collective-permute-start(bf16[8,384,128]{2,1,0:T(8,128)(2,1)S(1)} %copy-done.19), channel_id=1, source_target_pairs={{1,0},{2,1},{3,2},{4,3},{5,4},{6,5},{7,6},{8,7},{9,8},{10,9},{11,1... | collective-permute-start | bytes 2359304 | tf_op jit(solution)/shard_map/ppermute | solution.py:315
  20.5 3.0 %collective-permute-start.23 = (bf16[8,384,128]{2,1,0:T(8,128)(2,1)S(1)}, bf16[8,384,128]{2,1,0:T(8,128)(2,1)S(1)}, u32[]{:S(2)}, u32[]{:S(2)}) collective-permute-start(bf16[8,384,128]{2,1,0:T(8,128)(2,1)S(1)} %copy-done.19), channel_id=1, source_target_pairs={{0,1},{1,2},{2,3},{3,4},{4,5},{5,6},{6,7},{7,8},{8,9},{9,10},{10,1... | collective-permute-start | bytes 2359304 | tf_op jit(solution)/shard_map/ppermute | solution.py:314
  23.5 15.8 %collective-permute-done.24 = bf16[8,384,128]{2,1,0:T(8,128)(2,1)S(1)} collective-permute-done((bf16[8,384,128]{2,1,0:T(8,128)(2,1)S(1)}, bf16[8,384,128]{2,1,0:T(8,128)(2,1)S(1)}, u32[]{:S(2)}, u32[]{:S(2)}) %collective-permute-start.24) | collective-permute-done | bytes 786464 | tf_op jit(solution)/shard_map/ppermute | solution.py:315
  39.3 18.5 %collective-permute-done.23 = bf16[8,384,128]{2,1,0:T(8,128)(2,1)S(1)} collective-permute-done((bf16[8,384,128]{2,1,0:T(8,128)(2,1)S(1)}, bf16[8,384,128]{2,1,0:T(8,128)(2,1)S(1)}, u32[]{:S(2)}, u32[]{:S(2)}) %collective-permute-start.23) | collective-permute-done | bytes 786464 | tf_op jit(solution)/shard_map/ppermute | solution.py:314
  59.0 4.6 %all-to-all-start.2 = ((bf16[8,768,128]{2,1,0:T(8,128)(2,1)}), bf16[8,768,128]{2,1,0:T(8,128)(2,1)S(1)}, u32[]{:S(2)}, u32[]{:S(2)}) async-start(bf16[8,768,128]{2,1,0:T(8,128)(2,1)} %pad_maximum_fusion), calls=%async_computation.2 | async-start | bytes 3145728 | tf_op jit(solution)/shard_map/all_to_all | solution.py:305
  66.1 3.4 %collective-permute-start.1 = (bf16[8,192,128]{2,1,0:T(8,128)(2,1)}, bf16[8,192,128]{2,1,0:T(8,128)(2,1)}, u32[]{:S(2)}, u32[]{:S(2)}) collective-permute-start(bf16[8,192,128]{2,1,0:T(8,128)(2,1)} %slice.35), channel_id=1, source_target_pairs={{0,1},{1,2},{2,3},{3,4},{4,5},{5,6},{6,7},{7,8},{8,9},{9,10},{10,1... | collective-permute-start | bytes 1179656 | tf_op jit(solution)/shard_map/ppermute | solution.py:338
  70.7 2.5 %collective-permute-start.3 = (bf16[8,192,128]{2,1,0:T(8,128)(2,1)}, bf16[8,192,128]{2,1,0:T(8,128)(2,1)}, u32[]{:S(2)}, u32[]{:S(2)}) collective-permute-start(bf16[8,192,128]{2,1,0:T(8,128)(2,1)} %slice.35), channel_id=1, source_target_pairs={{1,0},{2,1},{3,2},{4,3},{5,4},{6,5},{7,6},{8,7},{9,8},{10,9},{11,1... | collective-permute-start | bytes 1179656 | tf_op jit(solution)/shard_map/ppermute | solution.py:338
  80.8 4.2 %collective-permute-start.13 = (bf16[8,384,128]{2,1,0:T(8,128)(2,1)}, bf16[8,384,128]{2,1,0:T(8,128)(2,1)}, u32[]{:S(2)}, u32[]{:S(2)}) collective-permute-start(bf16[8,384,128]{2,1,0:T(8,128)(2,1)} %slice.36), channel_id=1, source_target_pairs={{0,1},{1,2},{2,3},{3,4},{4,5},{5,6},{6,7},{7,8},{8,9},{9,10},{10,1... | collective-permute-start | bytes 2359304 | tf_op jit(solution)/shard_map/ppermute | solution.py:328
  85.1 1.9 collective-permute-start.14
  88.0 1.5 copy-done.12
  95.6 1.5 copy-done.13
  99.4 28.2 %collective-permute-done.5.x_in = bf16[384,128]{1,0:T(8,128)(2,1)} collective-permute-done((bf16[384,128]{1,0:T(8,128)(2,1)}, bf16[384,128]{1,0:T(8,128)(2,1)}, u32[]{:S(2)}, u32[]{:S(2)}) %collective-permute-start.5) | collective-permute-done | bytes 98336 | tf_op jit(solution)/shard_map/ppermute | solution.py:375
  127.6 11.6 %shard_map.103 = (bf16[384,128]{1,0:T(8,128)(2,1)S(1)}, bf16[384,128]{1,0:T(8,128)(2,1)S(1)}, bf16[384,128]{1,0:T(8,128)(2,1)S(1)}, bf16[384,128]{1,0:T(8,128)(2...) custom-call(s32[2]{0:T(128)S(1)} %pad_add_fusion.place, ...), custom_call_target="tpu_custom_call", output_to_operand_aliasing={{0}: (11, {}), {1}: (12, {}), {2}: (13, {}), {3}: (14, {}),... | custom-call | flops 3758096384 | bytes 2359296 | tf_op jit(solution)/shard_map/pallas_call | solution.py:240
  141.1 3.9 %collective-permute-start.7 = (bf16[384,128]{1,0:T(8,128)(2,1)S(1)}, bf16[384,128]{1,0:T(8,128)(2,1)S(1)}, u32[]{:S(2)}, u32[]{:S(2)}) collective-permute-start(bf16[384,128]{1,0:T(8,128)(2,1)S(1)} %get-tuple-element.79), channel_id=1, source_target_pairs={{0,32},{32,0},{64,96},{96,64},{128,160},{160,128},{192,224},{224,1... | collective-permute-start | bytes 294920 | tf_op jit(solution)/shard_map/ppermute | solution.py:384
  147.2 14.8 %shard_map.107 = (bf16[384,128]{1,0:T(8,128)(2,1)S(1)}, bf16[384,128]{1,0:T(8,128)(2,1)S(1)}, bf16[384,128]{1,0:T(8,128)(2,1)S(1)}, bf16[384,128]{1,0:T(8,128)(2...) custom-call(s32[2]{0:T(128)S(1)} %pad_add_fusion.place, ...), custom_call_target="tpu_custom_call", output_to_operand_aliasing={{0}: (8, {}), {1}: (9, {}), {2}: (10, {}), {3}: (11, {}), {... | custom-call | flops 3758096384 | bytes 2359296 | tf_op jit(solution)/shard_map/pallas_call | solution.py:240
  162.3 1.8 collective-permute-start.28
  164.0 2.7 %collective-permute-start.29 = (bf16[384,128]{1,0:T(8,128)(2,1)S(1)}, bf16[384,128]{1,0:T(8,128)(2,1)S(1)}, u32[]{:S(2)}, u32[]{:S(2)}) collective-permute-start(bf16[384,128]{1,0:T(8,128)(2,1)S(1)} %get-tuple-element.115), channel_id=1, source_target_pairs={{0,64},{16,80},{32,96},{48,112},{64,0},{80,16},{96,32},{112,48},{1... | collective-permute-start | bytes 294920 | tf_op jit(solution)/shard_map/ppermute | solution.py:384
  166.7 12.4 %shard_map.105 = (bf16[384,128]{1,0:T(8,128)(2,1)S(1)}, bf16[384,128]{1,0:T(8,128)(2,1)S(1)}, bf16[384,128]{1,0:T(8,128)(2,1)S(1)}, bf16[384,128]{1,0:T(8,128)(2...) custom-call(s32[2]{0:T(128)S(1)} %pad_add_fusion.place, ...), custom_call_target="tpu_custom_call", output_to_operand_aliasing={{0}: (8, {}), {1}: (9, {}), {2}: (10, {}), {3}: (11, {}), {... | custom-call | flops 3758096384 | bytes 2359296 | tf_op jit(solution)/shard_map/pallas_call | solution.py:240
  180.3 2.1 collective-permute-start.31
  183.7 2.5 %collective-permute-done.30.refs_5_ = bf16[384,128]{1,0:T(8,128)(2,1)S(1)} collective-permute-done((bf16[384,128]{1,0:T(8,128)(2,1)S(1)}, bf16[384,128]{1,0:T(8,128)(2,1)S(1)}, u32[]{:S(2)}, u32[]{:S(2)}) %collective-permute-start.30) | collective-permute-done | bytes 98336 | tf_op jit(solution)/shard_map/ppermute | solution.py:384
  186.2 2.3 %collective-permute-done.31.refs_6_ = bf16[384,128]{1,0:T(8,128)(2,1)S(1)} collective-permute-done((bf16[384,128]{1,0:T(8,128)(2,1)S(1)}, bf16[384,128]{1,0:T(8,128)(2,1)S(1)}, u32[]{:S(2)}, u32[]{:S(2)}) %collective-permute-start.31) | collective-permute-done | bytes 98336 | tf_op jit(solution)/shard_map/ppermute | solution.py:384
  192.9 1.8 collective-permute-start.22
  196.0 5.2 %collective-permute-start.9 = (bf16[384,128]{1,0:T(8,128)(2,1)}, bf16[384,128]{1,0:T(8,128)(2,1)S(1)}, u32[]{:S(2)}, u32[]{:S(2)}) collective-permute-start(bf16[384,128]{1,0:T(8,128)(2,1)} %get-tuple-element.81), channel_id=1, source_target_pairs={{0,64},{32,96},{64,0},{96,32},{128,192},{160,224},{192,128},{224,1... | collective-permute-start | bytes 294920 | tf_op jit(solution)/shard_map/ppermute | solution.py:384
  202.5 3.6 %collective-permute-start.11 = (bf16[384,128]{1,0:T(8,128)(2,1)}, bf16[384,128]{1,0:T(8,128)(2,1)S(1)}, u32[]{:S(2)}, u32[]{:S(2)}) collective-permute-start(bf16[384,128]{1,0:T(8,128)(2,1)} %get-tuple-element.83), channel_id=1, source_target_pairs={{0,96},{32,64},{64,32},{96,0},{128,224},{160,192},{192,160},{224,1... | collective-permute-start | bytes 294920 | tf_op jit(solution)/shard_map/ppermute | solution.py:384
  207.6 2.2 %shard_map.108.refs_8_ = bf16[1,384,2560]{2,1,0:T(8,128)(2,1)} custom-call(s32[2]{0:T(128)} %copy-done.11, bf16[384,128]{1,0:T(8,128)(2,1)} %copy-done, bf16[384,128]{1,0:T(8,128)(2,1)} %copy-done.20, bf16[384,128]{1,0:T(8,128)(2,1)} %copy-done.21, bf16[384,128]{1,0:T(8,128)(2,1)} %copy-done.22, bf16[384,128]{1,0:T(8,128)(2,1)} %copy-done.23, ...), custom_call_target="tpu_custom_call" | custom-call | tf_op jit(solution)/shard_map/pallas_call | solution.py:388
  209.8 2.2 %shard_map.109.refs_8_ = bf16[1,384,2560]{2,1,0:T(8,128)(2,1)} custom-call(s32[2]{0:T(128)} %copy-done.11, bf16[384,128]{1,0:T(8,128)(2,1)} %copy-done.7, bf16[384,128]{1,0:T(8,128)(2,1)} %copy-done.29, bf16[384,128]{1,0:T(8,128)(2,1)} %copy-done.30, bf16[384,128]{1,0:T(8,128)(2,1)} %copy-done.31, ...), custom_call_target="tpu_custom_call", output_to_operand_aliasing={{}: (9, {})} | custom-call | tf_op jit(solution)/shard_map/pallas_call | solution.py:388
  212.8 2.0 shard_map.110
  (178 shorter events, 38.9 us)
Async XLA Ops:
  3.0 10.3 %all-to-all-start = ((f32[8,5,384]{2,1,0:T(8,128)}), f32[8,5,384]{2,1,0:T(8,128)S(1)}, u32[]{:S(2)}, u32[]{:S(2)}) async-start(f32[8,5,384]{2,1,0:T(8,128)} %maximum_bitcast_fusion), calls=%async_computation | async-start | bytes 196608 | tf_op jit(solution)/shard_map/all_to_all | solution.py:305
  14.0 45.1 %all-to-all-start.1 = ((bf16[8,960,128]{2,1,0:T(8,128)(2,1)}), bf16[8,960,128]{2,1,0:T(8,128)(2,1)S(1)}, u32[]{:S(2)}, u32[]{:S(2)}) async-start(bf16[8,960,128]{2,1,0:T(8,128)(2,1)} %shard_map.101), calls=%async_computation.1 | async-start | bytes 3932160 | tf_op jit(solution)/shard_map/all_to_all | solution.py:305
  17.6 21.7 %collective-permute-start.24 = (bf16[8,384,128]{2,1,0:T(8,128)(2,1)S(1)}, bf16[8,384,128]{2,1,0:T(8,128)(2,1)S(1)}, u32[]{:S(2)}, u32[]{:S(2)}) collective-permute-start(bf16[8,384,128]{2,1,0:T(8,128)(2,1)S(1)} %copy-done.19), channel_id=1, source_target_pairs={{1,0},{2,1},{3,2},{4,3},{5,4},{6,5},{7,6},{8,7},{9,8},{10,9},{11,1... | collective-permute-start | bytes 2359304 | tf_op jit(solution)/shard_map/ppermute | solution.py:315
  20.5 37.2 %collective-permute-start.23 = (bf16[8,384,128]{2,1,0:T(8,128)(2,1)S(1)}, bf16[8,384,128]{2,1,0:T(8,128)(2,1)S(1)}, u32[]{:S(2)}, u32[]{:S(2)}) collective-permute-start(bf16[8,384,128]{2,1,0:T(8,128)(2,1)S(1)} %copy-done.19), channel_id=1, source_target_pairs={{0,1},{1,2},{2,3},{3,4},{4,5},{5,6},{6,7},{7,8},{8,9},{9,10},{10,1... | collective-permute-start | bytes 2359304 | tf_op jit(solution)/shard_map/ppermute | solution.py:314
  59.0 34.8 %all-to-all-start.2 = ((bf16[8,768,128]{2,1,0:T(8,128)(2,1)}), bf16[8,768,128]{2,1,0:T(8,128)(2,1)S(1)}, u32[]{:S(2)}, u32[]{:S(2)}) async-start(bf16[8,768,128]{2,1,0:T(8,128)(2,1)} %pad_maximum_fusion), calls=%async_computation.2 | async-start | bytes 3145728 | tf_op jit(solution)/shard_map/all_to_all | solution.py:305
  64.8 16.1 %collective-permute-start = (bf16[8,192,128]{2,1,0:T(8,128)(2,1)}, bf16[8,192,128]{2,1,0:T(8,128)(2,1)}, u32[]{:S(2)}, u32[]{:S(2)}) collective-permute-start(bf16[8,192,128]{2,1,0:T(8,128)(2,1)} %slice.35), channel_id=1, source_target_pairs={{16,0},{17,1},{18,2},{19,3},{20,4},{21,5},{22,6},{23,7},{24,8},{25... | collective-permute-start | bytes 1179656 | tf_op jit(solution)/shard_map/ppermute | solution.py:338
  66.1 19.0 %collective-permute-start.1 = (bf16[8,192,128]{2,1,0:T(8,128)(2,1)}, bf16[8,192,128]{2,1,0:T(8,128)(2,1)}, u32[]{:S(2)}, u32[]{:S(2)}) collective-permute-start(bf16[8,192,128]{2,1,0:T(8,128)(2,1)} %slice.35), channel_id=1, source_target_pairs={{0,1},{1,2},{2,3},{3,4},{4,5},{5,6},{6,7},{7,8},{8,9},{9,10},{10,1... | collective-permute-start | bytes 1179656 | tf_op jit(solution)/shard_map/ppermute | solution.py:338
  69.4 17.6 %collective-permute-start.2 = (bf16[8,192,128]{2,1,0:T(8,128)(2,1)}, bf16[8,192,128]{2,1,0:T(8,128)(2,1)}, u32[]{:S(2)}, u32[]{:S(2)}) collective-permute-start(bf16[8,192,128]{2,1,0:T(8,128)(2,1)} %slice.35), channel_id=1, source_target_pairs={{16,1},{17,2},{18,3},{19,4},{20,5},{21,6},{22,7},{23,8},{24,9},{25... | collective-permute-start | bytes 1179656 | tf_op jit(solution)/shard_map/ppermute | solution.py:338
  70.7 16.3 %collective-permute-start.3 = (bf16[8,192,128]{2,1,0:T(8,128)(2,1)}, bf16[8,192,128]{2,1,0:T(8,128)(2,1)}, u32[]{:S(2)}, u32[]{:S(2)}) collective-permute-start(bf16[8,192,128]{2,1,0:T(8,128)(2,1)} %slice.35), channel_id=1, source_target_pairs={{1,0},{2,1},{3,2},{4,3},{5,4},{6,5},{7,6},{8,7},{9,8},{10,9},{11,1... | collective-permute-start | bytes 1179656 | tf_op jit(solution)/shard_map/ppermute | solution.py:338
  73.2 13.8 %collective-permute-start.4 = (bf16[8,192,128]{2,1,0:T(8,128)(2,1)}, bf16[8,192,128]{2,1,0:T(8,128)(2,1)}, u32[]{:S(2)}, u32[]{:S(2)}) collective-permute-start(bf16[8,192,128]{2,1,0:T(8,128)(2,1)} %slice.35), channel_id=1, source_target_pairs={{17,0},{18,1},{19,2},{20,3},{21,4},{22,5},{23,6},{24,7},{25,8},{26... | collective-permute-start | bytes 1179656 | tf_op jit(solution)/shard_map/ppermute | solution.py:338
  80.8 64.2 %collective-permute-start.13 = (bf16[8,384,128]{2,1,0:T(8,128)(2,1)}, bf16[8,384,128]{2,1,0:T(8,128)(2,1)}, u32[]{:S(2)}, u32[]{:S(2)}) collective-permute-start(bf16[8,384,128]{2,1,0:T(8,128)(2,1)} %slice.36), channel_id=1, source_target_pairs={{0,1},{1,2},{2,3},{3,4},{4,5},{5,6},{6,7},{7,8},{8,9},{9,10},{10,1... | collective-permute-start | bytes 2359304 | tf_op jit(solution)/shard_map/ppermute | solution.py:328
  85.1 59.9 %collective-permute-start.14 = (bf16[8,384,128]{2,1,0:T(8,128)(2,1)}, bf16[8,384,128]{2,1,0:T(8,128)(2,1)}, u32[]{:S(2)}, u32[]{:S(2)}) collective-permute-start(bf16[8,384,128]{2,1,0:T(8,128)(2,1)} %slice.36), channel_id=1, source_target_pairs={{1,0},{2,1},{3,2},{4,3},{5,4},{6,5},{7,6},{8,7},{9,8},{10,9},{11,1... | collective-permute-start | bytes 2359304 | tf_op jit(solution)/shard_map/ppermute | solution.py:329
  92.6 35.0 %collective-permute-start.5 = (bf16[384,128]{1,0:T(8,128)(2,1)}, bf16[384,128]{1,0:T(8,128)(2,1)}, u32[]{:S(2)}, u32[]{:S(2)}) collective-permute-start(bf16[384,128]{1,0:T(8,128)(2,1)} %get-tuple-element.68), channel_id=1, source_target_pairs={{0,128},{32,160},{64,192},{96,224},{1,129},{33,161},{65,193},{97,2... | collective-permute-start | bytes 294920 | tf_op jit(solution)/shard_map/ppermute | solution.py:375
  98.1 49.1 %collective-permute-start.25 = (bf16[384,128]{1,0:T(8,128)(2,1)S(1)}, bf16[384,128]{1,0:T(8,128)(2,1)S(1)}, u32[]{:S(2)}, u32[]{:S(2)}) collective-permute-start(bf16[384,128]{1,0:T(8,128)(2,1)S(1)} %get-tuple-element.102), channel_id=1, source_target_pairs={{0,128},{16,144},{32,160},{48,176},{64,192},{80,208},{96,224},{112... | collective-permute-start | bytes 294920 | tf_op jit(solution)/shard_map/ppermute | solution.py:375
  139.8 22.5 %collective-permute-start.6 = (bf16[384,128]{1,0:T(8,128)(2,1)S(1)}, bf16[384,128]{1,0:T(8,128)(2,1)S(1)}, u32[]{:S(2)}, u32[]{:S(2)}) collective-permute-start(bf16[384,128]{1,0:T(8,128)(2,1)S(1)} %get-tuple-element.78), channel_id=1, source_target_pairs={{0,16},{32,48},{64,80},{96,112},{128,144},{160,176},{192,208},{224... | collective-permute-start | bytes 294920 | tf_op jit(solution)/shard_map/ppermute | solution.py:384
  141.1 38.7 %collective-permute-start.7 = (bf16[384,128]{1,0:T(8,128)(2,1)S(1)}, bf16[384,128]{1,0:T(8,128)(2,1)S(1)}, u32[]{:S(2)}, u32[]{:S(2)}) collective-permute-start(bf16[384,128]{1,0:T(8,128)(2,1)S(1)} %get-tuple-element.79), channel_id=1, source_target_pairs={{0,32},{32,0},{64,96},{96,64},{128,160},{160,128},{192,224},{224,1... | collective-permute-start | bytes 294920 | tf_op jit(solution)/shard_map/ppermute | solution.py:384
  145.9 18.1 %collective-permute-start.15 = (bf16[384,128]{1,0:T(8,128)(2,1)S(1)}, bf16[384,128]{1,0:T(8,128)(2,1)S(1)}, u32[]{:S(2)}, u32[]{:S(2)}) collective-permute-start(bf16[384,128]{1,0:T(8,128)(2,1)S(1)} %get-tuple-element.85), channel_id=1, source_target_pairs={{0,128},{16,144},{32,160},{48,176},{64,192},{80,208},{96,224},{112... | collective-permute-start | bytes 294920 | tf_op jit(solution)/shard_map/ppermute | solution.py:375
  162.1 18.2 %collective-permute-start.26 = (bf16[384,128]{1,0:T(8,128)(2,1)S(1)}, bf16[384,128]{1,0:T(8,128)(2,1)S(1)}, u32[]{:S(2)}, u32[]{:S(2)}) collective-permute-start(bf16[384,128]{1,0:T(8,128)(2,1)S(1)} %get-tuple-element.112), channel_id=1, source_target_pairs={{0,16},{16,0},{32,48},{48,32},{64,80},{80,64},{96,112},{112,96},{1... | collective-permute-start | bytes 294920 | tf_op jit(solution)/shard_map/ppermute | solution.py:384
  162.2 20.2 %collective-permute-start.27 = (bf16[384,128]{1,0:T(8,128)(2,1)S(1)}, bf16[384,128]{1,0:T(8,128)(2,1)S(1)}, u32[]{:S(2)}, u32[]{:S(2)}) collective-permute-start(bf16[384,128]{1,0:T(8,128)(2,1)S(1)} %get-tuple-element.113), channel_id=1, source_target_pairs={{0,32},{16,48},{32,0},{48,16},{64,96},{80,112},{96,64},{112,80},{1... | collective-permute-start | bytes 294920 | tf_op jit(solution)/shard_map/ppermute | solution.py:384
  162.3 21.0 %collective-permute-start.28 = (bf16[384,128]{1,0:T(8,128)(2,1)S(1)}, bf16[384,128]{1,0:T(8,128)(2,1)S(1)}, u32[]{:S(2)}, u32[]{:S(2)}) collective-permute-start(bf16[384,128]{1,0:T(8,128)(2,1)S(1)} %get-tuple-element.114), channel_id=1, source_target_pairs={{0,48},{16,32},{32,16},{48,0},{64,112},{80,96},{96,80},{112,64},{1... | collective-permute-start | bytes 294920 | tf_op jit(solution)/shard_map/ppermute | solution.py:384
  164.0 19.6 %collective-permute-start.29 = (bf16[384,128]{1,0:T(8,128)(2,1)S(1)}, bf16[384,128]{1,0:T(8,128)(2,1)S(1)}, u32[]{:S(2)}, u32[]{:S(2)}) collective-permute-start(bf16[384,128]{1,0:T(8,128)(2,1)S(1)} %get-tuple-element.115), channel_id=1, source_target_pairs={{0,64},{16,80},{32,96},{48,112},{64,0},{80,16},{96,32},{112,48},{1... | collective-permute-start | bytes 294920 | tf_op jit(solution)/shard_map/ppermute | solution.py:384
  180.3 8.2 %collective-permute-start.31 = (bf16[384,128]{1,0:T(8,128)(2,1)S(1)}, bf16[384,128]{1,0:T(8,128)(2,1)S(1)}, u32[]{:S(2)}, u32[]{:S(2)}) collective-permute-start(bf16[384,128]{1,0:T(8,128)(2,1)S(1)} %get-tuple-element.117), channel_id=1, source_target_pairs={{0,96},{16,112},{32,64},{48,80},{64,32},{80,48},{96,0},{112,16},{1... | collective-permute-start | bytes 294920 | tf_op jit(solution)/shard_map/ppermute | solution.py:384
  182.4 8.2 %collective-permute-start.32 = (bf16[384,128]{1,0:T(8,128)(2,1)S(1)}, bf16[384,128]{1,0:T(8,128)(2,1)S(1)}, u32[]{:S(2)}, u32[]{:S(2)}) collective-permute-start(bf16[384,128]{1,0:T(8,128)(2,1)S(1)} %get-tuple-element.118), channel_id=1, source_target_pairs={{0,112},{16,96},{32,80},{48,64},{64,48},{80,32},{96,16},{112,0},{1... | collective-permute-start | bytes 294920 | tf_op jit(solution)/shard_map/ppermute | solution.py:384
  183.7 9.3 %collective-permute-start.17 = (bf16[384,128]{1,0:T(8,128)(2,1)S(1)}, bf16[384,128]{1,0:T(8,128)(2,1)S(1)}, u32[]{:S(2)}, u32[]{:S(2)}) collective-permute-start(bf16[384,128]{1,0:T(8,128)(2,1)S(1)} %get-tuple-element.96), channel_id=1, source_target_pairs={{0,32},{16,48},{32,0},{48,16},{64,96},{80,112},{96,64},{112,80},{1... | collective-permute-start | bytes 294920 | tf_op jit(solution)/shard_map/ppermute | solution.py:384
  186.2 8.5 %collective-permute-start.18 = (bf16[384,128]{1,0:T(8,128)(2,1)S(1)}, bf16[384,128]{1,0:T(8,128)(2,1)S(1)}, u32[]{:S(2)}, u32[]{:S(2)}) collective-permute-start(bf16[384,128]{1,0:T(8,128)(2,1)S(1)} %get-tuple-element.97), channel_id=1, source_target_pairs={{0,48},{16,32},{32,16},{48,0},{64,112},{80,96},{96,80},{112,64},{1... | collective-permute-start | bytes 294920 | tf_op jit(solution)/shard_map/ppermute | solution.py:384
  190.5 10.7 %collective-permute-start.20 = (bf16[384,128]{1,0:T(8,128)(2,1)S(1)}, bf16[384,128]{1,0:T(8,128)(2,1)S(1)}, u32[]{:S(2)}, u32[]{:S(2)}) collective-permute-start(bf16[384,128]{1,0:T(8,128)(2,1)S(1)} %get-tuple-element.99), channel_id=1, source_target_pairs={{0,80},{16,64},{32,112},{48,96},{64,16},{80,0},{96,48},{112,32},{1... | collective-permute-start | bytes 294920 | tf_op jit(solution)/shard_map/ppermute | solution.py:384
  191.4 11.1 %collective-permute-start.21 = (bf16[384,128]{1,0:T(8,128)(2,1)S(1)}, bf16[384,128]{1,0:T(8,128)(2,1)S(1)}, u32[]{:S(2)}, u32[]{:S(2)}) collective-permute-start(bf16[384,128]{1,0:T(8,128)(2,1)S(1)} %get-tuple-element.100), channel_id=1, source_target_pairs={{0,96},{16,112},{32,64},{48,80},{64,32},{80,48},{96,0},{112,16},{1... | collective-permute-start | bytes 294920 | tf_op jit(solution)/shard_map/ppermute | solution.py:384
  192.9 13.2 %collective-permute-start.22 = (bf16[384,128]{1,0:T(8,128)(2,1)S(1)}, bf16[384,128]{1,0:T(8,128)(2,1)S(1)}, u32[]{:S(2)}, u32[]{:S(2)}) collective-permute-start(bf16[384,128]{1,0:T(8,128)(2,1)S(1)} %get-tuple-element.101), channel_id=1, source_target_pairs={{0,112},{16,96},{32,80},{48,64},{64,48},{80,32},{96,16},{112,0},{1... | collective-permute-start | bytes 294920 | tf_op jit(solution)/shard_map/ppermute | solution.py:384
  194.7 17.3 %collective-permute-start.8 = (bf16[384,128]{1,0:T(8,128)(2,1)}, bf16[384,128]{1,0:T(8,128)(2,1)S(1)}, u32[]{:S(2)}, u32[]{:S(2)}) collective-permute-start(bf16[384,128]{1,0:T(8,128)(2,1)} %get-tuple-element.80), channel_id=1, source_target_pairs={{0,48},{32,16},{64,112},{96,80},{128,176},{160,144},{192,240},{224... | collective-permute-start | bytes 294920 | tf_op jit(solution)/shard_map/ppermute | solution.py:384
  196.0 16.0 %collective-permute-start.9 = (bf16[384,128]{1,0:T(8,128)(2,1)}, bf16[384,128]{1,0:T(8,128)(2,1)S(1)}, u32[]{:S(2)}, u32[]{:S(2)}) collective-permute-start(bf16[384,128]{1,0:T(8,128)(2,1)} %get-tuple-element.81), channel_id=1, source_target_pairs={{0,64},{32,96},{64,0},{96,32},{128,192},{160,224},{192,128},{224,1... | collective-permute-start | bytes 294920 | tf_op jit(solution)/shard_map/ppermute | solution.py:384
  201.2 10.8 %collective-permute-start.10 = (bf16[384,128]{1,0:T(8,128)(2,1)}, bf16[384,128]{1,0:T(8,128)(2,1)S(1)}, u32[]{:S(2)}, u32[]{:S(2)}) collective-permute-start(bf16[384,128]{1,0:T(8,128)(2,1)} %get-tuple-element.82), channel_id=1, source_target_pairs={{0,80},{32,112},{64,16},{96,48},{128,208},{160,240},{192,144},{224... | collective-permute-start | bytes 294920 | tf_op jit(solution)/shard_map/ppermute | solution.py:384
  202.5 9.5 %collective-permute-start.11 = (bf16[384,128]{1,0:T(8,128)(2,1)}, bf16[384,128]{1,0:T(8,128)(2,1)S(1)}, u32[]{:S(2)}, u32[]{:S(2)}) collective-permute-start(bf16[384,128]{1,0:T(8,128)(2,1)} %get-tuple-element.83), channel_id=1, source_target_pairs={{0,96},{32,64},{64,32},{96,0},{128,224},{160,192},{192,160},{224,1... | collective-permute-start | bytes 294920 | tf_op jit(solution)/shard_map/ppermute | solution.py:384
  (53 other events, 602.8 us)

commit v2 on v0

v2 whole, which is shorter than its diff:
```python
import functools
import math

import jax
import jax.numpy as jnp
from jax import lax
from jax.experimental import pallas as pl
from jax.experimental.pallas import tpu as pltpu
from jax.sharding import PartitionSpec as P

HD = 128
TILE = 64
HT = 2
WT = 3
NPATCH = 6
ROWS = 384
HALF = 192
CHANNELS = 2560
GROUP = 8
LAYERS = 8
KEYS = 1536
COLKEYS = 512
MASKED = -16384.0
QUERY_SCALE = math.log2(math.e) / math.sqrt(HD)
EPS = 1e-06

ANY = pl.BlockSpec(memory_space=pl.ANY)
VMEM = pl.BlockSpec(memory_space=pltpu.VMEM)
SMEM = pl.BlockSpec(memory_space=pltpu.SMEM)
HBM = pl.BlockSpec(memory_space=pltpu.HBM)

SMALL = pl.CostEstimate(flops=0, bytes_accessed=1024, transcendentals=0)

QUERY_ROWS = ((0, 256), (0, 384), (128, 384))


def column_order():
    return [(row, column) for column in range(WT) for row in range(HT)]


def eight_heads_kernel(values, chunk):
    for d in range(GROUP):
        chunk[d] = values[0, :, d * HD : (d + 1) * HD]


def by_owner_kernel(values, _, owned):
    for d in range(GROUP):
        second, head, half = GROUP + d, 2 * GROUP + d // 2, (d % 2) * HALF
        owned[d, :ROWS] = values[0, :, d * HD : (d + 1) * HD]
        owned[d, ROWS : 2 * ROWS] = values[0, :, second * HD : (second + 1) * HD]
        owned[d, 2 * ROWS :] = values[0, half : half + HALF, head * HD : (head + 1) * HD]


def split_kernel(owned, low, high, vectors, second, last):
    second[...] = owned[:, ROWS : 2 * ROWS]
    last[...] = owned[:, 2 * ROWS :]


def join_kernel(low, high, _, joined):
    joined[:, :ROWS] = low[...]
    joined[:, ROWS:] = high[...]


def pass_kernel(*refs):
    pass


def home_kernel(parts, *refs):
    sems, out = refs[-1], refs[-2]
    copies = []
    for piece, row, first_head, step in parts:
        for i, d in enumerate(range(0, GROUP, step)):
            copies.append(
                pltpu.make_async_copy(
                    refs[piece].at[d, pl.ds(row, ROWS)],
                    out.at[0, :, pl.ds((first_head + i) * HD, HD)],
                    sems.at[len(copies)],
                )
            )
    for copy in copies:
        copy.start()
    for copy in copies:
        copy.wait()


def row_scale(matrix):
    return lax.rsqrt(jnp.mean(matrix * matrix, axis=-1, keepdims=True) + EPS)


def attention_kernel(spec, place, x_in, params, bias, *refs):
    heads, stage, n_kv, n_skip, first_row = spec
    n_heads = len(heads)
    kv_refs = refs[:n_kv]
    layers_out, x_out = refs[n_kv + n_skip : n_kv + n_skip + 2]
    scratch = refs[n_kv + n_skip + 2 :]
    x_buf, kv_buf, out_buf = scratch[:3]
    key_bufs = scratch[3 : 3 + n_heads]
    value_bufs = scratch[3 + n_heads : 3 + 2 * n_heads]
    query_bufs = scratch[3 + 2 * n_heads : 3 + 3 * n_heads]
    kv_sems, x_sems, out_sems = scratch[3 + 3 * n_heads :]
    mine, upper = place[1], place[2]

    def work(count):
        def x_copy(h):
            chunk = heads[h][0]
            if stage == 0:
                head = 2 * GROUP + lax.div(mine, 2) if chunk == 2 else chunk * GROUP + mine
                source = x_in.at[:, pl.ds(pl.multiple_of(head * HD, HD), HD)]
            else:
                source = x_in.at[h]
            return pltpu.make_async_copy(source, x_buf.at[h], x_sems.at[h])

        def kv_copies(layer, h):
            return [
                pltpu.make_async_copy(
                    kv_refs[ref].at[layer, pl.ds(at, rows)],
                    kv_buf.at[h, layer, kind, pl.ds(to, rows)],
                    kv_sems.at[h, layer, i],
                )
                for i, (ref, at, rows, kind, to) in enumerate(heads[h][1])
            ]

        def out_copy(layer, h):
            return pltpu.make_async_copy(
                out_buf.at[h, layer],
                layers_out.at[layer, pl.ds(first_row + h * ROWS, ROWS)],
                out_sems.at[h, layer],
            )

        for h in range(count):
            x_copy(h).start()
        for layer in range(LAYERS):
            for h in range(count):
                for copy in kv_copies(layer, h):
                    copy.start()

        tile_of_row = lax.broadcasted_iota(jnp.int32, (KEYS, HD), 0) // TILE
        tile_of_lane = lax.broadcasted_iota(jnp.int32, (KEYS, HD), 1)
        one_hot = jnp.where(tile_of_row == tile_of_lane, 1.0, 0.0).astype(jnp.bfloat16)
        for h in range(count):
            key_bufs[h][:, HD:] = one_hot
            value_bufs[h][:, HD:] = jnp.ones((KEYS, HD), jnp.bfloat16)
            query_bufs[h][:, HD:] = bias[...]

        first = []
        for h in range(count):
            x_copy(h).wait()
            if stage == 0:
                x = jnp.concatenate(
                    [
                        x_buf[h, (row * WT + column) * TILE : (row * WT + column + 1) * TILE]
                        for row, column in column_order()
                    ],
                    axis=0,
                )
            else:
                x = x_buf[h]
            first.append(x.astype(jnp.float32))

        def layer_step(layer, xs):
            def gain(h, i):
                chunk = heads[h][0]
                return params[layer, i : i + 1, chunk * HD : (chunk + 1) * HD]

            for h in range(count):
                for copy in kv_copies(layer, h):
                    copy.wait()
            for h in range(count):
                key_gain = gain(h, 3)
                for column in range(WT):
                    for slot, which in ((0, 1), (2, 2), (4, 0)):
                        for row in range(HT):
                            at = column * COLKEYS + (slot + row) * TILE
                            tile = (row * WT + column) * TILE
                            stale = kv_buf[h, layer, which, tile : tile + TILE]
                            value_bufs[h][at : at + TILE, :HD] = stale
                            wide = stale.astype(jnp.float32)
                            key_bufs[h][at : at + TILE, :HD] = (
                                wide * row_scale(wide) * key_gain
                            ).astype(jnp.bfloat16)

            for h in range(count):
                x = xs[h]
                hidden = x * row_scale(x) * (1.0 + gain(h, 0)) + gain(h, 1)
                new_values = hidden.astype(jnp.bfloat16)
                scaled = hidden * row_scale(hidden)
                new_keys = (scaled * gain(h, 3)).astype(jnp.bfloat16)
                query_bufs[h][:, :HD] = (scaled * (gain(h, 2) * QUERY_SCALE)).astype(jnp.bfloat16)
                for column in range(WT):
                    at = column * COLKEYS + 6 * TILE
                    rows = slice(column * 2 * TILE, (column + 1) * 2 * TILE)
                    value_bufs[h][at : at + 2 * TILE, :HD] = new_values[rows]
                    key_bufs[h][at : at + 2 * TILE, :HD] = new_keys[rows]

            sums = [[] for _ in range(count)]
            for column in range(WT):
                keys = slice(column * COLKEYS, (column + 1) * COLKEYS)
                begin, end = QUERY_ROWS[column]
                for h in range(count):
                    scores = lax.dot_general(
                        query_bufs[h][begin:end],
                        key_bufs[h][keys],
                        (((1,), (1,)), ((), ())),
                        preferred_element_type=jnp.float32,
                    )
                    weights = jnp.exp2(scores).astype(jnp.bfloat16)
                    sums[h].append(
                        jnp.dot(weights, value_bufs[h][keys], preferred_element_type=jnp.float32)
                    )
            results = []
            for h in range(count):
                left, middle, right = sums[h]
                total = [
                    left[:128] + middle[:128],
                    left[128:] + middle[128:256] + right[:128],
                    middle[256:] + right[128:],
                ]
                mixed = jnp.concatenate([t[:, :HD] / t[:, HD:] for t in total], axis=0)
                out = (xs[h] + gain(h, 4) * mixed).astype(jnp.bfloat16)
                for i, (row, column) in enumerate(column_order()):
                    tile = (row * WT + column) * TILE
                    out_buf[h, layer, tile : tile + TILE] = out[i * TILE : (i + 1) * TILE]
                out_copy(layer, h).start()
                results.append(out.astype(jnp.float32))
            return tuple(results)

        last = lax.fori_loop(0, LAYERS, layer_step, tuple(first))
        ends = []
        for h in range(count):
            x_buf[h] = last[h].astype(jnp.bfloat16)
            ends.append(pltpu.make_async_copy(x_buf.at[h], x_out.at[h], x_sems.at[h]))
            ends[-1].start()
        for h in range(count):
            for layer in range(LAYERS):
                out_copy(layer, h).wait()
            ends[h].wait()

    works = upper == stage
    if heads[0][0] == 2:
        works = works & (lax.rem(mine, 2) == 0)
    pl.when(works)(lambda: work(n_heads))


def attention(place, x_in, params, bias, kv, heads, stage, previous, before, first_row, rows):
    n_heads = len(heads)
    skipped = list(previous) + list(before)
    n_copies = max(len(head[1]) for head in heads)
    return pl.pallas_call(
        functools.partial(attention_kernel, (heads, stage, len(kv), len(skipped), first_row)),
        out_shape=[
            jax.ShapeDtypeStruct((LAYERS, rows, HD), jnp.bfloat16),
            jax.ShapeDtypeStruct((n_heads, ROWS, HD), jnp.bfloat16),
        ],
        in_specs=[SMEM, HBM if stage == 0 else ANY, VMEM, VMEM]
        + [ANY] * len(kv)
        + [HBM] * len(previous)
        + [ANY] * len(before),
        out_specs=[HBM, ANY],
        scratch_shapes=[
            pltpu.VMEM((n_heads, ROWS, HD), jnp.bfloat16),
            pltpu.VMEM((n_heads, LAYERS, 3, ROWS, HD), jnp.bfloat16),
            pltpu.VMEM((n_heads, LAYERS, ROWS, HD), jnp.bfloat16),
        ]
        + [pltpu.VMEM((KEYS, 2 * HD), jnp.bfloat16)] * (2 * n_heads)
        + [pltpu.VMEM((ROWS, 2 * HD), jnp.bfloat16)] * n_heads
        + [
            pltpu.SemaphoreType.DMA((n_heads, LAYERS, n_copies)),
            pltpu.SemaphoreType.DMA((n_heads,)),
            pltpu.SemaphoreType.DMA((n_heads, LAYERS)),
        ],
        input_output_aliases={4 + len(kv): 0} if previous else {},
        compiler_params=pltpu.CompilerParams(vmem_limit_bytes=32 * 1024 * 1024),
        cost_estimate=SMALL,
    )(place, x_in, params, bias, *kv, *skipped)


def bias_table(tile_list, tile_count, plan, block_index):
    slot_live = jnp.arange(tile_list.shape[1])[None, :] < tile_count[:, None]
    window_ids = (block_index - 1) * NPATCH + jnp.arange(3 * NPATCH)
    window = jnp.any(
        (tile_list[:, :, None] == window_ids[None, None, :]) & slot_live[:, :, None], axis=1
    )
    patches = jnp.arange(NPATCH)
    position = jnp.sum(jnp.where(plan[None, :] == patches[:, None], patches[None, :], 0), axis=1)
    is_new = position[None, :] <= position[:, None]
    near = window[:, NPATCH : 2 * NPATCH]
    kinds = [window[:, :NPATCH], window[:, 2 * NPATCH :], near & ~is_new, near & is_new]
    listed = jnp.stack(kinds, axis=1).reshape(NPATCH, 4, HT, WT).transpose(0, 3, 1, 2)
    listed = listed.reshape(HT, WT, 4 * NPATCH).transpose(1, 0, 2).reshape(NPATCH, 4 * NPATCH)
    bias = jnp.where(listed, 0.0, MASKED).astype(jnp.bfloat16)
    bias = jnp.pad(bias, ((0, 0), (0, HD - 4 * NPATCH)))
    return jnp.repeat(bias, TILE, axis=0)


def on_device(
    tokens_in,
    stale_values,
    mod_scale,
    mod_shift,
    query_gain,
    key_gain,
    branch_gain,
    tile_list,
    tile_count,
    patch_order,
):
    n_section, n_seq = lax.axis_size("section"), lax.axis_size("seq")
    section = lax.axis_index("section")
    mine = lax.rem(section, GROUP)
    upper = lax.div(section, GROUP)
    groups = [list(range(GROUP)), list(range(GROUP, 2 * GROUP))]
    forward = [(i, i + 1) for i in range(n_seq - 1)]
    backward = [(i + 1, i) for i in range(n_seq - 1)]
    place = jnp.stack([section, mine, upper]).astype(jnp.int32)

    def exchange(array):
        return lax.all_to_all(array, "section", 0, 0, axis_index_groups=groups, tiled=True)

    def both_ways(array):
        return lax.ppermute(array, "seq", forward), lax.ppermute(array, "seq", backward)

    def shape(*dims):
        return jax.ShapeDtypeStruct(dims, jnp.bfloat16)

    def call(kernel, out_shape, in_specs, out_specs, *args, **options):
        return pl.pallas_call(
            kernel,
            out_shape=out_shape,
            in_specs=in_specs,
            out_specs=out_specs,
            cost_estimate=SMALL,
            **options,
        )(*args)

    raw = call(
        eight_heads_kernel,
        shape(GROUP, ROWS, HD),
        [pl.BlockSpec((1, ROWS, GROUP * HD), lambda i: (0, 0, 0))],
        pl.BlockSpec((GROUP, ROWS, HD), lambda i: (0, 0, 0)),
        stale_values,
        grid=(1,),
    )
    raw_sides = both_ways(raw)
    own = exchange(
        call(
            by_owner_kernel,
            shape(GROUP, 2 * ROWS + HALF, HD),
            [VMEM, ANY],
            VMEM,
            stale_values,
            raw,
        )
    )

    vectors = jnp.concatenate(
        [mod_scale, mod_shift, query_gain, key_gain, branch_gain], axis=0
    ).reshape(5, 20, HD)
    vectors = jnp.concatenate(
        [
            vectors[:, :GROUP],
            vectors[:, GROUP : 2 * GROUP],
            jnp.repeat(vectors[:, 2 * GROUP :], 2, axis=1),
        ],
        axis=-1,
    ).transpose(1, 0, 2)
    vectors = call(
        pass_kernel,
        jax.ShapeDtypeStruct(vectors.shape, vectors.dtype),
        [HBM, ANY],
        HBM,
        vectors,
        own,
        input_output_aliases={0: 0},
    )
    params = exchange(vectors)
    bias = bias_table(tile_list, tile_count, patch_order[0], lax.axis_index("seq"))

    own_b, own_c = call(
        split_kernel,
        [shape(GROUP, ROWS, HD), shape(GROUP, HALF, HD)],
        [VMEM, ANY, ANY, ANY],
        [VMEM, VMEM],
        own,
        *raw_sides,
        params,
    )
    sides_b = both_ways(own_b)
    joined = call(
        join_kernel, shape(GROUP, 2 * ROWS, HD), [VMEM, VMEM, ANY], VMEM, *raw_sides, own_b
    )
    sides_a = exchange(joined)

    def to_first_core(array, step, from_core):
        pairs = []
        for s in range(from_core, n_section, 2):
            for f in range(n_seq):
                if 0 <= f + step < n_seq:
                    pairs.append((s * n_seq + f, (s - from_core) * n_seq + f + step))
        return lax.ppermute(array, ("section", "seq"), pairs)

    sides_c = [to_first_core(own_c, step, c) for step in (1, -1) for c in range(2)]
    own_c_other = to_first_core(own_c, 0, 1)

    head_a = (0, ((0, 0, ROWS, 0, 0), (1, 0, ROWS, 1, 0), (1, ROWS, ROWS, 2, 0)))
    head_b = (1, tuple((i, 0, ROWS, i, 0) for i in range(3)))
    head_c = (2, tuple((i, 0, HALF, i // 2, (i % 2) * HALF) for i in range(6)))
    kinds = {
        "a": ([own, sides_a], (head_a,), 0, 2 * ROWS),
        "b": ([own_b, *sides_b], (head_b,), ROWS, 2 * ROWS),
        "c": ([own_c, own_c_other, *sides_c], (head_c,), 0, ROWS),
    }

    def run(name, stage, x_in, previous, before):
        kv, heads, *rows = kinds[name]
        return attention(place, x_in, params, bias, kv, heads, stage, previous, before, *rows)

    def hop(last, step):
        return lax.ppermute(last, "section", [(i, i + GROUP) for i in range(0, GROUP, step)])

    def home(pieces, parts, out):
        before = [] if out is None else [out]
        return call(
            functools.partial(home_kernel, parts),
            shape(1, ROWS, CHANNELS),
            [VMEM] * len(pieces) + [HBM] * len(before),
            HBM,
            *pieces,
            *before,
            scratch_shapes=[pltpu.SemaphoreType.DMA((3 * GROUP,))],
            input_output_aliases={len(pieces): 0} if before else {},
        )

    layers, last_a = run("a", 0, tokens_in, [], [])
    next_a = hop(last_a, 1)
    layers, last_b = run("b", 0, tokens_in, [layers], [])
    next_b = hop(last_b, 1)
    layers, done_a = run("a", 1, next_a, [layers], [])
    layers_c, last_c = run("c", 0, tokens_in, [], [done_a, next_b])
    next_c = hop(last_c, 2)
    layers, done_b = run("b", 1, next_b, [layers], [last_c])
    layers = call(
        pass_kernel,
        shape(LAYERS, 2 * ROWS, HD),
        [HBM, ANY],
        HBM,
        layers,
        next_c,
        input_output_aliases={0: 0},
    )
    layers_c, _ = run("c", 1, next_c, [layers_c], [done_b])
    out = home([exchange(layers)], ((0, 0, 0, 1), (0, ROWS, GROUP, 1)), None)
    out = home([exchange(layers_c)], ((0, 0, 2 * GROUP, 2),), out)
    return out


def solution(mesh):
    return jax.shard_map(
        on_device,
        mesh=mesh,
        in_specs=(
            P("seq", None),
            P("section", "seq", None),
            P("section", None),
            P("section", None),
            P("section", None),
            P("section", None),
            P("section", None),
            P("seq", None),
            P("seq"),
            P("seq", None),
        ),
        out_specs=P("section", "seq", None),
        check_vma=False,
    )
```

time: 1080 us -> 206 us (0.19)
  the two profiles are of different devices: /device:TPU:221 before, /device:TPU:198 now
where the time goes in v2:
time: 206 us; the launch traced here: 203 us
  waiting for transfers between devices  84.8 us (41%)
  Pallas kernels  53.9 us (26%)
  starting transfers between devices  45.5 us (22%)
  local copies, waits for them, and re-layouts  17.1 us (8%)
    all_to_all x5, waiting for transfers between devices, exchange(): lax.all_to_all(array, 'section', 0, 0, axis_index_groups=groups, tiled=True)  42.9 us
    pallas_call x6, Pallas kernels, attention(): pl.pallas_call(functools.partial(attention_kernel, (heads, stage, len(kv)...  38.5 us
    ppermute x3, waiting for transfers between devices, hop(): lax.ppermute(last, 'section', [(i, i + GROUP) for i in range(0, GROUP, st...  37.5 us
    all_to_all x5, starting transfers between devices, exchange(): lax.all_to_all(array, 'section', 0, 0, axis_index_groups=groups, tiled=True)  20.2 us
    pallas_call x8, Pallas kernels, call(): pl.pallas_call(kernel, out_shape=out_shape, in_specs=in_specs, out_specs=...  15.4 us
    ppermute x5, starting transfers between devices, to_first_core(): return lax.ppermute(array, ('section', 'seq'), pairs)  9.69 us
    unnamed x46, local copies, waits for them, and re-layouts  9.66 us
    ppermute x2, starting transfers between devices, both_ways(): lax.ppermute(array, 'seq', forward)  5.88 us
  transfers between devices with their start and end apart: 17, of which 6 were waited for; matrix products, arithmetic and copies ran while one was open for 4% of the time, Pallas kernels for 20%

profile of v2, /device:TPU:198, one launch (start us, length us, event | category | flops | bytes accessed | tf_op | source)
XLA Modules:
  0.0 203.4 jit_solution(16659910454749097938)
XLA Ops:
  0.0 2.2 %shard_map.100._ = bf16[8,384,128]{2,1,0:T(8,128)(2,1)} custom-call(bf16[1,384,2560]{2,1,0:T(8,128)(2,1)} %values.3), custom_call_target="tpu_custom_call" | custom-call | bytes 1024 | tf_op jit(solution)/shard_map/pallas_call | solution.py:326
  2.2 3.2 %shard_map.101 = bf16[8,960,128]{2,1,0:T(8,128)(2,1)} custom-call(bf16[1,384,2560]{2,1,0:T(8,128)(2,1)} %values.3, bf16[8,384,128]{2,1,0:T(8,128)(2,1)} %shard_map.100._), custom_call_target="tpu_custom_call" | custom-call | bytes 1024 | tf_op jit(solution)/shard_map/pallas_call | solution.py:326
  5.3 4.6 %all-to-all-start = ((bf16[8,960,128]{2,1,0:T(8,128)(2,1)}), bf16[8,960,128]{2,1,0:T(8,128)(2,1)S(1)}, u32[]{:S(2)}, u32[]{:S(2)}) async-start(bf16[8,960,128]{2,1,0:T(8,128)(2,1)} %shard_map.101), calls=%async_computation | async-start | bytes 3932160 | tf_op jit(solution)/shard_map/all_to_all | solution.py:317
  9.9 2.9 %collective-permute-start = (bf16[8,384,128]{2,1,0:T(8,128)(2,1)S(1)}, bf16[8,384,128]{2,1,0:T(8,128)(2,1)S(1)}, u32[]{:S(2)}, u32[]{:S(2)}) collective-permute-start(bf16[8,384,128]{2,1,0:T(8,128)(2,1)S(1)} %copy-done.17), channel_id=1, source_target_pairs={{0,1},{1,2},{2,3},{3,4},{4,5},{5,6},{6,7},{7,8},{8,9},{9,10},{10,1... | collective-permute-start | bytes 2359304 | tf_op jit(solution)/shard_map/ppermute | solution.py:320
  12.9 2.9 %collective-permute-start.1 = (bf16[8,384,128]{2,1,0:T(8,128)(2,1)S(1)}, bf16[8,384,128]{2,1,0:T(8,128)(2,1)}, u32[]{:S(2)}, u32[]{:S(2)}) collective-permute-start(bf16[8,384,128]{2,1,0:T(8,128)(2,1)S(1)} %copy-done.17), channel_id=1, source_target_pairs={{1,0},{2,1},{3,2},{4,3},{5,4},{6,5},{7,6},{8,7},{9,8},{10,9},{11,1... | collective-permute-start | bytes 2359304 | tf_op jit(solution)/shard_map/ppermute | solution.py:320
  15.8 1.5 concatenate.7
  19.4 16.3 %all-to-all-done.refs_1_.owned.refs_0_ = bf16[8,960,128]{2,1,0:T(8,128)(2,1)S(1)} async-done(((bf16[8,960,128]{2,1,0:T(8,128)(2,1)}), bf16[8,960,128]{2,1,0:T(8,128)(2,1)S(1)}, u32[]{:S(2)}, u32[]{:S(2)}) %all-to-all-start) | async-done | bytes 1966112 | tf_op jit(solution)/shard_map/all_to_all | solution.py:317
  37.0 3.4 %all-to-all-start.1 = ((f32[8,5,384]{2,1,0:T(8,128)}), f32[8,5,384]{2,1,0:T(8,128)S(1)}, u32[]{:S(2)}, u32[]{:S(2)}) async-start(f32[8,5,384]{2,1,0:T(8,128)} %shard_map.102), calls=%async_computation.1 | async-start | bytes 196608 | tf_op jit(solution)/shard_map/all_to_all | solution.py:317
  40.4 5.7 %all-to-all-done.1.vectors.params = f32[8,5,384]{2,1,0:T(8,128)S(1)} async-done(((f32[8,5,384]{2,1,0:T(8,128)}), f32[8,5,384]{2,1,0:T(8,128)S(1)}, u32[]{:S(2)}, u32[]{:S(2)}) %all-to-all-start.1) | async-done | bytes 61472 | tf_op jit(solution)/shard_map/all_to_all | solution.py:317
  46.7 2.6 %shard_map.103 = (bf16[8,384,128]{2,1,0:T(8,128)(2,1)}, bf16[8,192,128]{2,1,0:T(8,128)(2,1)}) custom-call(bf16[8,960,128]{2,1,0:T(8,128)(2,1)} %copy-done, bf16[8,384,128]{2,1,0:T(8,128)(2,1)} %copy-done.18, bf16[8,384,128]{2,1,0:T(8,128)(2,1)} %collective-permute-done.1.high, f32[8,5,384]{2,1,0:T(8,128)} %copy-done.9), custom_call_target="tpu_custom_call" | custom-call | bytes 1024 | tf_op jit(solution)/shard_map/pallas_call | solution.py:326
  49.3 2.6 %shard_map.104 = bf16[8,768,128]{2,1,0:T(8,128)(2,1)} custom-call(bf16[8,384,128]{2,1,0:T(8,128)(2,1)} %copy-done.18, bf16[8,384,128]{2,1,0:T(8,128)(2,1)} %collective-permute-done.1.high, bf16[8,384,128]{2,1,0:T(8,128)(2,1)} %get-tuple-element.19._.refs_0_), custom_call_target="tpu_custom_call" | custom-call | bytes 1024 | tf_op jit(solution)/shard_map/pallas_call | solution.py:326
  52.0 3.7 %all-to-all-start.2 = ((bf16[8,768,128]{2,1,0:T(8,128)(2,1)}), bf16[8,768,128]{2,1,0:T(8,128)(2,1)S(1)}, u32[]{:S(2)}, u32[]{:S(2)}) async-start(bf16[8,768,128]{2,1,0:T(8,128)(2,1)} %shard_map.104), calls=%async_computation.2 | async-start | bytes 3145728 | tf_op jit(solution)/shard_map/all_to_all | solution.py:317
  55.7 3.0 %collective-permute-start.8 = (bf16[8,384,128]{2,1,0:T(8,128)(2,1)}, bf16[8,384,128]{2,1,0:T(8,128)(2,1)}, u32[]{:S(2)}, u32[]{:S(2)}) collective-permute-start(bf16[8,384,128]{2,1,0:T(8,128)(2,1)} %get-tuple-element.19._.refs_0_), channel_id=1, source_target_pairs={{0,1},{1,2},{2,3},{3,4},{4,5},{5,6},{6,7},{7,8},{8,9},{9,10},{10,1... | collective-permute-start | bytes 2359304 | tf_op jit(solution)/shard_map/ppermute | solution.py:320
  58.8 2.9 %collective-permute-start.9 = (bf16[8,384,128]{2,1,0:T(8,128)(2,1)}, bf16[8,384,128]{2,1,0:T(8,128)(2,1)}, u32[]{:S(2)}, u32[]{:S(2)}) collective-permute-start(bf16[8,384,128]{2,1,0:T(8,128)(2,1)} %get-tuple-element.19._.refs_0_), channel_id=1, source_target_pairs={{1,0},{2,1},{3,2},{4,3},{5,4},{6,5},{7,6},{8,7},{9,8},{10,9},{11,1... | collective-permute-start | bytes 2359304 | tf_op jit(solution)/shard_map/ppermute | solution.py:320
  64.9 1.3 copy.24
  66.9 3.8 %collective-permute-start.3 = (bf16[8,192,128]{2,1,0:T(8,128)(2,1)}, bf16[8,192,128]{2,1,0:T(8,128)(2,1)}, u32[]{:S(2)}, u32[]{:S(2)}) collective-permute-start(bf16[8,192,128]{2,1,0:T(8,128)(2,1)} %get-tuple-element.18.refs_0_), channel_id=1, source_target_pairs={{0,1},{1,2},{2,3},{3,4},{4,5},{5,6},{6,7},{7,8},{8,9},{9,10},{10,1... | collective-permute-start | bytes 1179656 | tf_op jit(solution)/shard_map/ppermute | solution.py:399
  70.7 1.3 collective-permute-start.4
  72.0 2.0 %collective-permute-start.5 = (bf16[8,192,128]{2,1,0:T(8,128)(2,1)}, bf16[8,192,128]{2,1,0:T(8,128)(2,1)}, u32[]{:S(2)}, u32[]{:S(2)}) collective-permute-start(bf16[8,192,128]{2,1,0:T(8,128)(2,1)} %get-tuple-element.18.refs_0_), channel_id=1, source_target_pairs={{1,0},{2,1},{3,2},{4,3},{5,4},{6,5},{7,6},{8,7},{9,8},{10,9},{11,1... | collective-permute-start | bytes 1179656 | tf_op jit(solution)/shard_map/ppermute | solution.py:399
  74.1 4.3 %collective-permute-done.8.refs_1_ = bf16[8,384,128]{2,1,0:T(8,128)(2,1)} collective-permute-done((bf16[8,384,128]{2,1,0:T(8,128)(2,1)}, bf16[8,384,128]{2,1,0:T(8,128)(2,1)}, u32[]{:S(2)}, u32[]{:S(2)}) %collective-permute-start.8) | collective-permute-done | bytes 786464 | tf_op jit(solution)/shard_map/ppermute | solution.py:320
  82.4 1.5 copy-done.3
  84.0 1.4 copy-done.6
  87.1 1.3 collective-permute-start.7
  89.3 37.5 %collective-permute-done.7.x_in = bf16[1,384,128]{2,1,0:T(8,128)(2,1)S(1)} collective-permute-done((bf16[1,384,128]{2,1,0:T(8,128)(2,1)S(1)}, bf16[1,384,128]{2,1,0:T(8,128)(2,1)S(1)}, u32[]{:S(2)}, u32[]{:S(2)}) %collective-permute-start.7) | collective-permute-done | bytes 98336 | tf_op jit(solution)/shard_map/ppermute | solution.py:418
  128.2 13.4 %shard_map.107 = (bf16[8,768,128]{2,1,0:T(8,128)(2,1)S(1)}, bf16[1,384,128]{2,1,0:T(8,128)(2,1)S(1)}) custom-call(s32[3]{0:T(128)S(1)} %pad_add_fusion.place, bf16[1,384,128]{2,1,0:T(8,128)(2,1)S(1)} %collective-permute-done.7.x_in, f32[8,5,384]{2,1,0:T(8,128)S(1)} %copy-done.11, bf16[384,128]{1,0:T(8,128)(2,1)S(1)} %bitcast.24, ...), custom_call_target="tpu_custom_call", output_to_operand_aliasing={{0}: (6, {})} | custom-call | bytes 1024 | tf_op jit(solution)/shard_map/pallas_call | solution.py:248
  144.0 11.4 %shard_map.109 = (bf16[8,768,128]{2,1,0:T(8,128)(2,1)S(1)}, bf16[1,384,128]{2,1,0:T(8,128)(2,1)S(1)}) custom-call(s32[3]{0:T(128)S(1)} %pad_add_fusion.place, bf16[1,384,128]{2,1,0:T(8,128)(2,1)S(1)} %collective-permute-done.10.refs_7_.x_in, f32[8,5,384]{2,1,0:T(8,128)S(1)} %copy-done.11, ...), custom_call_target="tpu_custom_call", output_to_operand_aliasing={{0}: (7, {})} | custom-call | bytes 1024 | tf_op jit(solution)/shard_map/pallas_call | solution.py:248
  157.3 5.0 %all-to-all-start.4 = ((bf16[8,768,128]{2,1,0:T(8,128)(2,1)}), bf16[8,768,128]{2,1,0:T(8,128)(2,1)S(1)}, u32[]{:S(2)}, u32[]{:S(2)}) async-start(bf16[8,768,128]{2,1,0:T(8,128)(2,1)} %shard_map.111), calls=%async_computation.4 | async-start | bytes 3145728 | tf_op jit(solution)/shard_map/all_to_all | solution.py:317
  162.2 10.9 %shard_map.110 = (bf16[8,384,128]{2,1,0:T(8,128)(2,1)}, bf16[1,384,128]{2,1,0:T(8,128)(2,1)}) custom-call(s32[3]{0:T(128)S(1)} %pad_add_fusion.place, bf16[1,384,128]{2,1,0:T(8,128)(2,1)S(1)} %copy-done.14, f32[8,5,384]{2,1,0:T(8,128)S(1)} %copy-done.11, bf16[384,128]{1,0:T(8,128)(2,1)S(1)} %bitcast.27, ...), custom_call_target="tpu_custom_call", output_to_operand_aliasing={{0}: (10, {})} | custom-call | bytes 1024 | tf_op jit(solution)/shard_map/pallas_call | solution.py:248
  173.2 10.6 %all-to-all-done.4.refs_0_ = bf16[8,768,128]{2,1,0:T(8,128)(2,1)S(1)} async-done(((bf16[8,768,128]{2,1,0:T(8,128)(2,1)}), bf16[8,768,128]{2,1,0:T(8,128)(2,1)S(1)}, u32[]{:S(2)}, u32[]{:S(2)}) %all-to-all-start.4) | async-done | bytes 1572896 | tf_op jit(solution)/shard_map/all_to_all | solution.py:317
  183.8 3.5 %all-to-all-start.3 = ((bf16[8,384,128]{2,1,0:T(8,128)(2,1)}), bf16[8,384,128]{2,1,0:T(8,128)(2,1)S(1)}, u32[]{:S(2)}, u32[]{:S(2)}) async-start(bf16[8,384,128]{2,1,0:T(8,128)(2,1)} %get-tuple-element.29), calls=%async_computation.3 | async-start | bytes 1572864 | tf_op jit(solution)/shard_map/all_to_all | solution.py:317
  187.4 2.7 %shard_map.112.refs_1_ = bf16[1,384,2560]{2,1,0:T(8,128)(2,1)} custom-call(bf16[8,768,128]{2,1,0:T(8,128)(2,1)} %copy-done.15), custom_call_target="tpu_custom_call" | custom-call | bytes 1024 | tf_op jit(solution)/shard_map/pallas_call | solution.py:326
  190.1 10.3 %all-to-all-done.3.refs_0_ = bf16[8,384,128]{2,1,0:T(8,128)(2,1)S(1)} async-done(((bf16[8,384,128]{2,1,0:T(8,128)(2,1)}), bf16[8,384,128]{2,1,0:T(8,128)(2,1)S(1)}, u32[]{:S(2)}, u32[]{:S(2)}) %all-to-all-start.3) | async-done | bytes 786464 | tf_op jit(solution)/shard_map/all_to_all | solution.py:317
  201.4 2.1 %shard_map.113 = bf16[1,384,2560]{2,1,0:T(8,128)(2,1)} custom-call(bf16[8,384,128]{2,1,0:T(8,128)(2,1)} %copy-done.16, bf16[1,384,2560]{2,1,0:T(8,128)(2,1)} %shard_map.112.refs_1_), custom_call_target="tpu_custom_call", output_to_operand_aliasing={{}: (1, {})} | custom-call | bytes 1024 | tf_op jit(solution)/shard_map/pallas_call | solution.py:326
  (88 shorter events, 21.0 us)
Async XLA Ops:
  5.3 4.6 %copy-start.17 = (bf16[8,384,128]{2,1,0:T(8,128)(2,1)S(1)}, bf16[8,384,128]{2,1,0:T(8,128)(2,1)}, u32[]{:S(2)}) copy-start(bf16[8,384,128]{2,1,0:T(8,128)(2,1)} %shard_map.100._) | copy-start | bytes 2359300
  5.3 10.5 %copy-start.19 = (f32[1,2560]{1,0:T(1,128)S(1)}, f32[1,2560]{1,0:T(1,128)}, u32[]{:S(2)}) copy-start(f32[1,2560]{1,0:T(1,128)} %param.12) | copy-start | bytes 30724
  5.3 30.4 %all-to-all-start = ((bf16[8,960,128]{2,1,0:T(8,128)(2,1)}), bf16[8,960,128]{2,1,0:T(8,128)(2,1)S(1)}, u32[]{:S(2)}, u32[]{:S(2)}) async-start(bf16[8,960,128]{2,1,0:T(8,128)(2,1)} %shard_map.101), calls=%async_computation | async-start | bytes 3932160 | tf_op jit(solution)/shard_map/all_to_all | solution.py:317
  9.9 30.4 %collective-permute-start = (bf16[8,384,128]{2,1,0:T(8,128)(2,1)S(1)}, bf16[8,384,128]{2,1,0:T(8,128)(2,1)S(1)}, u32[]{:S(2)}, u32[]{:S(2)}) collective-permute-start(bf16[8,384,128]{2,1,0:T(8,128)(2,1)S(1)} %copy-done.17), channel_id=1, source_target_pairs={{0,1},{1,2},{2,3},{3,4},{4,5},{5,6},{6,7},{7,8},{8,9},{9,10},{10,1... | collective-permute-start | bytes 2359304 | tf_op jit(solution)/shard_map/ppermute | solution.py:320
  12.9 27.5 %collective-permute-start.1 = (bf16[8,384,128]{2,1,0:T(8,128)(2,1)S(1)}, bf16[8,384,128]{2,1,0:T(8,128)(2,1)}, u32[]{:S(2)}, u32[]{:S(2)}) collective-permute-start(bf16[8,384,128]{2,1,0:T(8,128)(2,1)S(1)} %copy-done.17), channel_id=1, source_target_pairs={{1,0},{2,1},{3,2},{4,3},{5,4},{6,5},{7,6},{8,7},{9,8},{10,9},{11,1... | collective-permute-start | bytes 2359304 | tf_op jit(solution)/shard_map/ppermute | solution.py:320
  37.0 9.1 %all-to-all-start.1 = ((f32[8,5,384]{2,1,0:T(8,128)}), f32[8,5,384]{2,1,0:T(8,128)S(1)}, u32[]{:S(2)}, u32[]{:S(2)}) async-start(f32[8,5,384]{2,1,0:T(8,128)} %shard_map.102), calls=%async_computation.1 | async-start | bytes 196608 | tf_op jit(solution)/shard_map/all_to_all | solution.py:317
  40.4 5.7 %copy-start.18 = (bf16[8,384,128]{2,1,0:T(8,128)(2,1)}, bf16[8,384,128]{2,1,0:T(8,128)(2,1)S(1)}, u32[]{:S(2)}) copy-start(bf16[8,384,128]{2,1,0:T(8,128)(2,1)S(1)} %collective-permute-done.low) | copy-start | bytes 2359300
  52.0 6.7 %copy-start.21 = (s32[6]{0:T(128)S(1)}, s32[6]{0:T(128)}, u32[]{:S(2)}) copy-start(s32[6]{0:T(128)} %param.18) | copy-start | bytes 76
  52.0 9.7 %copy-start.22 = (s32[1,6]{1,0:T(1,128)S(1)}, s32[1,6]{1,0:T(1,128)}, u32[]{:S(2)}) copy-start(s32[1,6]{1,0:T(1,128)} %param.19) | copy-start | bytes 76
  52.0 11.1 %copy-start.20 = (s32[6,18]{1,0:T(8,128)S(1)}, s32[6,18]{1,0:T(8,128)}, u32[]{:S(2)}) copy-start(s32[6,18]{1,0:T(8,128)} %param.17) | copy-start | bytes 1300
  52.0 30.4 %copy-start.1 = (bf16[8,960,128]{2,1,0:T(8,128)(2,1)S(1)}, bf16[8,960,128]{2,1,0:T(8,128)(2,1)}, u32[]{:S(2)}) copy-start(bf16[8,960,128]{2,1,0:T(8,128)(2,1)} %copy-done) | copy-start | bytes 5898244
  52.0 29.2 %all-to-all-start.2 = ((bf16[8,768,128]{2,1,0:T(8,128)(2,1)}), bf16[8,768,128]{2,1,0:T(8,128)(2,1)S(1)}, u32[]{:S(2)}, u32[]{:S(2)}) async-start(bf16[8,768,128]{2,1,0:T(8,128)(2,1)} %shard_map.104), calls=%async_computation.2 | async-start | bytes 3145728 | tf_op jit(solution)/shard_map/all_to_all | solution.py:317
  55.7 22.6 %collective-permute-start.8 = (bf16[8,384,128]{2,1,0:T(8,128)(2,1)}, bf16[8,384,128]{2,1,0:T(8,128)(2,1)}, u32[]{:S(2)}, u32[]{:S(2)}) collective-permute-start(bf16[8,384,128]{2,1,0:T(8,128)(2,1)} %get-tuple-element.19._.refs_0_), channel_id=1, source_target_pairs={{0,1},{1,2},{2,3},{3,4},{4,5},{5,6},{6,7},{7,8},{8,9},{9,10},{10,1... | collective-permute-start | bytes 2359304 | tf_op jit(solution)/shard_map/ppermute | solution.py:320
  58.8 28.4 %collective-permute-start.9 = (bf16[8,384,128]{2,1,0:T(8,128)(2,1)}, bf16[8,384,128]{2,1,0:T(8,128)(2,1)}, u32[]{:S(2)}, u32[]{:S(2)}) collective-permute-start(bf16[8,384,128]{2,1,0:T(8,128)(2,1)} %get-tuple-element.19._.refs_0_), channel_id=1, source_target_pairs={{1,0},{2,1},{3,2},{4,3},{5,4},{6,5},{7,6},{8,7},{9,8},{10,9},{11,1... | collective-permute-start | bytes 2359304 | tf_op jit(solution)/shard_map/ppermute | solution.py:320
  61.8 10.2 %collective-permute-start.2 = (bf16[8,192,128]{2,1,0:T(8,128)(2,1)}, bf16[8,192,128]{2,1,0:T(8,128)(2,1)}, u32[]{:S(2)}, u32[]{:S(2)}) collective-permute-start(bf16[8,192,128]{2,1,0:T(8,128)(2,1)} %get-tuple-element.18.refs_0_), channel_id=1, source_target_pairs={{16,0},{17,1},{18,2},{19,3},{20,4},{21,5},{22,6},{23,7},{24,8},{25... | collective-permute-start | bytes 1179656 | tf_op jit(solution)/shard_map/ppermute | solution.py:399
  66.9 74.7 %collective-permute-start.3 = (bf16[8,192,128]{2,1,0:T(8,128)(2,1)}, bf16[8,192,128]{2,1,0:T(8,128)(2,1)}, u32[]{:S(2)}, u32[]{:S(2)}) collective-permute-start(bf16[8,192,128]{2,1,0:T(8,128)(2,1)} %get-tuple-element.18.refs_0_), channel_id=1, source_target_pairs={{0,1},{1,2},{2,3},{3,4},{4,5},{5,6},{6,7},{7,8},{8,9},{9,10},{10,1... | collective-permute-start | bytes 1179656 | tf_op jit(solution)/shard_map/ppermute | solution.py:399
  70.7 70.9 %collective-permute-start.4 = (bf16[8,192,128]{2,1,0:T(8,128)(2,1)}, bf16[8,192,128]{2,1,0:T(8,128)(2,1)}, u32[]{:S(2)}, u32[]{:S(2)}) collective-permute-start(bf16[8,192,128]{2,1,0:T(8,128)(2,1)} %get-tuple-element.18.refs_0_), channel_id=1, source_target_pairs={{16,1},{17,2},{18,3},{19,4},{20,5},{21,6},{22,7},{23,8},{24,9},{25... | collective-permute-start | bytes 1179656 | tf_op jit(solution)/shard_map/ppermute | solution.py:399
  72.0 69.6 %collective-permute-start.5 = (bf16[8,192,128]{2,1,0:T(8,128)(2,1)}, bf16[8,192,128]{2,1,0:T(8,128)(2,1)}, u32[]{:S(2)}, u32[]{:S(2)}) collective-permute-start(bf16[8,192,128]{2,1,0:T(8,128)(2,1)} %get-tuple-element.18.refs_0_), channel_id=1, source_target_pairs={{1,0},{2,1},{3,2},{4,3},{5,4},{6,5},{7,6},{8,7},{9,8},{10,9},{11,1... | collective-permute-start | bytes 1179656 | tf_op jit(solution)/shard_map/ppermute | solution.py:399
  78.3 63.3 %collective-permute-start.6 = (bf16[8,192,128]{2,1,0:T(8,128)(2,1)}, bf16[8,192,128]{2,1,0:T(8,128)(2,1)}, u32[]{:S(2)}, u32[]{:S(2)}) collective-permute-start(bf16[8,192,128]{2,1,0:T(8,128)(2,1)} %get-tuple-element.18.refs_0_), channel_id=1, source_target_pairs={{17,0},{18,1},{19,2},{20,3},{21,4},{22,5},{23,6},{24,7},{25,8},{26... | collective-permute-start | bytes 1179656 | tf_op jit(solution)/shard_map/ppermute | solution.py:399
  82.4 1.5 copy-start.3
  86.3 2.2 %copy-start.8 = (bf16[8,384,128]{2,1,0:T(8,128)(2,1)S(1)}, bf16[8,384,128]{2,1,0:T(8,128)(2,1)}, u32[]{:S(2)}) copy-start(bf16[8,384,128]{2,1,0:T(8,128)(2,1)} %get-tuple-element.19._.refs_0_) | copy-start | bytes 2359300
  86.3 2.2 %copy-start.11 = (f32[8,5,384]{2,1,0:T(8,128)S(1)}, f32[8,5,384]{2,1,0:T(8,128)}, u32[]{:S(2)}) copy-start(f32[8,5,384]{2,1,0:T(8,128)} %copy-done.9) | copy-start | bytes 184324
  87.1 39.7 %collective-permute-start.7 = (bf16[1,384,128]{2,1,0:T(8,128)(2,1)S(1)}, bf16[1,384,128]{2,1,0:T(8,128)(2,1)S(1)}, u32[]{:S(2)}, u32[]{:S(2)}) collective-permute-start(bf16[1,384,128]{2,1,0:T(8,128)(2,1)S(1)} %get-tuple-element.20), channel_id=1, source_target_pairs={{0,128},{16,144},{32,160},{48,176},{64,192},{80,208},{96,224},{112... | collective-permute-start | bytes 294920 | tf_op jit(solution)/shard_map/ppermute | solution.py:418
  88.5 39.7 %copy-start.7 = (bf16[8,768,128]{2,1,0:T(8,128)(2,1)S(1)}, bf16[8,768,128]{2,1,0:T(8,128)(2,1)}, u32[]{:S(2)}) copy-start(bf16[8,768,128]{2,1,0:T(8,128)(2,1)} %copy-done.5) | copy-start | bytes 4718596
  126.8 14.8 %collective-permute-start.10 = (bf16[1,384,128]{2,1,0:T(8,128)(2,1)S(1)}, bf16[1,384,128]{2,1,0:T(8,128)(2,1)S(1)}, u32[]{:S(2)}, u32[]{:S(2)}) collective-permute-start(bf16[1,384,128]{2,1,0:T(8,128)(2,1)S(1)} %get-tuple-element.24), channel_id=1, source_target_pairs={{0,128},{16,144},{32,160},{48,176},{64,192},{80,208},{96,224},{112... | collective-permute-start | bytes 294920 | tf_op jit(solution)/shard_map/ppermute | solution.py:418
  128.1 13.5 %copy-start.4 = (bf16[384,2560]{1,0:T(8,128)(2,1)S(1)}, bf16[384,2560]{1,0:T(8,128)(2,1)}, u32[]{:S(2)}) copy-start(bf16[384,2560]{1,0:T(8,128)(2,1)} %x_in.5) | copy-start | bytes 5898244
  128.2 13.5 %copy-start.12 = (bf16[8,192,128]{2,1,0:T(8,128)(2,1)S(1)}, bf16[8,192,128]{2,1,0:T(8,128)(2,1)}, u32[]{:S(2)}) copy-start(bf16[8,192,128]{2,1,0:T(8,128)(2,1)} %get-tuple-element.18.refs_0_) | copy-start | bytes 1179652
  142.7 13.9 %collective-permute-start.11 = (bf16[1,384,128]{2,1,0:T(8,128)(2,1)S(1)}, bf16[1,384,128]{2,1,0:T(8,128)(2,1)S(1)}, u32[]{:S(2)}, u32[]{:S(2)}) collective-permute-start(bf16[1,384,128]{2,1,0:T(8,128)(2,1)S(1)} %get-tuple-element.25.refs_4_), channel_id=1, source_target_pairs={{0,128},{32,160},{64,192},{96,224},{1,129},{33,161},{65,193},{97,2... | collective-permute-start | bytes 294920 | tf_op jit(solution)/shard_map/ppermute | solution.py:418
  157.3 5.0 %copy-start.14 = (bf16[1,384,128]{2,1,0:T(8,128)(2,1)S(1)}, bf16[1,384,128]{2,1,0:T(8,128)(2,1)}, u32[]{:S(2)}) copy-start(bf16[1,384,128]{2,1,0:T(8,128)(2,1)} %copy-done.13) | copy-start | bytes 294916
  157.3 26.6 %all-to-all-start.4 = ((bf16[8,768,128]{2,1,0:T(8,128)(2,1)}), bf16[8,768,128]{2,1,0:T(8,128)(2,1)S(1)}, u32[]{:S(2)}, u32[]{:S(2)}) async-start(bf16[8,768,128]{2,1,0:T(8,128)(2,1)} %shard_map.111), calls=%async_computation.4 | async-start | bytes 3145728 | tf_op jit(solution)/shard_map/all_to_all | solution.py:317
  183.8 3.6 %copy-start.15 = (bf16[8,768,128]{2,1,0:T(8,128)(2,1)}, bf16[8,768,128]{2,1,0:T(8,128)(2,1)S(1)}, u32[]{:S(2)}) copy-start(bf16[8,768,128]{2,1,0:T(8,128)(2,1)S(1)} %all-to-all-done.4.refs_0_) | copy-start | bytes 4718596
  183.8 16.6 %all-to-all-start.3 = ((bf16[8,384,128]{2,1,0:T(8,128)(2,1)}), bf16[8,384,128]{2,1,0:T(8,128)(2,1)S(1)}, u32[]{:S(2)}, u32[]{:S(2)}) async-start(bf16[8,384,128]{2,1,0:T(8,128)(2,1)} %get-tuple-element.29), calls=%async_computation.3 | async-start | bytes 1572864 | tf_op jit(solution)/shard_map/all_to_all | solution.py:317
  (8 other events, 8.1 us)

commit v3 on v2

--- a/solution.py
+++ b/solution.py
@@ -30,6 +30,8 @@
 HBM = pl.BlockSpec(memory_space=pltpu.HBM)
 
 SMALL = pl.CostEstimate(flops=0, bytes_accessed=1024, transcendentals=0)
+
+LARGE = pl.CostEstimate(flops=2**37, bytes_accessed=2**26, transcendentals=2**20)
 
 QUERY_ROWS = ((0, 256), (0, 384), (128, 384))
 
@@ -241,7 +243,7 @@
     pl.when(works)(lambda: work(n_heads))
 
 
-def attention(place, x_in, params, bias, kv, heads, stage, previous, before, first_row, rows):
+def attention(place, x_in, params, bias, kv, heads, stage, previous, before, first_row, rows, cost):
     n_heads = len(heads)
     skipped = list(previous) + list(before)
     n_copies = max(len(head[1]) for head in heads)
@@ -270,7 +272,7 @@
         ],
         input_output_aliases={4 + len(kv): 0} if previous else {},
         compiler_params=pltpu.CompilerParams(vmem_limit_bytes=32 * 1024 * 1024),
-        cost_estimate=SMALL,
+        cost_estimate=cost,
     )(place, x_in, params, bias, *kv, *skipped)
 
 
@@ -405,14 +407,14 @@
     head_b = (1, tuple((i, 0, ROWS, i, 0) for i in range(3)))
     head_c = (2, tuple((i, 0, HALF, i // 2, (i % 2) * HALF) for i in range(6)))
     kinds = {
-        "a": ([own, sides_a], (head_a,), 0, 2 * ROWS),
-        "b": ([own_b, *sides_b], (head_b,), ROWS, 2 * ROWS),
-        "c": ([own_c, own_c_other, *sides_c], (head_c,), 0, ROWS),
+        "a": ([own, sides_a], (head_a,), 0, ROWS),
+        "b": ([own_b, *sides_b], (head_b,), 0, 2 * ROWS),
+        "c": ([own_c, own_c_other, *sides_c], (head_c,), ROWS, 2 * ROWS),
     }
 
-    def run(name, stage, x_in, previous, before):
+    def run(name, stage, x_in, previous, before, cost=SMALL):
         kv, heads, *rows = kinds[name]
-        return attention(place, x_in, params, bias, kv, heads, stage, previous, before, *rows)
+        return attention(place, x_in, params, bias, kv, heads, stage, previous, before, *rows, cost)
 
     def hop(last, step):
         return lax.ppermute(last, "section", [(i, i + GROUP) for i in range(0, GROUP, step)])
@@ -430,26 +432,18 @@
             input_output_aliases={len(pieces): 0} if before else {},
         )
 
-    layers, last_a = run("a", 0, tokens_in, [], [])
+    layers_a, last_a = run("a", 0, tokens_in, [], [])
     next_a = hop(last_a, 1)
-    layers, last_b = run("b", 0, tokens_in, [layers], [])
+    layers, last_b = run("b", 0, tokens_in, [], [last_a])
     next_b = hop(last_b, 1)
-    layers, done_a = run("a", 1, next_a, [layers], [])
-    layers_c, last_c = run("c", 0, tokens_in, [], [done_a, next_b])
+    layers_a, done_a = run("a", 1, next_a, [layers_a], [last_b])
+    arrived_a = exchange(layers_a)
+    layers, last_c = run("c", 0, tokens_in, [layers], [done_a, next_b])
     next_c = hop(last_c, 2)
-    layers, done_b = run("b", 1, next_b, [layers], [last_c])
-    layers = call(
-        pass_kernel,
-        shape(LAYERS, 2 * ROWS, HD),
-        [HBM, ANY],
-        HBM,
-        layers,
-        next_c,
-        input_output_aliases={0: 0},
-    )
-    layers_c, _ = run("c", 1, next_c, [layers_c], [done_b])
-    out = home([exchange(layers)], ((0, 0, 0, 1), (0, ROWS, GROUP, 1)), None)
-    out = home([exchange(layers_c)], ((0, 0, 2 * GROUP, 2),), out)
+    layers, done_b = run("b", 1, next_b, [layers], [], LARGE)
+    layers, _ = run("c", 1, next_c, [layers], [arrived_a])
+    out = home([arrived_a], ((0, 0, 0, 1),), None)
+    out = home([exchange(layers)], ((0, 0, GROUP, 1), (0, ROWS, 2 * GROUP, 2)), out)
     return out
 
 

time: 206 us -> 201 us (0.976)
  local copies, waits for them, and re-layouts: 17.1 us -> 13 us
    unnamed x46, local copies, waits for them, and re-layouts: 9.66 us -> 5.62 us
    pallas_call x8 -> x7, Pallas kernels: 15.4 us -> 15.5 us  [call(): pl.pallas_call(kernel, out_shape=out_shape, in_specs=in_specs, out_specs=...]
  transfers between devices with their start and end apart: 17 -> 17, of which waited for: 6 -> 6; matrix products, arithmetic and copies ran while one was open for 4% -> 5% of each run, Pallas kernels for 20% -> 14%
where the time goes in v3:
time: 201 us; the launch traced here: 198 us
  waiting for transfers between devices  83.7 us (42%)
  Pallas kernels  53 us (26%)
  starting transfers between devices  45.5 us (23%)
  local copies, waits for them, and re-layouts  13 us (6%)
    all_to_all x5, waiting for transfers between devices, exchange(): lax.all_to_all(array, 'section', 0, 0, axis_index_groups=groups, tiled=True)  43.4 us
    pallas_call x6, Pallas kernels, attention(): pl.pallas_call(functools.partial(attention_kernel, (heads, stage, len(kv)...  37.6 us
    ppermute x3, waiting for transfers between devices, hop(): lax.ppermute(last, 'section', [(i, i + GROUP) for i in range(0, GROUP, st...  36 us
    all_to_all x5, starting transfers between devices, exchange(): lax.all_to_all(array, 'section', 0, 0, axis_index_groups=groups, tiled=True)  20.1 us
    pallas_call x7, Pallas kernels, call(): pl.pallas_call(kernel, out_shape=out_shape, in_specs=in_specs, out_specs=...  15.5 us
    ppermute x5, starting transfers between devices, to_first_core(): return lax.ppermute(array, ('section', 'seq'), pairs)  9.69 us
    ppermute x2, starting transfers between devices, both_ways(): lax.ppermute(array, 'seq', forward)  5.88 us
    ppermute x2, starting transfers between devices, both_ways(): lax.ppermute(array, 'seq', backward)  5.82 us
  transfers between devices with their start and end apart: 17, of which 6 were waited for; matrix products, arithmetic and copies ran while one was open for 5% of the time, Pallas kernels for 14%

profile of v3, /device:TPU:198, one launch (start us, length us, event | category | flops | bytes accessed | tf_op | source)
XLA Modules:
  0.0 197.6 jit_solution(2337697164204563965)
XLA Ops:
  0.0 2.2 %shard_map.100._ = bf16[8,384,128]{2,1,0:T(8,128)(2,1)} custom-call(bf16[1,384,2560]{2,1,0:T(8,128)(2,1)} %values.3), custom_call_target="tpu_custom_call" | custom-call | bytes 1024 | tf_op jit(solution)/shard_map/pallas_call | solution.py:328
  2.2 3.2 %shard_map.101 = bf16[8,960,128]{2,1,0:T(8,128)(2,1)} custom-call(bf16[1,384,2560]{2,1,0:T(8,128)(2,1)} %values.3, bf16[8,384,128]{2,1,0:T(8,128)(2,1)} %shard_map.100._), custom_call_target="tpu_custom_call" | custom-call | bytes 1024 | tf_op jit(solution)/shard_map/pallas_call | solution.py:328
  5.3 4.6 %all-to-all-start = ((bf16[8,960,128]{2,1,0:T(8,128)(2,1)}), bf16[8,960,128]{2,1,0:T(8,128)(2,1)S(1)}, u32[]{:S(2)}, u32[]{:S(2)}) async-start(bf16[8,960,128]{2,1,0:T(8,128)(2,1)} %shard_map.101), calls=%async_computation | async-start | bytes 3932160 | tf_op jit(solution)/shard_map/all_to_all | solution.py:319
  9.9 2.9 %collective-permute-start = (bf16[8,384,128]{2,1,0:T(8,128)(2,1)S(1)}, bf16[8,384,128]{2,1,0:T(8,128)(2,1)S(1)}, u32[]{:S(2)}, u32[]{:S(2)}) collective-permute-start(bf16[8,384,128]{2,1,0:T(8,128)(2,1)S(1)} %copy-done.17), channel_id=1, source_target_pairs={{0,1},{1,2},{2,3},{3,4},{4,5},{5,6},{6,7},{7,8},{8,9},{9,10},{10,1... | collective-permute-start | bytes 2359304 | tf_op jit(solution)/shard_map/ppermute | solution.py:322
  12.9 2.9 %collective-permute-start.1 = (bf16[8,384,128]{2,1,0:T(8,128)(2,1)S(1)}, bf16[8,384,128]{2,1,0:T(8,128)(2,1)}, u32[]{:S(2)}, u32[]{:S(2)}) collective-permute-start(bf16[8,384,128]{2,1,0:T(8,128)(2,1)S(1)} %copy-done.17), channel_id=1, source_target_pairs={{1,0},{2,1},{3,2},{4,3},{5,4},{6,5},{7,6},{8,7},{9,8},{10,9},{11,1... | collective-permute-start | bytes 2359304 | tf_op jit(solution)/shard_map/ppermute | solution.py:322
  15.8 1.5 concatenate.7
  19.4 16.3 %all-to-all-done.refs_1_.owned.refs_0_ = bf16[8,960,128]{2,1,0:T(8,128)(2,1)S(1)} async-done(((bf16[8,960,128]{2,1,0:T(8,128)(2,1)}), bf16[8,960,128]{2,1,0:T(8,128)(2,1)S(1)}, u32[]{:S(2)}, u32[]{:S(2)}) %all-to-all-start) | async-done | bytes 1966112 | tf_op jit(solution)/shard_map/all_to_all | solution.py:319
  37.0 3.4 %all-to-all-start.1 = ((f32[8,5,384]{2,1,0:T(8,128)}), f32[8,5,384]{2,1,0:T(8,128)S(1)}, u32[]{:S(2)}, u32[]{:S(2)}) async-start(f32[8,5,384]{2,1,0:T(8,128)} %shard_map.102), calls=%async_computation.1 | async-start | bytes 196608 | tf_op jit(solution)/shard_map/all_to_all | solution.py:319
  40.4 5.7 %all-to-all-done.1.vectors.params = f32[8,5,384]{2,1,0:T(8,128)S(1)} async-done(((f32[8,5,384]{2,1,0:T(8,128)}), f32[8,5,384]{2,1,0:T(8,128)S(1)}, u32[]{:S(2)}, u32[]{:S(2)}) %all-to-all-start.1) | async-done | bytes 61472 | tf_op jit(solution)/shard_map/all_to_all | solution.py:319
  46.7 2.7 %shard_map.103 = (bf16[8,384,128]{2,1,0:T(8,128)(2,1)}, bf16[8,192,128]{2,1,0:T(8,128)(2,1)}) custom-call(bf16[8,960,128]{2,1,0:T(8,128)(2,1)} %copy-done, bf16[8,384,128]{2,1,0:T(8,128)(2,1)} %copy-done.18, bf16[8,384,128]{2,1,0:T(8,128)(2,1)} %collective-permute-done.1.high, f32[8,5,384]{2,1,0:T(8,128)} %copy-done.5), custom_call_target="tpu_custom_call" | custom-call | bytes 1024 | tf_op jit(solution)/shard_map/pallas_call | solution.py:328
  49.4 2.6 %shard_map.104 = bf16[8,768,128]{2,1,0:T(8,128)(2,1)} custom-call(bf16[8,384,128]{2,1,0:T(8,128)(2,1)} %copy-done.18, bf16[8,384,128]{2,1,0:T(8,128)(2,1)} %collective-permute-done.1.high, bf16[8,384,128]{2,1,0:T(8,128)(2,1)} %get-tuple-element.18._.refs_0_), custom_call_target="tpu_custom_call" | custom-call | bytes 1024 | tf_op jit(solution)/shard_map/pallas_call | solution.py:328
  52.1 3.7 %all-to-all-start.2 = ((bf16[8,768,128]{2,1,0:T(8,128)(2,1)}), bf16[8,768,128]{2,1,0:T(8,128)(2,1)S(1)}, u32[]{:S(2)}, u32[]{:S(2)}) async-start(bf16[8,768,128]{2,1,0:T(8,128)(2,1)} %shard_map.104), calls=%async_computation.2 | async-start | bytes 3145728 | tf_op jit(solution)/shard_map/all_to_all | solution.py:319
  55.8 3.0 %collective-permute-start.7 = (bf16[8,384,128]{2,1,0:T(8,128)(2,1)}, bf16[8,384,128]{2,1,0:T(8,128)(2,1)}, u32[]{:S(2)}, u32[]{:S(2)}) collective-permute-start(bf16[8,384,128]{2,1,0:T(8,128)(2,1)} %get-tuple-element.18._.refs_0_), channel_id=1, source_target_pairs={{0,1},{1,2},{2,3},{3,4},{4,5},{5,6},{6,7},{7,8},{8,9},{9,10},{10,1... | collective-permute-start | bytes 2359304 | tf_op jit(solution)/shard_map/ppermute | solution.py:322
  58.8 2.9 %collective-permute-start.8 = (bf16[8,384,128]{2,1,0:T(8,128)(2,1)}, bf16[8,384,128]{2,1,0:T(8,128)(2,1)}, u32[]{:S(2)}, u32[]{:S(2)}) collective-permute-start(bf16[8,384,128]{2,1,0:T(8,128)(2,1)} %get-tuple-element.18._.refs_0_), channel_id=1, source_target_pairs={{1,0},{2,1},{3,2},{4,3},{5,4},{6,5},{7,6},{8,7},{9,8},{10,9},{11,1... | collective-permute-start | bytes 2359304 | tf_op jit(solution)/shard_map/ppermute | solution.py:322
  65.0 1.3 copy.23
  66.9 3.8 %collective-permute-start.3 = (bf16[8,192,128]{2,1,0:T(8,128)(2,1)}, bf16[8,192,128]{2,1,0:T(8,128)(2,1)}, u32[]{:S(2)}, u32[]{:S(2)}) collective-permute-start(bf16[8,192,128]{2,1,0:T(8,128)(2,1)} %get-tuple-element.17.refs_0_), channel_id=1, source_target_pairs={{0,1},{1,2},{2,3},{3,4},{4,5},{5,6},{6,7},{7,8},{8,9},{9,10},{10,1... | collective-permute-start | bytes 1179656 | tf_op jit(solution)/shard_map/ppermute | solution.py:401
  70.7 1.3 collective-permute-start.4
  72.0 2.0 %collective-permute-start.5 = (bf16[8,192,128]{2,1,0:T(8,128)(2,1)}, bf16[8,192,128]{2,1,0:T(8,128)(2,1)}, u32[]{:S(2)}, u32[]{:S(2)}) collective-permute-start(bf16[8,192,128]{2,1,0:T(8,128)(2,1)} %get-tuple-element.17.refs_0_), channel_id=1, source_target_pairs={{1,0},{2,1},{3,2},{4,3},{5,4},{6,5},{7,6},{8,7},{9,8},{10,9},{11,1... | collective-permute-start | bytes 1179656 | tf_op jit(solution)/shard_map/ppermute | solution.py:401
  74.1 4.3 %collective-permute-done.7.refs_1_ = bf16[8,384,128]{2,1,0:T(8,128)(2,1)} collective-permute-done((bf16[8,384,128]{2,1,0:T(8,128)(2,1)}, bf16[8,384,128]{2,1,0:T(8,128)(2,1)}, u32[]{:S(2)}, u32[]{:S(2)}) %collective-permute-start.7) | collective-permute-done | bytes 786464 | tf_op jit(solution)/shard_map/ppermute | solution.py:322
  81.3 1.6 copy-done.2
  84.7 1.3 collective-permute-start.9
  86.8 36.0 %collective-permute-done.9.x_in = bf16[1,384,128]{2,1,0:T(8,128)(2,1)S(1)} collective-permute-done((bf16[1,384,128]{2,1,0:T(8,128)(2,1)S(1)}, bf16[1,384,128]{2,1,0:T(8,128)(2,1)S(1)}, u32[]{:S(2)}, u32[]{:S(2)}) %collective-permute-start.9) | collective-permute-done | bytes 98336 | tf_op jit(solution)/shard_map/ppermute | solution.py:420
  124.1 12.9 %shard_map.107 = (bf16[8,384,128]{2,1,0:T(8,128)(2,1)}, bf16[1,384,128]{2,1,0:T(8,128)(2,1)S(1)}) custom-call(s32[3]{0:T(128)S(1)} %pad_add_fusion.place, bf16[1,384,128]{2,1,0:T(8,128)(2,1)S(1)} %collective-permute-done.9.x_in, f32[8,5,384]{2,1,0:T(8,128)S(1)} %copy-done.6, bf16[384,128]{1,0:T(8,128)(2,1)S(1)} %bitcast.24, ...), custom_call_target="tpu_custom_call", output_to_operand_aliasing={{0}: (6, {})} | custom-call | bytes 1024 | tf_op jit(solution)/shard_map/pallas_call | solution.py:250
  138.3 1.4 collective-permute-start.11
  139.7 4.9 %all-to-all-start.3 = ((bf16[8,384,128]{2,1,0:T(8,128)(2,1)}), bf16[8,384,128]{2,1,0:T(8,128)(2,1)S(1)}, u32[]{:S(2)}, u32[]{:S(2)}) async-start(bf16[8,384,128]{2,1,0:T(8,128)(2,1)} %get-tuple-element.27), calls=%async_computation.3 | async-start | bytes 1572864 | tf_op jit(solution)/shard_map/all_to_all | solution.py:319
  144.6 11.0 %shard_map.109 = (bf16[8,768,128]{2,1,0:T(8,128)(2,1)}, bf16[1,384,128]{2,1,0:T(8,128)(2,1)}) custom-call(s32[3]{0:T(128)S(1)} %pad_add_fusion.place, bf16[1,384,128]{2,1,0:T(8,128)(2,1)S(1)} %copy-done.15, f32[8,5,384]{2,1,0:T(8,128)S(1)} %copy-done.7, bf16[384,128]{1,0:T(8,128)(2,1)S(1)} %bitcast.26, ...), custom_call_target="tpu_custom_call", output_to_operand_aliasing={{0}: (7, {})} | custom-call | flops 137438953472 | bytes 67108864 | tf_op jit(solution)/shard_map/pallas_call | solution.py:250
  155.6 2.1 %all-to-all-done.3.refs_7_.refs_0_ = bf16[8,384,128]{2,1,0:T(8,128)(2,1)S(1)} async-done(((bf16[8,384,128]{2,1,0:T(8,128)(2,1)}), bf16[8,384,128]{2,1,0:T(8,128)(2,1)S(1)}, u32[]{:S(2)}, u32[]{:S(2)}) %all-to-all-start.3) | async-done | bytes 786464 | tf_op jit(solution)/shard_map/all_to_all | solution.py:319
  157.7 10.9 %shard_map.110 = (bf16[8,768,128]{2,1,0:T(8,128)(2,1)}, bf16[1,384,128]{2,1,0:T(8,128)(2,1)}) custom-call(s32[3]{0:T(128)S(1)} %pad_add_fusion.place, bf16[1,384,128]{2,1,0:T(8,128)(2,1)S(1)} %collective-permute-done.11.x_in, f32[8,5,384]{2,1,0:T(8,128)S(1)} %copy-done.7, bf16[384,128]{1,0:T(8,128)(2,1)S(1)} %bitcast.27, ...), custom_call_target="tpu_custom_call", output_to_operand_aliasing={{0}: (10, {})} | custom-call | bytes 1024 | tf_op jit(solution)/shard_map/pallas_call | solution.py:250
  168.7 3.6 %all-to-all-start.4 = ((bf16[8,768,128]{2,1,0:T(8,128)(2,1)}), bf16[8,768,128]{2,1,0:T(8,128)(2,1)S(1)}, u32[]{:S(2)}, u32[]{:S(2)}) async-start(bf16[8,768,128]{2,1,0:T(8,128)(2,1)} %get-tuple-element.28), calls=%async_computation.4 | async-start | bytes 3145728 | tf_op jit(solution)/shard_map/all_to_all | solution.py:319
  172.3 2.2 %shard_map.111.refs_1_ = bf16[1,384,2560]{2,1,0:T(8,128)(2,1)} custom-call(bf16[8,384,128]{2,1,0:T(8,128)(2,1)} %copy-done.4), custom_call_target="tpu_custom_call" | custom-call | bytes 1024 | tf_op jit(solution)/shard_map/pallas_call | solution.py:328
  174.5 19.3 %all-to-all-done.4.refs_0_ = bf16[8,768,128]{2,1,0:T(8,128)(2,1)S(1)} async-done(((bf16[8,768,128]{2,1,0:T(8,128)(2,1)}), bf16[8,768,128]{2,1,0:T(8,128)(2,1)S(1)}, u32[]{:S(2)}, u32[]{:S(2)}) %all-to-all-start.4) | async-done | bytes 1572896 | tf_op jit(solution)/shard_map/all_to_all | solution.py:319
  195.0 2.6 %shard_map.112 = bf16[1,384,2560]{2,1,0:T(8,128)(2,1)} custom-call(bf16[8,768,128]{2,1,0:T(8,128)(2,1)} %copy-done.16, bf16[1,384,2560]{2,1,0:T(8,128)(2,1)} %shard_map.111.refs_1_), custom_call_target="tpu_custom_call", output_to_operand_aliasing={{}: (1, {})} | custom-call | bytes 1024 | tf_op jit(solution)/shard_map/pallas_call | solution.py:328
  (87 shorter events, 17.1 us)
Async XLA Ops:
  5.3 4.6 %copy-start.17 = (bf16[8,384,128]{2,1,0:T(8,128)(2,1)S(1)}, bf16[8,384,128]{2,1,0:T(8,128)(2,1)}, u32[]{:S(2)}) copy-start(bf16[8,384,128]{2,1,0:T(8,128)(2,1)} %shard_map.100._) | copy-start | bytes 2359300
  5.3 10.5 %copy-start.19 = (f32[1,2560]{1,0:T(1,128)S(1)}, f32[1,2560]{1,0:T(1,128)}, u32[]{:S(2)}) copy-start(f32[1,2560]{1,0:T(1,128)} %param.12) | copy-start | bytes 30724
  5.3 30.4 %all-to-all-start = ((bf16[8,960,128]{2,1,0:T(8,128)(2,1)}), bf16[8,960,128]{2,1,0:T(8,128)(2,1)S(1)}, u32[]{:S(2)}, u32[]{:S(2)}) async-start(bf16[8,960,128]{2,1,0:T(8,128)(2,1)} %shard_map.101), calls=%async_computation | async-start | bytes 3932160 | tf_op jit(solution)/shard_map/all_to_all | solution.py:319
  9.9 30.4 %collective-permute-start = (bf16[8,384,128]{2,1,0:T(8,128)(2,1)S(1)}, bf16[8,384,128]{2,1,0:T(8,128)(2,1)S(1)}, u32[]{:S(2)}, u32[]{:S(2)}) collective-permute-start(bf16[8,384,128]{2,1,0:T(8,128)(2,1)S(1)} %copy-done.17), channel_id=1, source_target_pairs={{0,1},{1,2},{2,3},{3,4},{4,5},{5,6},{6,7},{7,8},{8,9},{9,10},{10,1... | collective-permute-start | bytes 2359304 | tf_op jit(solution)/shard_map/ppermute | solution.py:322
  12.9 27.5 %collective-permute-start.1 = (bf16[8,384,128]{2,1,0:T(8,128)(2,1)S(1)}, bf16[8,384,128]{2,1,0:T(8,128)(2,1)}, u32[]{:S(2)}, u32[]{:S(2)}) collective-permute-start(bf16[8,384,128]{2,1,0:T(8,128)(2,1)S(1)} %copy-done.17), channel_id=1, source_target_pairs={{1,0},{2,1},{3,2},{4,3},{5,4},{6,5},{7,6},{8,7},{9,8},{10,9},{11,1... | collective-permute-start | bytes 2359304 | tf_op jit(solution)/shard_map/ppermute | solution.py:322
  37.0 9.1 %all-to-all-start.1 = ((f32[8,5,384]{2,1,0:T(8,128)}), f32[8,5,384]{2,1,0:T(8,128)S(1)}, u32[]{:S(2)}, u32[]{:S(2)}) async-start(f32[8,5,384]{2,1,0:T(8,128)} %shard_map.102), calls=%async_computation.1 | async-start | bytes 196608 | tf_op jit(solution)/shard_map/all_to_all | solution.py:319
  40.4 5.7 %copy-start.18 = (bf16[8,384,128]{2,1,0:T(8,128)(2,1)}, bf16[8,384,128]{2,1,0:T(8,128)(2,1)S(1)}, u32[]{:S(2)}) copy-start(bf16[8,384,128]{2,1,0:T(8,128)(2,1)S(1)} %collective-permute-done.low) | copy-start | bytes 2359300
  52.0 6.7 %copy-start.21 = (s32[6]{0:T(128)S(1)}, s32[6]{0:T(128)}, u32[]{:S(2)}) copy-start(s32[6]{0:T(128)} %param.18) | copy-start | bytes 76
  52.0 9.7 %copy-start.22 = (s32[1,6]{1,0:T(1,128)S(1)}, s32[1,6]{1,0:T(1,128)}, u32[]{:S(2)}) copy-start(s32[1,6]{1,0:T(1,128)} %param.19) | copy-start | bytes 76
  52.0 11.1 %copy-start.20 = (s32[6,18]{1,0:T(8,128)S(1)}, s32[6,18]{1,0:T(8,128)}, u32[]{:S(2)}) copy-start(s32[6,18]{1,0:T(8,128)} %param.17) | copy-start | bytes 1300
  52.0 29.3 %copy-start.1 = (bf16[8,960,128]{2,1,0:T(8,128)(2,1)S(1)}, bf16[8,960,128]{2,1,0:T(8,128)(2,1)}, u32[]{:S(2)}) copy-start(bf16[8,960,128]{2,1,0:T(8,128)(2,1)} %copy-done) | copy-start | bytes 5898244
  52.1 29.2 %all-to-all-start.2 = ((bf16[8,768,128]{2,1,0:T(8,128)(2,1)}), bf16[8,768,128]{2,1,0:T(8,128)(2,1)S(1)}, u32[]{:S(2)}, u32[]{:S(2)}) async-start(bf16[8,768,128]{2,1,0:T(8,128)(2,1)} %shard_map.104), calls=%async_computation.2 | async-start | bytes 3145728 | tf_op jit(solution)/shard_map/all_to_all | solution.py:319
  55.8 22.6 %collective-permute-start.7 = (bf16[8,384,128]{2,1,0:T(8,128)(2,1)}, bf16[8,384,128]{2,1,0:T(8,128)(2,1)}, u32[]{:S(2)}, u32[]{:S(2)}) collective-permute-start(bf16[8,384,128]{2,1,0:T(8,128)(2,1)} %get-tuple-element.18._.refs_0_), channel_id=1, source_target_pairs={{0,1},{1,2},{2,3},{3,4},{4,5},{5,6},{6,7},{7,8},{8,9},{9,10},{10,1... | collective-permute-start | bytes 2359304 | tf_op jit(solution)/shard_map/ppermute | solution.py:322
  58.8 25.8 %collective-permute-start.8 = (bf16[8,384,128]{2,1,0:T(8,128)(2,1)}, bf16[8,384,128]{2,1,0:T(8,128)(2,1)}, u32[]{:S(2)}, u32[]{:S(2)}) collective-permute-start(bf16[8,384,128]{2,1,0:T(8,128)(2,1)} %get-tuple-element.18._.refs_0_), channel_id=1, source_target_pairs={{1,0},{2,1},{3,2},{4,3},{5,4},{6,5},{7,6},{8,7},{9,8},{10,9},{11,1... | collective-permute-start | bytes 2359304 | tf_op jit(solution)/shard_map/ppermute | solution.py:322
  61.9 10.2 %collective-permute-start.2 = (bf16[8,192,128]{2,1,0:T(8,128)(2,1)}, bf16[8,192,128]{2,1,0:T(8,128)(2,1)}, u32[]{:S(2)}, u32[]{:S(2)}) collective-permute-start(bf16[8,192,128]{2,1,0:T(8,128)(2,1)} %get-tuple-element.17.refs_0_), channel_id=1, source_target_pairs={{16,0},{17,1},{18,2},{19,3},{20,4},{21,5},{22,6},{23,7},{24,8},{25... | collective-permute-start | bytes 1179656 | tf_op jit(solution)/shard_map/ppermute | solution.py:401
  66.9 70.1 %collective-permute-start.3 = (bf16[8,192,128]{2,1,0:T(8,128)(2,1)}, bf16[8,192,128]{2,1,0:T(8,128)(2,1)}, u32[]{:S(2)}, u32[]{:S(2)}) collective-permute-start(bf16[8,192,128]{2,1,0:T(8,128)(2,1)} %get-tuple-element.17.refs_0_), channel_id=1, source_target_pairs={{0,1},{1,2},{2,3},{3,4},{4,5},{5,6},{6,7},{7,8},{8,9},{9,10},{10,1... | collective-permute-start | bytes 1179656 | tf_op jit(solution)/shard_map/ppermute | solution.py:401
  70.7 66.4 %collective-permute-start.4 = (bf16[8,192,128]{2,1,0:T(8,128)(2,1)}, bf16[8,192,128]{2,1,0:T(8,128)(2,1)}, u32[]{:S(2)}, u32[]{:S(2)}) collective-permute-start(bf16[8,192,128]{2,1,0:T(8,128)(2,1)} %get-tuple-element.17.refs_0_), channel_id=1, source_target_pairs={{16,1},{17,2},{18,3},{19,4},{20,5},{21,6},{22,7},{23,8},{24,9},{25... | collective-permute-start | bytes 1179656 | tf_op jit(solution)/shard_map/ppermute | solution.py:401
  72.0 65.1 %collective-permute-start.5 = (bf16[8,192,128]{2,1,0:T(8,128)(2,1)}, bf16[8,192,128]{2,1,0:T(8,128)(2,1)}, u32[]{:S(2)}, u32[]{:S(2)}) collective-permute-start(bf16[8,192,128]{2,1,0:T(8,128)(2,1)} %get-tuple-element.17.refs_0_), channel_id=1, source_target_pairs={{1,0},{2,1},{3,2},{4,3},{5,4},{6,5},{7,6},{8,7},{9,8},{10,9},{11,1... | collective-permute-start | bytes 1179656 | tf_op jit(solution)/shard_map/ppermute | solution.py:401
  78.4 58.7 %collective-permute-start.6 = (bf16[8,192,128]{2,1,0:T(8,128)(2,1)}, bf16[8,192,128]{2,1,0:T(8,128)(2,1)}, u32[]{:S(2)}, u32[]{:S(2)}) collective-permute-start(bf16[8,192,128]{2,1,0:T(8,128)(2,1)} %get-tuple-element.17.refs_0_), channel_id=1, source_target_pairs={{17,0},{18,1},{19,2},{20,3},{21,4},{22,5},{23,6},{24,7},{25,8},{26... | collective-permute-start | bytes 1179656 | tf_op jit(solution)/shard_map/ppermute | solution.py:401
  81.3 55.8 %copy-start.8 = (bf16[6,64,128]{2,1,0:T(8,128)(2,1)}, bf16[6,64,128]{2,1,0:T(8,128)(2,1)S(1)}, u32[]{:S(2)}) copy-start(bf16[6,64,128]{2,1,0:T(8,128)(2,1)S(1)} %broadcast_in_dim.40) | copy-start | bytes 294916
  84.7 38.2 %collective-permute-start.9 = (bf16[1,384,128]{2,1,0:T(8,128)(2,1)S(1)}, bf16[1,384,128]{2,1,0:T(8,128)(2,1)S(1)}, u32[]{:S(2)}, u32[]{:S(2)}) collective-permute-start(bf16[1,384,128]{2,1,0:T(8,128)(2,1)S(1)} %get-tuple-element.19.refs_3_), channel_id=1, source_target_pairs={{0,128},{16,144},{32,160},{48,176},{64,192},{80,208},{96,224},{112... | collective-permute-start | bytes 294920 | tf_op jit(solution)/shard_map/ppermute | solution.py:420
  122.8 14.3 %collective-permute-start.10 = (bf16[1,384,128]{2,1,0:T(8,128)(2,1)S(1)}, bf16[1,384,128]{2,1,0:T(8,128)(2,1)S(1)}, u32[]{:S(2)}, u32[]{:S(2)}) collective-permute-start(bf16[1,384,128]{2,1,0:T(8,128)(2,1)S(1)} %get-tuple-element.22.refs_3_), channel_id=1, source_target_pairs={{0,128},{16,144},{32,160},{48,176},{64,192},{80,208},{96,224},{112... | collective-permute-start | bytes 294920 | tf_op jit(solution)/shard_map/ppermute | solution.py:420
  124.1 13.0 %copy-start.12 = (bf16[8,192,128]{2,1,0:T(8,128)(2,1)S(1)}, bf16[8,192,128]{2,1,0:T(8,128)(2,1)}, u32[]{:S(2)}) copy-start(bf16[8,192,128]{2,1,0:T(8,128)(2,1)} %get-tuple-element.17.refs_0_) | copy-start | bytes 1179652
  138.2 6.3 %copy-start.7 = (f32[8,5,384]{2,1,0:T(8,128)S(1)}, f32[8,5,384]{2,1,0:T(8,128)}, u32[]{:S(2)}) copy-start(f32[8,5,384]{2,1,0:T(8,128)} %copy-done.5) | copy-start | bytes 184324
  138.3 6.3 %copy-start.9 = (bf16[6,64,128]{2,1,0:T(8,128)(2,1)S(1)}, bf16[6,64,128]{2,1,0:T(8,128)(2,1)}, u32[]{:S(2)}) copy-start(bf16[6,64,128]{2,1,0:T(8,128)(2,1)} %copy-done.8) | copy-start | bytes 294916
  138.3 6.3 %copy-start.11 = (bf16[8,384,128]{2,1,0:T(8,128)(2,1)S(1)}, bf16[8,384,128]{2,1,0:T(8,128)(2,1)}, u32[]{:S(2)}) copy-start(bf16[8,384,128]{2,1,0:T(8,128)(2,1)} %get-tuple-element.18._.refs_0_) | copy-start | bytes 2359300
  138.3 6.3 %copy-start.15 = (bf16[1,384,128]{2,1,0:T(8,128)(2,1)S(1)}, bf16[1,384,128]{2,1,0:T(8,128)(2,1)}, u32[]{:S(2)}) copy-start(bf16[1,384,128]{2,1,0:T(8,128)(2,1)} %copy-done.14) | copy-start | bytes 294916
  138.3 17.3 %collective-permute-start.11 = (bf16[1,384,128]{2,1,0:T(8,128)(2,1)S(1)}, bf16[1,384,128]{2,1,0:T(8,128)(2,1)S(1)}, u32[]{:S(2)}, u32[]{:S(2)}) collective-permute-start(bf16[1,384,128]{2,1,0:T(8,128)(2,1)S(1)} %get-tuple-element.24), channel_id=1, source_target_pairs={{0,128},{32,160},{64,192},{96,224},{1,129},{33,161},{65,193},{97,2... | collective-permute-start | bytes 294920 | tf_op jit(solution)/shard_map/ppermute | solution.py:420
  139.7 18.0 %all-to-all-start.3 = ((bf16[8,384,128]{2,1,0:T(8,128)(2,1)}), bf16[8,384,128]{2,1,0:T(8,128)(2,1)S(1)}, u32[]{:S(2)}, u32[]{:S(2)}) async-start(bf16[8,384,128]{2,1,0:T(8,128)(2,1)} %get-tuple-element.27), calls=%async_computation.3 | async-start | bytes 1572864 | tf_op jit(solution)/shard_map/all_to_all | solution.py:319
  144.6 13.1 %copy-start.13 = (bf16[8,192,128]{2,1,0:T(8,128)(2,1)S(1)}, bf16[8,192,128]{2,1,0:T(8,128)(2,1)}, u32[]{:S(2)}) copy-start(bf16[8,192,128]{2,1,0:T(8,128)(2,1)} %get-tuple-element.17.refs_0_) | copy-start | bytes 1179652
  157.7 10.9 %copy-start.4 = (bf16[8,384,128]{2,1,0:T(8,128)(2,1)}, bf16[8,384,128]{2,1,0:T(8,128)(2,1)S(1)}, u32[]{:S(2)}) copy-start(bf16[8,384,128]{2,1,0:T(8,128)(2,1)S(1)} %all-to-all-done.3.refs_7_.refs_0_) | copy-start | bytes 2359300
  168.7 25.1 %all-to-all-start.4 = ((bf16[8,768,128]{2,1,0:T(8,128)(2,1)}), bf16[8,768,128]{2,1,0:T(8,128)(2,1)S(1)}, u32[]{:S(2)}, u32[]{:S(2)}) async-start(bf16[8,768,128]{2,1,0:T(8,128)(2,1)} %get-tuple-element.28), calls=%async_computation.4 | async-start | bytes 3145728 | tf_op jit(solution)/shard_map/all_to_all | solution.py:319
  (8 other events, 11.0 us)

commit v4 on v3

--- a/solution.py
+++ b/solution.py
@@ -434,7 +434,7 @@
 
     layers_a, last_a = run("a", 0, tokens_in, [], [])
     next_a = hop(last_a, 1)
-    layers, last_b = run("b", 0, tokens_in, [], [last_a])
+    layers, last_b = run("b", 0, tokens_in, [], [last_a], LARGE)
     next_b = hop(last_b, 1)
     layers_a, done_a = run("a", 1, next_a, [layers_a], [last_b])
     arrived_a = exchange(layers_a)

time: 201 us -> 199 us (0.990)
  waiting for transfers between devices: 83.7 us -> 80.4 us
    ppermute x2, waiting for transfers between devices: 4.28 us -> 0.01 us  [both_ways(): lax.ppermute(array, 'seq', forward)]
    all_to_all x5, waiting for transfers between devices: 43.4 us -> 46.9 us  [exchange(): lax.all_to_all(array, 'section', 0, 0, axis_index_groups=groups, tiled=True)]
    ppermute x3, waiting for transfers between devices: 36 us -> 33.4 us  [hop(): lax.ppermute(last, 'section', [(i, i + GROUP) for i in range(0, GROUP, st...]
    unnamed x46 -> x54, local copies, waits for them, and re-layouts: 5.62 us -> 5.76 us
where the time goes in v4:
time: 199 us; the launch traced here: 196 us
  waiting for transfers between devices  80.4 us (40%)
  Pallas kernels  53.9 us (27%)
  starting transfers between devices  46 us (23%)
  local copies, waits for them, and re-layouts  13.3 us (7%)
    all_to_all x5, waiting for transfers between devices, exchange(): lax.all_to_all(array, 'section', 0, 0, axis_index_groups=groups, tiled=True)  46.9 us
    pallas_call x6, Pallas kernels, attention(): pl.pallas_call(functools.partial(attention_kernel, (heads, stage, len(kv)...  38.4 us
    ppermute x3, waiting for transfers between devices, hop(): lax.ppermute(last, 'section', [(i, i + GROUP) for i in range(0, GROUP, st...  33.4 us
    all_to_all x5, starting transfers between devices, exchange(): lax.all_to_all(array, 'section', 0, 0, axis_index_groups=groups, tiled=True)  19.7 us
    pallas_call x7, Pallas kernels, call(): pl.pallas_call(kernel, out_shape=out_shape, in_specs=in_specs, out_specs=...  15.5 us
    ppermute x5, starting transfers between devices, to_first_core(): return lax.ppermute(array, ('section', 'seq'), pairs)  10.6 us
    ppermute x2, starting transfers between devices, both_ways(): lax.ppermute(array, 'seq', forward)  5.87 us
    ppermute x2, starting transfers between devices, both_ways(): lax.ppermute(array, 'seq', backward)  5.83 us
  transfers between devices with their start and end apart: 17, of which 6 were waited for; matrix products, arithmetic and copies ran while one was open for 5% of the time, Pallas kernels for 14%

profile of v4, /device:TPU:198, one launch (start us, length us, event | category | flops | bytes accessed | tf_op | source)
XLA Modules:
  0.0 195.8 jit_solution(7574268088627380281)
XLA Ops:
  0.0 2.2 %shard_map.100._ = bf16[8,384,128]{2,1,0:T(8,128)(2,1)} custom-call(bf16[1,384,2560]{2,1,0:T(8,128)(2,1)} %values.3), custom_call_target="tpu_custom_call" | custom-call | bytes 1024 | tf_op jit(solution)/shard_map/pallas_call | solution.py:328
  2.2 3.2 %shard_map.101 = bf16[8,960,128]{2,1,0:T(8,128)(2,1)} custom-call(bf16[1,384,2560]{2,1,0:T(8,128)(2,1)} %values.3, bf16[8,384,128]{2,1,0:T(8,128)(2,1)} %shard_map.100._), custom_call_target="tpu_custom_call" | custom-call | bytes 1024 | tf_op jit(solution)/shard_map/pallas_call | solution.py:328
  5.3 4.6 %all-to-all-start = ((bf16[8,960,128]{2,1,0:T(8,128)(2,1)}), bf16[8,960,128]{2,1,0:T(8,128)(2,1)S(1)}, u32[]{:S(2)}, u32[]{:S(2)}) async-start(bf16[8,960,128]{2,1,0:T(8,128)(2,1)} %shard_map.101), calls=%async_computation | async-start | bytes 3932160 | tf_op jit(solution)/shard_map/all_to_all | solution.py:319
  9.9 2.9 %collective-permute-start = (bf16[8,384,128]{2,1,0:T(8,128)(2,1)S(1)}, bf16[8,384,128]{2,1,0:T(8,128)(2,1)S(1)}, u32[]{:S(2)}, u32[]{:S(2)}) collective-permute-start(bf16[8,384,128]{2,1,0:T(8,128)(2,1)S(1)} %copy-done.21), channel_id=1, source_target_pairs={{0,1},{1,2},{2,3},{3,4},{4,5},{5,6},{6,7},{7,8},{8,9},{9,10},{10,1... | collective-permute-start | bytes 2359304 | tf_op jit(solution)/shard_map/ppermute | solution.py:322
  12.9 2.9 %collective-permute-start.1 = (bf16[8,384,128]{2,1,0:T(8,128)(2,1)S(1)}, bf16[8,384,128]{2,1,0:T(8,128)(2,1)}, u32[]{:S(2)}, u32[]{:S(2)}) collective-permute-start(bf16[8,384,128]{2,1,0:T(8,128)(2,1)S(1)} %copy-done.21), channel_id=1, source_target_pairs={{1,0},{2,1},{3,2},{4,3},{5,4},{6,5},{7,6},{8,7},{9,8},{10,9},{11,1... | collective-permute-start | bytes 2359304 | tf_op jit(solution)/shard_map/ppermute | solution.py:322
  15.8 1.5 concatenate.7
  19.4 16.3 %all-to-all-done.refs_1_.owned.refs_0_ = bf16[8,960,128]{2,1,0:T(8,128)(2,1)S(1)} async-done(((bf16[8,960,128]{2,1,0:T(8,128)(2,1)}), bf16[8,960,128]{2,1,0:T(8,128)(2,1)S(1)}, u32[]{:S(2)}, u32[]{:S(2)}) %all-to-all-start) | async-done | bytes 1966112 | tf_op jit(solution)/shard_map/all_to_all | solution.py:319
  37.0 3.4 %all-to-all-start.1 = ((f32[8,5,384]{2,1,0:T(8,128)}), f32[8,5,384]{2,1,0:T(8,128)S(1)}, u32[]{:S(2)}, u32[]{:S(2)}) async-start(f32[8,5,384]{2,1,0:T(8,128)} %shard_map.102), calls=%async_computation.1 | async-start | bytes 196608 | tf_op jit(solution)/shard_map/all_to_all | solution.py:319
  40.4 5.7 %all-to-all-done.1.vectors.params = f32[8,5,384]{2,1,0:T(8,128)S(1)} async-done(((f32[8,5,384]{2,1,0:T(8,128)}), f32[8,5,384]{2,1,0:T(8,128)S(1)}, u32[]{:S(2)}, u32[]{:S(2)}) %all-to-all-start.1) | async-done | bytes 61472 | tf_op jit(solution)/shard_map/all_to_all | solution.py:319
  46.7 2.7 %shard_map.103 = (bf16[8,384,128]{2,1,0:T(8,128)(2,1)}, bf16[8,192,128]{2,1,0:T(8,128)(2,1)}) custom-call(bf16[8,960,128]{2,1,0:T(8,128)(2,1)} %copy-done, bf16[8,384,128]{2,1,0:T(8,128)(2,1)} %copy-done.22, bf16[8,384,128]{2,1,0:T(8,128)(2,1)} %collective-permute-done.1.high, f32[8,5,384]{2,1,0:T(8,128)} %copy-done.5), custom_call_target="tpu_custom_call" | custom-call | bytes 1024 | tf_op jit(solution)/shard_map/pallas_call | solution.py:328
  49.4 2.6 %shard_map.104 = bf16[8,768,128]{2,1,0:T(8,128)(2,1)} custom-call(bf16[8,384,128]{2,1,0:T(8,128)(2,1)} %copy-done.22, bf16[8,384,128]{2,1,0:T(8,128)(2,1)} %collective-permute-done.1.high, bf16[8,384,128]{2,1,0:T(8,128)(2,1)} %get-tuple-element.18._.refs_0_), custom_call_target="tpu_custom_call" | custom-call | bytes 1024 | tf_op jit(solution)/shard_map/pallas_call | solution.py:328
  52.0 3.7 %all-to-all-start.2 = ((bf16[8,768,128]{2,1,0:T(8,128)(2,1)}), bf16[8,768,128]{2,1,0:T(8,128)(2,1)S(1)}, u32[]{:S(2)}, u32[]{:S(2)}) async-start(bf16[8,768,128]{2,1,0:T(8,128)(2,1)} %shard_map.104), calls=%async_computation.2 | async-start | bytes 3145728 | tf_op jit(solution)/shard_map/all_to_all | solution.py:319
  55.9 2.9 %collective-permute-start.7 = (bf16[8,384,128]{2,1,0:T(8,128)(2,1)}, bf16[8,384,128]{2,1,0:T(8,128)(2,1)}, u32[]{:S(2)}, u32[]{:S(2)}) collective-permute-start(bf16[8,384,128]{2,1,0:T(8,128)(2,1)} %get-tuple-element.18._.refs_0_), channel_id=1, source_target_pairs={{0,1},{1,2},{2,3},{3,4},{4,5},{5,6},{6,7},{7,8},{8,9},{9,10},{10,1... | collective-permute-start | bytes 2359304 | tf_op jit(solution)/shard_map/ppermute | solution.py:322
  58.9 2.9 %collective-permute-start.8 = (bf16[8,384,128]{2,1,0:T(8,128)(2,1)}, bf16[8,384,128]{2,1,0:T(8,128)(2,1)}, u32[]{:S(2)}, u32[]{:S(2)}) collective-permute-start(bf16[8,384,128]{2,1,0:T(8,128)(2,1)} %get-tuple-element.18._.refs_0_), channel_id=1, source_target_pairs={{1,0},{2,1},{3,2},{4,3},{5,4},{6,5},{7,6},{8,7},{9,8},{10,9},{11,1... | collective-permute-start | bytes 2359304 | tf_op jit(solution)/shard_map/ppermute | solution.py:322
  65.0 1.3 copy.23
  68.6 3.8 %collective-permute-start.3 = (bf16[8,192,128]{2,1,0:T(8,128)(2,1)}, bf16[8,192,128]{2,1,0:T(8,128)(2,1)}, u32[]{:S(2)}, u32[]{:S(2)}) collective-permute-start(bf16[8,192,128]{2,1,0:T(8,128)(2,1)} %get-tuple-element.17.refs_0_), channel_id=1, source_target_pairs={{0,1},{1,2},{2,3},{3,4},{4,5},{5,6},{6,7},{7,8},{8,9},{9,10},{10,1... | collective-permute-start | bytes 1179656 | tf_op jit(solution)/shard_map/ppermute | solution.py:401
  72.4 1.3 collective-permute-start.4
  73.7 3.5 %all-to-all-done.2.refs_1_ = bf16[8,768,128]{2,1,0:T(8,128)(2,1)S(1)} async-done(((bf16[8,768,128]{2,1,0:T(8,128)(2,1)}), bf16[8,768,128]{2,1,0:T(8,128)(2,1)S(1)}, u32[]{:S(2)}, u32[]{:S(2)}) %all-to-all-start.2) | async-done | bytes 1572896 | tf_op jit(solution)/shard_map/all_to_all | solution.py:319
  77.3 1.6 copy-done.2
  80.8 2.9 %collective-permute-start.5 = (bf16[8,192,128]{2,1,0:T(8,128)(2,1)S(1)}, bf16[8,192,128]{2,1,0:T(8,128)(2,1)S(1)}, u32[]{:S(2)}, u32[]{:S(2)}) collective-permute-start(bf16[8,192,128]{2,1,0:T(8,128)(2,1)S(1)} %copy-done.10), channel_id=1, source_target_pairs={{1,0},{2,1},{3,2},{4,3},{5,4},{6,5},{7,6},{8,7},{9,8},{10,9},{11,1... | collective-permute-start | bytes 1179656 | tf_op jit(solution)/shard_map/ppermute | solution.py:401
  83.7 1.3 collective-permute-start.6
  87.2 33.4 %collective-permute-done.9.x_in = bf16[1,384,128]{2,1,0:T(8,128)(2,1)S(1)} collective-permute-done((bf16[1,384,128]{2,1,0:T(8,128)(2,1)S(1)}, bf16[1,384,128]{2,1,0:T(8,128)(2,1)S(1)}, u32[]{:S(2)}, u32[]{:S(2)}) %collective-permute-start.9) | collective-permute-done | bytes 98336 | tf_op jit(solution)/shard_map/ppermute | solution.py:420
  121.9 12.9 %shard_map.107 = (bf16[8,384,128]{2,1,0:T(8,128)(2,1)}, bf16[1,384,128]{2,1,0:T(8,128)(2,1)S(1)}) custom-call(s32[3]{0:T(128)S(1)} %pad_add_fusion.place, bf16[1,384,128]{2,1,0:T(8,128)(2,1)S(1)} %collective-permute-done.9.x_in, f32[8,5,384]{2,1,0:T(8,128)S(1)} %copy-done.6, bf16[384,128]{1,0:T(8,128)(2,1)S(1)} %bitcast.24, ...), custom_call_target="tpu_custom_call", output_to_operand_aliasing={{0}: (6, {})} | custom-call | bytes 1024 | tf_op jit(solution)/shard_map/pallas_call | solution.py:250
  136.1 1.4 collective-permute-start.11
  137.5 4.5 %all-to-all-start.3 = ((bf16[8,384,128]{2,1,0:T(8,128)(2,1)}), bf16[8,384,128]{2,1,0:T(8,128)(2,1)S(1)}, u32[]{:S(2)}, u32[]{:S(2)}) async-start(bf16[8,384,128]{2,1,0:T(8,128)(2,1)} %get-tuple-element.27), calls=%async_computation.3 | async-start | bytes 1572864 | tf_op jit(solution)/shard_map/all_to_all | solution.py:319
  142.0 11.0 %shard_map.109 = (bf16[8,768,128]{2,1,0:T(8,128)(2,1)}, bf16[1,384,128]{2,1,0:T(8,128)(2,1)}) custom-call(s32[3]{0:T(128)S(1)} %pad_add_fusion.place, bf16[1,384,128]{2,1,0:T(8,128)(2,1)S(1)} %copy-done.19, f32[8,5,384]{2,1,0:T(8,128)S(1)} %copy-done.7, bf16[384,128]{1,0:T(8,128)(2,1)S(1)} %bitcast.26, ...), custom_call_target="tpu_custom_call", output_to_operand_aliasing={{0}: (7, {})} | custom-call | flops 137438953472 | bytes 67108864 | tf_op jit(solution)/shard_map/pallas_call | solution.py:250
  153.0 2.1 %all-to-all-done.3.refs_7_.refs_0_ = bf16[8,384,128]{2,1,0:T(8,128)(2,1)S(1)} async-done(((bf16[8,384,128]{2,1,0:T(8,128)(2,1)}), bf16[8,384,128]{2,1,0:T(8,128)(2,1)S(1)}, u32[]{:S(2)}, u32[]{:S(2)}) %all-to-all-start.3) | async-done | bytes 786464 | tf_op jit(solution)/shard_map/all_to_all | solution.py:319
  155.1 11.8 %shard_map.110 = (bf16[8,768,128]{2,1,0:T(8,128)(2,1)}, bf16[1,384,128]{2,1,0:T(8,128)(2,1)}) custom-call(s32[3]{0:T(128)S(1)} %pad_add_fusion.place, bf16[1,384,128]{2,1,0:T(8,128)(2,1)S(1)} %collective-permute-done.11.x_in, f32[8,5,384]{2,1,0:T(8,128)S(1)} %copy-done.7, bf16[384,128]{1,0:T(8,128)(2,1)S(1)} %bitcast.27, ...), custom_call_target="tpu_custom_call", output_to_operand_aliasing={{0}: (10, {})} | custom-call | bytes 1024 | tf_op jit(solution)/shard_map/pallas_call | solution.py:250
  166.9 3.6 %all-to-all-start.4 = ((bf16[8,768,128]{2,1,0:T(8,128)(2,1)}), bf16[8,768,128]{2,1,0:T(8,128)(2,1)S(1)}, u32[]{:S(2)}, u32[]{:S(2)}) async-start(bf16[8,768,128]{2,1,0:T(8,128)(2,1)} %get-tuple-element.28), calls=%async_computation.4 | async-start | bytes 3145728 | tf_op jit(solution)/shard_map/all_to_all | solution.py:319
  170.5 2.2 %shard_map.111.refs_1_ = bf16[1,384,2560]{2,1,0:T(8,128)(2,1)} custom-call(bf16[8,384,128]{2,1,0:T(8,128)(2,1)} %copy-done.4), custom_call_target="tpu_custom_call" | custom-call | bytes 1024 | tf_op jit(solution)/shard_map/pallas_call | solution.py:328
  172.7 19.3 %all-to-all-done.4.refs_0_ = bf16[8,768,128]{2,1,0:T(8,128)(2,1)S(1)} async-done(((bf16[8,768,128]{2,1,0:T(8,128)(2,1)}), bf16[8,768,128]{2,1,0:T(8,128)(2,1)S(1)}, u32[]{:S(2)}, u32[]{:S(2)}) %all-to-all-start.4) | async-done | bytes 1572896 | tf_op jit(solution)/shard_map/all_to_all | solution.py:319
  193.2 2.6 %shard_map.112 = bf16[1,384,2560]{2,1,0:T(8,128)(2,1)} custom-call(bf16[8,768,128]{2,1,0:T(8,128)(2,1)} %copy-done.20, bf16[1,384,2560]{2,1,0:T(8,128)(2,1)} %shard_map.111.refs_1_), custom_call_target="tpu_custom_call", output_to_operand_aliasing={{}: (1, {})} | custom-call | bytes 1024 | tf_op jit(solution)/shard_map/pallas_call | solution.py:328
  (95 shorter events, 17.3 us)
Async XLA Ops:
  5.3 10.5 %copy-start.23 = (f32[1,2560]{1,0:T(1,128)S(1)}, f32[1,2560]{1,0:T(1,128)}, u32[]{:S(2)}) copy-start(f32[1,2560]{1,0:T(1,128)} %param.12) | copy-start | bytes 30724
  5.3 30.4 %all-to-all-start = ((bf16[8,960,128]{2,1,0:T(8,128)(2,1)}), bf16[8,960,128]{2,1,0:T(8,128)(2,1)S(1)}, u32[]{:S(2)}, u32[]{:S(2)}) async-start(bf16[8,960,128]{2,1,0:T(8,128)(2,1)} %shard_map.101), calls=%async_computation | async-start | bytes 3932160 | tf_op jit(solution)/shard_map/all_to_all | solution.py:319
  9.9 30.4 %collective-permute-start = (bf16[8,384,128]{2,1,0:T(8,128)(2,1)S(1)}, bf16[8,384,128]{2,1,0:T(8,128)(2,1)S(1)}, u32[]{:S(2)}, u32[]{:S(2)}) collective-permute-start(bf16[8,384,128]{2,1,0:T(8,128)(2,1)S(1)} %copy-done.21), channel_id=1, source_target_pairs={{0,1},{1,2},{2,3},{3,4},{4,5},{5,6},{6,7},{7,8},{8,9},{9,10},{10,1... | collective-permute-start | bytes 2359304 | tf_op jit(solution)/shard_map/ppermute | solution.py:322
  12.9 27.5 %collective-permute-start.1 = (bf16[8,384,128]{2,1,0:T(8,128)(2,1)S(1)}, bf16[8,384,128]{2,1,0:T(8,128)(2,1)}, u32[]{:S(2)}, u32[]{:S(2)}) collective-permute-start(bf16[8,384,128]{2,1,0:T(8,128)(2,1)S(1)} %copy-done.21), channel_id=1, source_target_pairs={{1,0},{2,1},{3,2},{4,3},{5,4},{6,5},{7,6},{8,7},{9,8},{10,9},{11,1... | collective-permute-start | bytes 2359304 | tf_op jit(solution)/shard_map/ppermute | solution.py:322
  37.0 9.1 %all-to-all-start.1 = ((f32[8,5,384]{2,1,0:T(8,128)}), f32[8,5,384]{2,1,0:T(8,128)S(1)}, u32[]{:S(2)}, u32[]{:S(2)}) async-start(f32[8,5,384]{2,1,0:T(8,128)} %shard_map.102), calls=%async_computation.1 | async-start | bytes 196608 | tf_op jit(solution)/shard_map/all_to_all | solution.py:319
  52.0 9.8 %copy-start.26 = (s32[6]{0:T(128)S(1)}, s32[6]{0:T(128)}, u32[]{:S(2)}) copy-start(s32[6]{0:T(128)} %param.18) | copy-start | bytes 76
  52.0 9.8 %copy-start.24 = (s32[6,18]{1,0:T(8,128)S(1)}, s32[6,18]{1,0:T(8,128)}, u32[]{:S(2)}) copy-start(s32[6,18]{1,0:T(8,128)} %param.17) | copy-start | bytes 1300
  52.0 25.3 %copy-start.1 = (bf16[8,960,128]{2,1,0:T(8,128)(2,1)S(1)}, bf16[8,960,128]{2,1,0:T(8,128)(2,1)}, u32[]{:S(2)}) copy-start(bf16[8,960,128]{2,1,0:T(8,128)(2,1)} %copy-done) | copy-start | bytes 5898244
  52.0 25.2 %all-to-all-start.2 = ((bf16[8,768,128]{2,1,0:T(8,128)(2,1)}), bf16[8,768,128]{2,1,0:T(8,128)(2,1)S(1)}, u32[]{:S(2)}, u32[]{:S(2)}) async-start(bf16[8,768,128]{2,1,0:T(8,128)(2,1)} %shard_map.104), calls=%async_computation.2 | async-start | bytes 3145728 | tf_op jit(solution)/shard_map/all_to_all | solution.py:319
  55.9 27.8 %collective-permute-start.7 = (bf16[8,384,128]{2,1,0:T(8,128)(2,1)}, bf16[8,384,128]{2,1,0:T(8,128)(2,1)}, u32[]{:S(2)}, u32[]{:S(2)}) collective-permute-start(bf16[8,384,128]{2,1,0:T(8,128)(2,1)} %get-tuple-element.18._.refs_0_), channel_id=1, source_target_pairs={{0,1},{1,2},{2,3},{3,4},{4,5},{5,6},{6,7},{7,8},{8,9},{9,10},{10,1... | collective-permute-start | bytes 2359304 | tf_op jit(solution)/shard_map/ppermute | solution.py:322
  58.9 26.1 %collective-permute-start.8 = (bf16[8,384,128]{2,1,0:T(8,128)(2,1)}, bf16[8,384,128]{2,1,0:T(8,128)(2,1)}, u32[]{:S(2)}, u32[]{:S(2)}) collective-permute-start(bf16[8,384,128]{2,1,0:T(8,128)(2,1)} %get-tuple-element.18._.refs_0_), channel_id=1, source_target_pairs={{1,0},{2,1},{3,2},{4,3},{5,4},{6,5},{7,6},{8,7},{9,8},{10,9},{11,1... | collective-permute-start | bytes 2359304 | tf_op jit(solution)/shard_map/ppermute | solution.py:322
  62.0 18.6 %collective-permute-start.2 = (bf16[8,192,128]{2,1,0:T(8,128)(2,1)}, bf16[8,192,128]{2,1,0:T(8,128)(2,1)}, u32[]{:S(2)}, u32[]{:S(2)}) collective-permute-start(bf16[8,192,128]{2,1,0:T(8,128)(2,1)} %get-tuple-element.17.refs_0_), channel_id=1, source_target_pairs={{16,0},{17,1},{18,2},{19,3},{20,4},{21,5},{22,6},{23,7},{24,8},{25... | collective-permute-start | bytes 1179656 | tf_op jit(solution)/shard_map/ppermute | solution.py:401
  68.6 66.2 %collective-permute-start.3 = (bf16[8,192,128]{2,1,0:T(8,128)(2,1)}, bf16[8,192,128]{2,1,0:T(8,128)(2,1)}, u32[]{:S(2)}, u32[]{:S(2)}) collective-permute-start(bf16[8,192,128]{2,1,0:T(8,128)(2,1)} %get-tuple-element.17.refs_0_), channel_id=1, source_target_pairs={{0,1},{1,2},{2,3},{3,4},{4,5},{5,6},{6,7},{7,8},{8,9},{9,10},{10,1... | collective-permute-start | bytes 1179656 | tf_op jit(solution)/shard_map/ppermute | solution.py:401
  72.4 62.4 %collective-permute-start.4 = (bf16[8,192,128]{2,1,0:T(8,128)(2,1)}, bf16[8,192,128]{2,1,0:T(8,128)(2,1)}, u32[]{:S(2)}, u32[]{:S(2)}) collective-permute-start(bf16[8,192,128]{2,1,0:T(8,128)(2,1)} %get-tuple-element.17.refs_0_), channel_id=1, source_target_pairs={{16,1},{17,2},{18,3},{19,4},{20,5},{21,6},{22,7},{23,8},{24,9},{25... | collective-permute-start | bytes 1179656 | tf_op jit(solution)/shard_map/ppermute | solution.py:401
  77.3 57.6 %copy-start.8 = (bf16[6,64,128]{2,1,0:T(8,128)(2,1)}, bf16[6,64,128]{2,1,0:T(8,128)(2,1)S(1)}, u32[]{:S(2)}) copy-start(bf16[6,64,128]{2,1,0:T(8,128)(2,1)S(1)} %broadcast_in_dim.40) | copy-start | bytes 294916
  79.8 6.5 %copy-start.3 = (bf16[384,2560]{1,0:T(8,128)(2,1)S(1)}, bf16[384,2560]{1,0:T(8,128)(2,1)}, u32[]{:S(2)}) copy-start(bf16[384,2560]{1,0:T(8,128)(2,1)} %x_in.5) | copy-start | bytes 5898244
  79.8 6.5 %copy-start.16 = (bf16[8,384,128]{2,1,0:T(8,128)(2,1)S(1)}, bf16[8,384,128]{2,1,0:T(8,128)(2,1)}, u32[]{:S(2)}) copy-start(bf16[8,384,128]{2,1,0:T(8,128)(2,1)} %get-tuple-element.18._.refs_0_) | copy-start | bytes 2359300
  80.8 54.1 %collective-permute-start.5 = (bf16[8,192,128]{2,1,0:T(8,128)(2,1)S(1)}, bf16[8,192,128]{2,1,0:T(8,128)(2,1)S(1)}, u32[]{:S(2)}, u32[]{:S(2)}) collective-permute-start(bf16[8,192,128]{2,1,0:T(8,128)(2,1)S(1)} %copy-done.10), channel_id=1, source_target_pairs={{1,0},{2,1},{3,2},{4,3},{5,4},{6,5},{7,6},{8,7},{9,8},{10,9},{11,1... | collective-permute-start | bytes 1179656 | tf_op jit(solution)/shard_map/ppermute | solution.py:401
  83.7 51.2 %collective-permute-start.6 = (bf16[8,192,128]{2,1,0:T(8,128)(2,1)S(1)}, bf16[8,192,128]{2,1,0:T(8,128)(2,1)S(1)}, u32[]{:S(2)}, u32[]{:S(2)}) collective-permute-start(bf16[8,192,128]{2,1,0:T(8,128)(2,1)S(1)} %copy-done.10), channel_id=1, source_target_pairs={{17,0},{18,1},{19,2},{20,3},{21,4},{22,5},{23,6},{24,7},{25,8},{26... | collective-permute-start | bytes 1179656 | tf_op jit(solution)/shard_map/ppermute | solution.py:401
  85.0 35.6 %collective-permute-start.9 = (bf16[1,384,128]{2,1,0:T(8,128)(2,1)S(1)}, bf16[1,384,128]{2,1,0:T(8,128)(2,1)S(1)}, u32[]{:S(2)}, u32[]{:S(2)}) collective-permute-start(bf16[1,384,128]{2,1,0:T(8,128)(2,1)S(1)} %get-tuple-element.19.refs_3_), channel_id=1, source_target_pairs={{0,128},{16,144},{32,160},{48,176},{64,192},{80,208},{96,224},{112... | collective-permute-start | bytes 294920 | tf_op jit(solution)/shard_map/ppermute | solution.py:420
  120.6 14.3 %collective-permute-start.10 = (bf16[1,384,128]{2,1,0:T(8,128)(2,1)S(1)}, bf16[1,384,128]{2,1,0:T(8,128)(2,1)S(1)}, u32[]{:S(2)}, u32[]{:S(2)}) collective-permute-start(bf16[1,384,128]{2,1,0:T(8,128)(2,1)S(1)} %get-tuple-element.22.refs_3_), channel_id=1, source_target_pairs={{0,128},{16,144},{32,160},{48,176},{64,192},{80,208},{96,224},{112... | collective-permute-start | bytes 294920 | tf_op jit(solution)/shard_map/ppermute | solution.py:420
  136.0 5.9 %copy-start.7 = (f32[8,5,384]{2,1,0:T(8,128)S(1)}, f32[8,5,384]{2,1,0:T(8,128)}, u32[]{:S(2)}) copy-start(f32[8,5,384]{2,1,0:T(8,128)} %copy-done.5) | copy-start | bytes 184324
  136.0 5.9 %copy-start.9 = (bf16[6,64,128]{2,1,0:T(8,128)(2,1)S(1)}, bf16[6,64,128]{2,1,0:T(8,128)(2,1)}, u32[]{:S(2)}) copy-start(bf16[6,64,128]{2,1,0:T(8,128)(2,1)} %copy-done.8) | copy-start | bytes 294916
  136.0 5.9 %copy-start.17 = (bf16[8,384,128]{2,1,0:T(8,128)(2,1)S(1)}, bf16[8,384,128]{2,1,0:T(8,128)(2,1)}, u32[]{:S(2)}) copy-start(bf16[8,384,128]{2,1,0:T(8,128)(2,1)} %get-tuple-element.18._.refs_0_) | copy-start | bytes 2359300
  136.1 5.9 %copy-start.19 = (bf16[1,384,128]{2,1,0:T(8,128)(2,1)S(1)}, bf16[1,384,128]{2,1,0:T(8,128)(2,1)}, u32[]{:S(2)}) copy-start(bf16[1,384,128]{2,1,0:T(8,128)(2,1)} %copy-done.18) | copy-start | bytes 294916
  136.1 16.9 %collective-permute-start.11 = (bf16[1,384,128]{2,1,0:T(8,128)(2,1)S(1)}, bf16[1,384,128]{2,1,0:T(8,128)(2,1)S(1)}, u32[]{:S(2)}, u32[]{:S(2)}) collective-permute-start(bf16[1,384,128]{2,1,0:T(8,128)(2,1)S(1)} %get-tuple-element.24), channel_id=1, source_target_pairs={{0,128},{32,160},{64,192},{96,224},{1,129},{33,161},{65,193},{97,2... | collective-permute-start | bytes 294920 | tf_op jit(solution)/shard_map/ppermute | solution.py:420
  137.5 17.6 %all-to-all-start.3 = ((bf16[8,384,128]{2,1,0:T(8,128)(2,1)}), bf16[8,384,128]{2,1,0:T(8,128)(2,1)S(1)}, u32[]{:S(2)}, u32[]{:S(2)}) async-start(bf16[8,384,128]{2,1,0:T(8,128)(2,1)} %get-tuple-element.27), calls=%async_computation.3 | async-start | bytes 1572864 | tf_op jit(solution)/shard_map/all_to_all | solution.py:319
  142.0 13.1 %copy-start.11 = (bf16[8,192,128]{2,1,0:T(8,128)(2,1)S(1)}, bf16[8,192,128]{2,1,0:T(8,128)(2,1)}, u32[]{:S(2)}) copy-start(bf16[8,192,128]{2,1,0:T(8,128)(2,1)} %get-tuple-element.17.refs_0_) | copy-start | bytes 1179652
  142.0 13.1 %copy-start.13 = (bf16[8,192,128]{2,1,0:T(8,128)(2,1)S(1)}, bf16[8,192,128]{2,1,0:T(8,128)(2,1)}, u32[]{:S(2)}) copy-start(bf16[8,192,128]{2,1,0:T(8,128)(2,1)} %copy-done.12) | copy-start | bytes 1179652
  142.0 13.1 %copy-start.15 = (bf16[8,192,128]{2,1,0:T(8,128)(2,1)S(1)}, bf16[8,192,128]{2,1,0:T(8,128)(2,1)}, u32[]{:S(2)}) copy-start(bf16[8,192,128]{2,1,0:T(8,128)(2,1)} %copy-done.14) | copy-start | bytes 1179652
  155.1 11.8 %copy-start.4 = (bf16[8,384,128]{2,1,0:T(8,128)(2,1)}, bf16[8,384,128]{2,1,0:T(8,128)(2,1)S(1)}, u32[]{:S(2)}) copy-start(bf16[8,384,128]{2,1,0:T(8,128)(2,1)S(1)} %all-to-all-done.3.refs_7_.refs_0_) | copy-start | bytes 2359300
  166.9 25.1 %all-to-all-start.4 = ((bf16[8,768,128]{2,1,0:T(8,128)(2,1)}), bf16[8,768,128]{2,1,0:T(8,128)(2,1)S(1)}, u32[]{:S(2)}, u32[]{:S(2)}) async-start(bf16[8,768,128]{2,1,0:T(8,128)(2,1)} %get-tuple-element.28), calls=%async_computation.4 | async-start | bytes 3145728 | tf_op jit(solution)/shard_map/all_to_all | solution.py:319
  (12 other events, 24.0 us)

commit v5 on v4

--- a/solution.py
+++ b/solution.py
@@ -438,7 +438,7 @@
     next_b = hop(last_b, 1)
     layers_a, done_a = run("a", 1, next_a, [layers_a], [last_b])
     arrived_a = exchange(layers_a)
-    layers, last_c = run("c", 0, tokens_in, [layers], [done_a, next_b])
+    layers, last_c = run("c", 0, tokens_in, [layers], [done_a, next_b], LARGE)
     next_c = hop(last_c, 2)
     layers, done_b = run("b", 1, next_b, [layers], [], LARGE)
     layers, _ = run("c", 1, next_c, [layers], [arrived_a])

time: 199 us -> 199 us (level)
    unnamed x54 -> x56, local copies, waits for them, and re-layouts: 5.76 us -> 5.76 us
where the time goes in v5:
time: 199 us; the launch traced here: 196 us
  waiting for transfers between devices  80.5 us (40%)
  Pallas kernels  53.8 us (27%)
  starting transfers between devices  46 us (23%)
  local copies, waits for them, and re-layouts  13.2 us (7%)
    all_to_all x5, waiting for transfers between devices, exchange(): lax.all_to_all(array, 'section', 0, 0, axis_index_groups=groups, tiled=True)  47.1 us
    pallas_call x6, Pallas kernels, attention(): pl.pallas_call(functools.partial(attention_kernel, (heads, stage, len(kv)...  38.4 us
    ppermute x3, waiting for transfers between devices, hop(): lax.ppermute(last, 'section', [(i, i + GROUP) for i in range(0, GROUP, st...  33.4 us
    all_to_all x5, starting transfers between devices, exchange(): lax.all_to_all(array, 'section', 0, 0, axis_index_groups=groups, tiled=True)  19.7 us
    pallas_call x7, Pallas kernels, call(): pl.pallas_call(kernel, out_shape=out_shape, in_specs=in_specs, out_specs=...  15.4 us
    ppermute x5, starting transfers between devices, to_first_core(): return lax.ppermute(array, ('section', 'seq'), pairs)  10.6 us
    ppermute x2, starting transfers between devices, both_ways(): lax.ppermute(array, 'seq', forward)  5.87 us
    ppermute x2, starting transfers between devices, both_ways(): lax.ppermute(array, 'seq', backward)  5.83 us
  transfers between devices with their start and end apart: 17, of which 6 were waited for; matrix products, arithmetic and copies ran while one was open for 5% of the time, Pallas kernels for 14%

profile of v5, /device:TPU:198, one launch (start us, length us, event | category | flops | bytes accessed | tf_op | source)
XLA Modules:
  0.0 195.8 jit_solution(3759342809380861328)
XLA Ops:
  0.0 2.2 %shard_map.100._ = bf16[8,384,128]{2,1,0:T(8,128)(2,1)} custom-call(bf16[1,384,2560]{2,1,0:T(8,128)(2,1)} %values.3), custom_call_target="tpu_custom_call" | custom-call | bytes 1024 | tf_op jit(solution)/shard_map/pallas_call | solution.py:328
  2.2 3.2 %shard_map.101 = bf16[8,960,128]{2,1,0:T(8,128)(2,1)} custom-call(bf16[1,384,2560]{2,1,0:T(8,128)(2,1)} %values.3, bf16[8,384,128]{2,1,0:T(8,128)(2,1)} %shard_map.100._), custom_call_target="tpu_custom_call" | custom-call | bytes 1024 | tf_op jit(solution)/shard_map/pallas_call | solution.py:328
  5.3 4.6 %all-to-all-start = ((bf16[8,960,128]{2,1,0:T(8,128)(2,1)}), bf16[8,960,128]{2,1,0:T(8,128)(2,1)S(1)}, u32[]{:S(2)}, u32[]{:S(2)}) async-start(bf16[8,960,128]{2,1,0:T(8,128)(2,1)} %shard_map.101), calls=%async_computation | async-start | bytes 3932160 | tf_op jit(solution)/shard_map/all_to_all | solution.py:319
  9.9 2.9 %collective-permute-start = (bf16[8,384,128]{2,1,0:T(8,128)(2,1)S(1)}, bf16[8,384,128]{2,1,0:T(8,128)(2,1)S(1)}, u32[]{:S(2)}, u32[]{:S(2)}) collective-permute-start(bf16[8,384,128]{2,1,0:T(8,128)(2,1)S(1)} %copy-done.22), channel_id=1, source_target_pairs={{0,1},{1,2},{2,3},{3,4},{4,5},{5,6},{6,7},{7,8},{8,9},{9,10},{10,1... | collective-permute-start | bytes 2359304 | tf_op jit(solution)/shard_map/ppermute | solution.py:322
  12.9 2.9 %collective-permute-start.1 = (bf16[8,384,128]{2,1,0:T(8,128)(2,1)S(1)}, bf16[8,384,128]{2,1,0:T(8,128)(2,1)}, u32[]{:S(2)}, u32[]{:S(2)}) collective-permute-start(bf16[8,384,128]{2,1,0:T(8,128)(2,1)S(1)} %copy-done.22), channel_id=1, source_target_pairs={{1,0},{2,1},{3,2},{4,3},{5,4},{6,5},{7,6},{8,7},{9,8},{10,9},{11,1... | collective-permute-start | bytes 2359304 | tf_op jit(solution)/shard_map/ppermute | solution.py:322
  15.8 1.5 concatenate.7
  19.4 16.3 %all-to-all-done.refs_1_.owned.refs_0_ = bf16[8,960,128]{2,1,0:T(8,128)(2,1)S(1)} async-done(((bf16[8,960,128]{2,1,0:T(8,128)(2,1)}), bf16[8,960,128]{2,1,0:T(8,128)(2,1)S(1)}, u32[]{:S(2)}, u32[]{:S(2)}) %all-to-all-start) | async-done | bytes 1966112 | tf_op jit(solution)/shard_map/all_to_all | solution.py:319
  37.0 3.4 %all-to-all-start.1 = ((f32[8,5,384]{2,1,0:T(8,128)}), f32[8,5,384]{2,1,0:T(8,128)S(1)}, u32[]{:S(2)}, u32[]{:S(2)}) async-start(f32[8,5,384]{2,1,0:T(8,128)} %shard_map.102), calls=%async_computation.1 | async-start | bytes 196608 | tf_op jit(solution)/shard_map/all_to_all | solution.py:319
  40.4 5.7 %all-to-all-done.1.vectors.params = f32[8,5,384]{2,1,0:T(8,128)S(1)} async-done(((f32[8,5,384]{2,1,0:T(8,128)}), f32[8,5,384]{2,1,0:T(8,128)S(1)}, u32[]{:S(2)}, u32[]{:S(2)}) %all-to-all-start.1) | async-done | bytes 61472 | tf_op jit(solution)/shard_map/all_to_all | solution.py:319
  46.7 2.7 %shard_map.103 = (bf16[8,384,128]{2,1,0:T(8,128)(2,1)}, bf16[8,192,128]{2,1,0:T(8,128)(2,1)}) custom-call(bf16[8,960,128]{2,1,0:T(8,128)(2,1)} %copy-done, bf16[8,384,128]{2,1,0:T(8,128)(2,1)} %copy-done.23, bf16[8,384,128]{2,1,0:T(8,128)(2,1)} %collective-permute-done.1.high, f32[8,5,384]{2,1,0:T(8,128)} %copy-done.3), custom_call_target="tpu_custom_call" | custom-call | bytes 1024 | tf_op jit(solution)/shard_map/pallas_call | solution.py:328
  49.4 2.6 %shard_map.104 = bf16[8,768,128]{2,1,0:T(8,128)(2,1)} custom-call(bf16[8,384,128]{2,1,0:T(8,128)(2,1)} %copy-done.23, bf16[8,384,128]{2,1,0:T(8,128)(2,1)} %collective-permute-done.1.high, bf16[8,384,128]{2,1,0:T(8,128)(2,1)} %get-tuple-element.18._.refs_0_), custom_call_target="tpu_custom_call" | custom-call | bytes 1024 | tf_op jit(solution)/shard_map/pallas_call | solution.py:328
  52.0 3.7 %all-to-all-start.2 = ((bf16[8,768,128]{2,1,0:T(8,128)(2,1)}), bf16[8,768,128]{2,1,0:T(8,128)(2,1)S(1)}, u32[]{:S(2)}, u32[]{:S(2)}) async-start(bf16[8,768,128]{2,1,0:T(8,128)(2,1)} %shard_map.104), calls=%async_computation.2 | async-start | bytes 3145728 | tf_op jit(solution)/shard_map/all_to_all | solution.py:319
  55.9 2.9 %collective-permute-start.7 = (bf16[8,384,128]{2,1,0:T(8,128)(2,1)}, bf16[8,384,128]{2,1,0:T(8,128)(2,1)}, u32[]{:S(2)}, u32[]{:S(2)}) collective-permute-start(bf16[8,384,128]{2,1,0:T(8,128)(2,1)} %get-tuple-element.18._.refs_0_), channel_id=1, source_target_pairs={{0,1},{1,2},{2,3},{3,4},{4,5},{5,6},{6,7},{7,8},{8,9},{9,10},{10,1... | collective-permute-start | bytes 2359304 | tf_op jit(solution)/shard_map/ppermute | solution.py:322
  58.9 2.9 %collective-permute-start.8 = (bf16[8,384,128]{2,1,0:T(8,128)(2,1)}, bf16[8,384,128]{2,1,0:T(8,128)(2,1)}, u32[]{:S(2)}, u32[]{:S(2)}) collective-permute-start(bf16[8,384,128]{2,1,0:T(8,128)(2,1)} %get-tuple-element.18._.refs_0_), channel_id=1, source_target_pairs={{1,0},{2,1},{3,2},{4,3},{5,4},{6,5},{7,6},{8,7},{9,8},{10,9},{11,1... | collective-permute-start | bytes 2359304 | tf_op jit(solution)/shard_map/ppermute | solution.py:322
  62.0 1.3 collective-permute-start.2
  65.0 1.3 copy.23
  68.5 3.8 %collective-permute-start.3 = (bf16[8,192,128]{2,1,0:T(8,128)(2,1)}, bf16[8,192,128]{2,1,0:T(8,128)(2,1)}, u32[]{:S(2)}, u32[]{:S(2)}) collective-permute-start(bf16[8,192,128]{2,1,0:T(8,128)(2,1)} %get-tuple-element.17.refs_0_), channel_id=1, source_target_pairs={{0,1},{1,2},{2,3},{3,4},{4,5},{5,6},{6,7},{7,8},{8,9},{9,10},{10,1... | collective-permute-start | bytes 1179656 | tf_op jit(solution)/shard_map/ppermute | solution.py:401
  72.3 1.3 collective-permute-start.4
  73.6 3.7 %all-to-all-done.2.refs_1_ = bf16[8,768,128]{2,1,0:T(8,128)(2,1)S(1)} async-done(((bf16[8,768,128]{2,1,0:T(8,128)(2,1)}), bf16[8,768,128]{2,1,0:T(8,128)(2,1)S(1)}, u32[]{:S(2)}, u32[]{:S(2)}) %all-to-all-start.2) | async-done | bytes 1572896 | tf_op jit(solution)/shard_map/all_to_all | solution.py:319
  78.2 1.5 copy-done.7
  80.8 2.9 %collective-permute-start.5 = (bf16[8,192,128]{2,1,0:T(8,128)(2,1)S(1)}, bf16[8,192,128]{2,1,0:T(8,128)(2,1)S(1)}, u32[]{:S(2)}, u32[]{:S(2)}) collective-permute-start(bf16[8,192,128]{2,1,0:T(8,128)(2,1)S(1)} %copy-done.13), channel_id=1, source_target_pairs={{1,0},{2,1},{3,2},{4,3},{5,4},{6,5},{7,6},{8,7},{9,8},{10,9},{11,1... | collective-permute-start | bytes 1179656 | tf_op jit(solution)/shard_map/ppermute | solution.py:401
  87.2 33.4 %collective-permute-done.9.x_in = bf16[1,384,128]{2,1,0:T(8,128)(2,1)S(1)} collective-permute-done((bf16[1,384,128]{2,1,0:T(8,128)(2,1)S(1)}, bf16[1,384,128]{2,1,0:T(8,128)(2,1)S(1)}, u32[]{:S(2)}, u32[]{:S(2)}) %collective-permute-start.9) | collective-permute-done | bytes 98336 | tf_op jit(solution)/shard_map/ppermute | solution.py:420
  121.9 12.9 %shard_map.107 = (bf16[8,384,128]{2,1,0:T(8,128)(2,1)}, bf16[1,384,128]{2,1,0:T(8,128)(2,1)S(1)}) custom-call(s32[3]{0:T(128)S(1)} %pad_add_fusion.place, bf16[1,384,128]{2,1,0:T(8,128)(2,1)S(1)} %collective-permute-done.9.x_in, f32[8,5,384]{2,1,0:T(8,128)S(1)} %copy-done.5, bf16[384,128]{1,0:T(8,128)(2,1)S(1)} %bitcast.24, ...), custom_call_target="tpu_custom_call", output_to_operand_aliasing={{0}: (6, {})} | custom-call | bytes 1024 | tf_op jit(solution)/shard_map/pallas_call | solution.py:250
  136.1 1.4 collective-permute-start.11
  137.5 4.5 %all-to-all-start.3 = ((bf16[8,384,128]{2,1,0:T(8,128)(2,1)}), bf16[8,384,128]{2,1,0:T(8,128)(2,1)S(1)}, u32[]{:S(2)}, u32[]{:S(2)}) async-start(bf16[8,384,128]{2,1,0:T(8,128)(2,1)} %get-tuple-element.27), calls=%async_computation.3 | async-start | bytes 1572864 | tf_op jit(solution)/shard_map/all_to_all | solution.py:319
  142.0 11.0 %shard_map.109 = (bf16[8,768,128]{2,1,0:T(8,128)(2,1)}, bf16[1,384,128]{2,1,0:T(8,128)(2,1)}) custom-call(s32[3]{0:T(128)S(1)} %pad_add_fusion.place, bf16[1,384,128]{2,1,0:T(8,128)(2,1)S(1)} %copy-done.20, f32[8,5,384]{2,1,0:T(8,128)S(1)} %copy-done.6, bf16[384,128]{1,0:T(8,128)(2,1)S(1)} %bitcast.26, ...), custom_call_target="tpu_custom_call", output_to_operand_aliasing={{0}: (7, {})} | custom-call | flops 137438953472 | bytes 67108864 | tf_op jit(solution)/shard_map/pallas_call | solution.py:250
  153.0 2.1 %all-to-all-done.3.refs_7_.refs_0_ = bf16[8,384,128]{2,1,0:T(8,128)(2,1)S(1)} async-done(((bf16[8,384,128]{2,1,0:T(8,128)(2,1)}), bf16[8,384,128]{2,1,0:T(8,128)(2,1)S(1)}, u32[]{:S(2)}, u32[]{:S(2)}) %all-to-all-start.3) | async-done | bytes 786464 | tf_op jit(solution)/shard_map/all_to_all | solution.py:319
  155.1 11.8 %shard_map.110 = (bf16[8,768,128]{2,1,0:T(8,128)(2,1)}, bf16[1,384,128]{2,1,0:T(8,128)(2,1)}) custom-call(s32[3]{0:T(128)S(1)} %pad_add_fusion.place, bf16[1,384,128]{2,1,0:T(8,128)(2,1)S(1)} %collective-permute-done.11.x_in, f32[8,5,384]{2,1,0:T(8,128)S(1)} %copy-done.6, bf16[384,128]{1,0:T(8,128)(2,1)S(1)} %bitcast.27, ...), custom_call_target="tpu_custom_call", output_to_operand_aliasing={{0}: (10, {})} | custom-call | bytes 1024 | tf_op jit(solution)/shard_map/pallas_call | solution.py:250
  166.9 3.6 %all-to-all-start.4 = ((bf16[8,768,128]{2,1,0:T(8,128)(2,1)}), bf16[8,768,128]{2,1,0:T(8,128)(2,1)S(1)}, u32[]{:S(2)}, u32[]{:S(2)}) async-start(bf16[8,768,128]{2,1,0:T(8,128)(2,1)} %get-tuple-element.28), calls=%async_computation.4 | async-start | bytes 3145728 | tf_op jit(solution)/shard_map/all_to_all | solution.py:319
  170.5 2.2 %shard_map.111.refs_1_ = bf16[1,384,2560]{2,1,0:T(8,128)(2,1)} custom-call(bf16[8,384,128]{2,1,0:T(8,128)(2,1)} %copy-done.2), custom_call_target="tpu_custom_call" | custom-call | bytes 1024 | tf_op jit(solution)/shard_map/pallas_call | solution.py:328
  172.7 19.3 %all-to-all-done.4.refs_0_ = bf16[8,768,128]{2,1,0:T(8,128)(2,1)S(1)} async-done(((bf16[8,768,128]{2,1,0:T(8,128)(2,1)}), bf16[8,768,128]{2,1,0:T(8,128)(2,1)S(1)}, u32[]{:S(2)}, u32[]{:S(2)}) %all-to-all-start.4) | async-done | bytes 1572896 | tf_op jit(solution)/shard_map/all_to_all | solution.py:319
  193.2 2.6 %shard_map.112 = bf16[1,384,2560]{2,1,0:T(8,128)(2,1)} custom-call(bf16[8,768,128]{2,1,0:T(8,128)(2,1)} %copy-done.21, bf16[1,384,2560]{2,1,0:T(8,128)(2,1)} %shard_map.111.refs_1_), custom_call_target="tpu_custom_call", output_to_operand_aliasing={{}: (1, {})} | custom-call | bytes 1024 | tf_op jit(solution)/shard_map/pallas_call | solution.py:328
  (97 shorter events, 17.2 us)
Async XLA Ops:
  5.3 10.5 %copy-start.24 = (f32[1,2560]{1,0:T(1,128)S(1)}, f32[1,2560]{1,0:T(1,128)}, u32[]{:S(2)}) copy-start(f32[1,2560]{1,0:T(1,128)} %param.12) | copy-start | bytes 30724
  5.3 30.4 %all-to-all-start = ((bf16[8,960,128]{2,1,0:T(8,128)(2,1)}), bf16[8,960,128]{2,1,0:T(8,128)(2,1)S(1)}, u32[]{:S(2)}, u32[]{:S(2)}) async-start(bf16[8,960,128]{2,1,0:T(8,128)(2,1)} %shard_map.101), calls=%async_computation | async-start | bytes 3932160 | tf_op jit(solution)/shard_map/all_to_all | solution.py:319
  9.9 30.4 %collective-permute-start = (bf16[8,384,128]{2,1,0:T(8,128)(2,1)S(1)}, bf16[8,384,128]{2,1,0:T(8,128)(2,1)S(1)}, u32[]{:S(2)}, u32[]{:S(2)}) collective-permute-start(bf16[8,384,128]{2,1,0:T(8,128)(2,1)S(1)} %copy-done.22), channel_id=1, source_target_pairs={{0,1},{1,2},{2,3},{3,4},{4,5},{5,6},{6,7},{7,8},{8,9},{9,10},{10,1... | collective-permute-start | bytes 2359304 | tf_op jit(solution)/shard_map/ppermute | solution.py:322
  12.9 27.5 %collective-permute-start.1 = (bf16[8,384,128]{2,1,0:T(8,128)(2,1)S(1)}, bf16[8,384,128]{2,1,0:T(8,128)(2,1)}, u32[]{:S(2)}, u32[]{:S(2)}) collective-permute-start(bf16[8,384,128]{2,1,0:T(8,128)(2,1)S(1)} %copy-done.22), channel_id=1, source_target_pairs={{1,0},{2,1},{3,2},{4,3},{5,4},{6,5},{7,6},{8,7},{9,8},{10,9},{11,1... | collective-permute-start | bytes 2359304 | tf_op jit(solution)/shard_map/ppermute | solution.py:322
  37.0 9.1 %all-to-all-start.1 = ((f32[8,5,384]{2,1,0:T(8,128)}), f32[8,5,384]{2,1,0:T(8,128)S(1)}, u32[]{:S(2)}, u32[]{:S(2)}) async-start(f32[8,5,384]{2,1,0:T(8,128)} %shard_map.102), calls=%async_computation.1 | async-start | bytes 196608 | tf_op jit(solution)/shard_map/all_to_all | solution.py:319
  52.0 9.8 %copy-start.27 = (s32[6]{0:T(128)S(1)}, s32[6]{0:T(128)}, u32[]{:S(2)}) copy-start(s32[6]{0:T(128)} %param.18) | copy-start | bytes 76
  52.0 9.8 %copy-start.25 = (s32[6,18]{1,0:T(8,128)S(1)}, s32[6,18]{1,0:T(8,128)}, u32[]{:S(2)}) copy-start(s32[6,18]{1,0:T(8,128)} %param.17) | copy-start | bytes 1300
  52.0 25.3 %copy-start.1 = (bf16[8,960,128]{2,1,0:T(8,128)(2,1)S(1)}, bf16[8,960,128]{2,1,0:T(8,128)(2,1)}, u32[]{:S(2)}) copy-start(bf16[8,960,128]{2,1,0:T(8,128)(2,1)} %copy-done) | copy-start | bytes 5898244
  52.0 25.2 %all-to-all-start.2 = ((bf16[8,768,128]{2,1,0:T(8,128)(2,1)}), bf16[8,768,128]{2,1,0:T(8,128)(2,1)S(1)}, u32[]{:S(2)}, u32[]{:S(2)}) async-start(bf16[8,768,128]{2,1,0:T(8,128)(2,1)} %shard_map.104), calls=%async_computation.2 | async-start | bytes 3145728 | tf_op jit(solution)/shard_map/all_to_all | solution.py:319
  55.9 27.8 %collective-permute-start.7 = (bf16[8,384,128]{2,1,0:T(8,128)(2,1)}, bf16[8,384,128]{2,1,0:T(8,128)(2,1)}, u32[]{:S(2)}, u32[]{:S(2)}) collective-permute-start(bf16[8,384,128]{2,1,0:T(8,128)(2,1)} %get-tuple-element.18._.refs_0_), channel_id=1, source_target_pairs={{0,1},{1,2},{2,3},{3,4},{4,5},{5,6},{6,7},{7,8},{8,9},{9,10},{10,1... | collective-permute-start | bytes 2359304 | tf_op jit(solution)/shard_map/ppermute | solution.py:322
  58.9 26.1 %collective-permute-start.8 = (bf16[8,384,128]{2,1,0:T(8,128)(2,1)}, bf16[8,384,128]{2,1,0:T(8,128)(2,1)}, u32[]{:S(2)}, u32[]{:S(2)}) collective-permute-start(bf16[8,384,128]{2,1,0:T(8,128)(2,1)} %get-tuple-element.18._.refs_0_), channel_id=1, source_target_pairs={{1,0},{2,1},{3,2},{4,3},{5,4},{6,5},{7,6},{8,7},{9,8},{10,9},{11,1... | collective-permute-start | bytes 2359304 | tf_op jit(solution)/shard_map/ppermute | solution.py:322
  62.0 18.6 %collective-permute-start.2 = (bf16[8,192,128]{2,1,0:T(8,128)(2,1)}, bf16[8,192,128]{2,1,0:T(8,128)(2,1)}, u32[]{:S(2)}, u32[]{:S(2)}) collective-permute-start(bf16[8,192,128]{2,1,0:T(8,128)(2,1)} %get-tuple-element.17.refs_0_), channel_id=1, source_target_pairs={{16,0},{17,1},{18,2},{19,3},{20,4},{21,5},{22,6},{23,7},{24,8},{25... | collective-permute-start | bytes 1179656 | tf_op jit(solution)/shard_map/ppermute | solution.py:401
  68.5 66.3 %collective-permute-start.3 = (bf16[8,192,128]{2,1,0:T(8,128)(2,1)}, bf16[8,192,128]{2,1,0:T(8,128)(2,1)}, u32[]{:S(2)}, u32[]{:S(2)}) collective-permute-start(bf16[8,192,128]{2,1,0:T(8,128)(2,1)} %get-tuple-element.17.refs_0_), channel_id=1, source_target_pairs={{0,1},{1,2},{2,3},{3,4},{4,5},{5,6},{6,7},{7,8},{8,9},{9,10},{10,1... | collective-permute-start | bytes 1179656 | tf_op jit(solution)/shard_map/ppermute | solution.py:401
  72.3 62.5 %collective-permute-start.4 = (bf16[8,192,128]{2,1,0:T(8,128)(2,1)}, bf16[8,192,128]{2,1,0:T(8,128)(2,1)}, u32[]{:S(2)}, u32[]{:S(2)}) collective-permute-start(bf16[8,192,128]{2,1,0:T(8,128)(2,1)} %get-tuple-element.17.refs_0_), channel_id=1, source_target_pairs={{16,1},{17,2},{18,3},{19,4},{20,5},{21,6},{22,7},{23,8},{24,9},{25... | collective-permute-start | bytes 1179656 | tf_op jit(solution)/shard_map/ppermute | solution.py:401
  77.3 57.6 %copy-start.9 = (bf16[6,64,128]{2,1,0:T(8,128)(2,1)}, bf16[6,64,128]{2,1,0:T(8,128)(2,1)S(1)}, u32[]{:S(2)}) copy-start(bf16[6,64,128]{2,1,0:T(8,128)(2,1)S(1)} %broadcast_in_dim.40) | copy-start | bytes 294916
  79.8 6.5 %copy-start.5 = (f32[8,5,384]{2,1,0:T(8,128)S(1)}, f32[8,5,384]{2,1,0:T(8,128)}, u32[]{:S(2)}) copy-start(f32[8,5,384]{2,1,0:T(8,128)} %copy-done.3) | copy-start | bytes 184324
  79.8 6.5 %copy-start.11 = (bf16[8,384,128]{2,1,0:T(8,128)(2,1)S(1)}, bf16[8,384,128]{2,1,0:T(8,128)(2,1)}, u32[]{:S(2)}) copy-start(bf16[8,384,128]{2,1,0:T(8,128)(2,1)} %get-tuple-element.18._.refs_0_) | copy-start | bytes 2359300
  80.8 54.1 %collective-permute-start.5 = (bf16[8,192,128]{2,1,0:T(8,128)(2,1)S(1)}, bf16[8,192,128]{2,1,0:T(8,128)(2,1)S(1)}, u32[]{:S(2)}, u32[]{:S(2)}) collective-permute-start(bf16[8,192,128]{2,1,0:T(8,128)(2,1)S(1)} %copy-done.13), channel_id=1, source_target_pairs={{1,0},{2,1},{3,2},{4,3},{5,4},{6,5},{7,6},{8,7},{9,8},{10,9},{11,1... | collective-permute-start | bytes 1179656 | tf_op jit(solution)/shard_map/ppermute | solution.py:401
  83.7 51.2 %collective-permute-start.6 = (bf16[8,192,128]{2,1,0:T(8,128)(2,1)S(1)}, bf16[8,192,128]{2,1,0:T(8,128)(2,1)S(1)}, u32[]{:S(2)}, u32[]{:S(2)}) collective-permute-start(bf16[8,192,128]{2,1,0:T(8,128)(2,1)S(1)} %copy-done.13), channel_id=1, source_target_pairs={{17,0},{18,1},{19,2},{20,3},{21,4},{22,5},{23,6},{24,7},{25,8},{26... | collective-permute-start | bytes 1179656 | tf_op jit(solution)/shard_map/ppermute | solution.py:401
  85.0 35.6 %collective-permute-start.9 = (bf16[1,384,128]{2,1,0:T(8,128)(2,1)S(1)}, bf16[1,384,128]{2,1,0:T(8,128)(2,1)S(1)}, u32[]{:S(2)}, u32[]{:S(2)}) collective-permute-start(bf16[1,384,128]{2,1,0:T(8,128)(2,1)S(1)} %get-tuple-element.19.refs_3_), channel_id=1, source_target_pairs={{0,128},{16,144},{32,160},{48,176},{64,192},{80,208},{96,224},{112... | collective-permute-start | bytes 294920 | tf_op jit(solution)/shard_map/ppermute | solution.py:420
  120.6 14.3 %collective-permute-start.10 = (bf16[1,384,128]{2,1,0:T(8,128)(2,1)S(1)}, bf16[1,384,128]{2,1,0:T(8,128)(2,1)S(1)}, u32[]{:S(2)}, u32[]{:S(2)}) collective-permute-start(bf16[1,384,128]{2,1,0:T(8,128)(2,1)S(1)} %get-tuple-element.22.refs_3_), channel_id=1, source_target_pairs={{0,128},{16,144},{32,160},{48,176},{64,192},{80,208},{96,224},{112... | collective-permute-start | bytes 294920 | tf_op jit(solution)/shard_map/ppermute | solution.py:420
  121.9 13.1 %copy-start.8 = (bf16[384,2560]{1,0:T(8,128)(2,1)S(1)}, bf16[384,2560]{1,0:T(8,128)(2,1)}, u32[]{:S(2)}) copy-start(bf16[384,2560]{1,0:T(8,128)(2,1)} %x_in.5) | copy-start | bytes 5898244
  136.0 5.9 %copy-start.6 = (f32[8,5,384]{2,1,0:T(8,128)S(1)}, f32[8,5,384]{2,1,0:T(8,128)}, u32[]{:S(2)}) copy-start(f32[8,5,384]{2,1,0:T(8,128)} %copy-done.3) | copy-start | bytes 184324
  136.0 5.9 %copy-start.10 = (bf16[6,64,128]{2,1,0:T(8,128)(2,1)S(1)}, bf16[6,64,128]{2,1,0:T(8,128)(2,1)}, u32[]{:S(2)}) copy-start(bf16[6,64,128]{2,1,0:T(8,128)(2,1)} %copy-done.9) | copy-start | bytes 294916
  136.1 5.9 %copy-start.12 = (bf16[8,384,128]{2,1,0:T(8,128)(2,1)S(1)}, bf16[8,384,128]{2,1,0:T(8,128)(2,1)}, u32[]{:S(2)}) copy-start(bf16[8,384,128]{2,1,0:T(8,128)(2,1)} %get-tuple-element.18._.refs_0_) | copy-start | bytes 2359300
  136.1 16.9 %collective-permute-start.11 = (bf16[1,384,128]{2,1,0:T(8,128)(2,1)S(1)}, bf16[1,384,128]{2,1,0:T(8,128)(2,1)S(1)}, u32[]{:S(2)}, u32[]{:S(2)}) collective-permute-start(bf16[1,384,128]{2,1,0:T(8,128)(2,1)S(1)} %get-tuple-element.24), channel_id=1, source_target_pairs={{0,128},{32,160},{64,192},{96,224},{1,129},{33,161},{65,193},{97,2... | collective-permute-start | bytes 294920 | tf_op jit(solution)/shard_map/ppermute | solution.py:420
  137.5 17.6 %all-to-all-start.3 = ((bf16[8,384,128]{2,1,0:T(8,128)(2,1)}), bf16[8,384,128]{2,1,0:T(8,128)(2,1)S(1)}, u32[]{:S(2)}, u32[]{:S(2)}) async-start(bf16[8,384,128]{2,1,0:T(8,128)(2,1)} %get-tuple-element.27), calls=%async_computation.3 | async-start | bytes 1572864 | tf_op jit(solution)/shard_map/all_to_all | solution.py:319
  142.0 13.1 %copy-start.14 = (bf16[8,192,128]{2,1,0:T(8,128)(2,1)S(1)}, bf16[8,192,128]{2,1,0:T(8,128)(2,1)}, u32[]{:S(2)}) copy-start(bf16[8,192,128]{2,1,0:T(8,128)(2,1)} %get-tuple-element.17.refs_0_) | copy-start | bytes 1179652
  142.0 13.1 %copy-start.16 = (bf16[8,192,128]{2,1,0:T(8,128)(2,1)S(1)}, bf16[8,192,128]{2,1,0:T(8,128)(2,1)}, u32[]{:S(2)}) copy-start(bf16[8,192,128]{2,1,0:T(8,128)(2,1)} %copy-done.15) | copy-start | bytes 1179652
  142.0 13.1 %copy-start.18 = (bf16[8,192,128]{2,1,0:T(8,128)(2,1)S(1)}, bf16[8,192,128]{2,1,0:T(8,128)(2,1)}, u32[]{:S(2)}) copy-start(bf16[8,192,128]{2,1,0:T(8,128)(2,1)} %copy-done.17) | copy-start | bytes 1179652
  155.1 11.8 %copy-start.2 = (bf16[8,384,128]{2,1,0:T(8,128)(2,1)}, bf16[8,384,128]{2,1,0:T(8,128)(2,1)S(1)}, u32[]{:S(2)}) copy-start(bf16[8,384,128]{2,1,0:T(8,128)(2,1)S(1)} %all-to-all-done.3.refs_7_.refs_0_) | copy-start | bytes 2359300
  166.9 25.1 %all-to-all-start.4 = ((bf16[8,768,128]{2,1,0:T(8,128)(2,1)}), bf16[8,768,128]{2,1,0:T(8,128)(2,1)S(1)}, u32[]{:S(2)}, u32[]{:S(2)}) async-start(bf16[8,768,128]{2,1,0:T(8,128)(2,1)} %get-tuple-element.28), calls=%async_computation.4 | async-start | bytes 3145728 | tf_op jit(solution)/shard_map/all_to_all | solution.py:319
  (13 other events, 30.0 us)
